TPU v7x, 32 devices: a whole 2x2x4 slice. The times are simulated.
32 devices in a mesh: seq: 8 (over z, y), head: 4 (over x, core).
Axes of the slice: x: 2, y: 2, z: 4, core: 2. Of those that a mesh axis runs over, the one named last changes fastest.
Arguments:
- tokens: bfloat16 [8192, 2048], P('seq'), may hold values from -6 to 6
- codebook: bfloat16 [1024, 2048], replicated, may hold values from -6 to 6
- codes: int32 [8192], P('seq'), may hold values from 0 to 1023
- modality: int32 [8192], P('seq'), may hold values from 0 to 2, as said below
- segments: int32 [8, 1024], P('seq'), may hold values from 0 to 7, never falling along the last dimension, each value on 1 to 512 neighbouring positions
- sequence_source: int32 [8192], replicated, may hold values from 0 to 8191, as said below
- w_qkv: bfloat16 [2048, 3, 2048], P(None, None, 'head'), may hold values from -0.125 to 0.125
- w_out: bfloat16 [2048, 2048], P('head'), may hold values from -1 to 1
- w_up: bfloat16 [2048, 8192], P(None, 'head'), may hold values from -0.125 to 0.125
- w_down: bfloat16 [8192, 2048], P('head'), may hold values from -0.0625 to 0.0625
- norm1_gain: float32 [2048], replicated, may hold values from 0.1 to 1.9
- norm1_shift: float32 [2048], replicated, may hold values from -4 to 4
- norm2_gain: float32 [2048], replicated, may hold values from 0.1 to 1.9
- norm2_shift: float32 [2048], replicated, may hold values from -4 to 4
- cotangent: bfloat16 [8192, 2048], P('seq'), may hold values from -6 to 6
Outputs:
- block_output: bfloat16 [8192, 2048], P('seq')
- input_grad: bfloat16 [8192, 2048], P('seq')
- qkv_grad: float32 [2048, 3, 2048], P('seq', None, 'head')
- out_grad: float32 [2048, 2048], P('head', 'seq')
- up_grad: float32 [2048, 8192], P('seq', 'head')
- down_grad: float32 [8192, 2048], P('head', 'seq')
- gain_one_grad: float32 [2048], P('seq')
- shift_one_grad: float32 [2048], P('seq')
- gain_two_grad: float32 [2048], P('seq')
- shift_two_grad: float32 [2048], P('seq')
Inputs may be any that keep to these rules, and one draw needn't show every extreme that they name: `modality`: never falls along the tokens. `sequence_source`: A permutation of the 8192 grouped indices. Of the 1024 positions of each packed row, exactly 128 name grouped indices of each aligned block of 1024 grouped indices.
All inputs are finite; a program needn't handle non-finite values.
Results may differ from a plain program's by a relative error of at most 0.013.
Values may be sent and summed in bfloat16 or wider, within the bound.
No kernel may reach another device: no remote copies, remote signals or barrier semaphores. Data moves between devices by JAX's collectives and lax.ppermute only.
A program may use at most 256 MiB of HBM per device.

v0:
```python
from functools import partial
import math

import jax
import jax.numpy as jnp
from jax import lax
from jax.sharding import PartitionSpec as P

HEAD_DIM = 128


def normalize(values):
    centre = values - jnp.mean(values, axis=-1, keepdims=True)
    scaling = lax.rsqrt(jnp.mean(centre * centre, axis=-1, keepdims=True) + 1e-05)
    return (centre * scaling, scaling)


def norm_back(upstream, unit, scaling, gain):
    scaled = upstream * gain
    inner = (
        scaled
        - jnp.mean(scaled, axis=-1, keepdims=True)
        - unit * jnp.mean(scaled * unit, axis=-1, keepdims=True)
    )
    return (scaling * inner, jnp.sum(upstream * unit, axis=0), jnp.sum(upstream, axis=0))


def inverse_of(order):
    return jnp.zeros_like(order).at[order].set(jnp.arange(order.shape[0], dtype=jnp.int32))


def attention_scores(queries, keys_part, allowed, factor):
    scores = (
        jnp.einsum("qhc,khc->hqk", queries, keys_part, preferred_element_type=jnp.float32) * factor
    )
    return jnp.where(allowed[None], scores, -1e30)


def local(
    tokens,
    codebook,
    codes,
    modality,
    segments,
    sequence_source,
    w_qkv,
    w_out,
    w_up,
    w_down,
    norm1_gain,
    norm1_shift,
    norm2_gain,
    norm2_shift,
    cotangent,
):
    row_count = tokens.shape[0]
    local_width = w_out.shape[0]
    head_count = local_width // HEAD_DIM
    factor = 1.0 / math.sqrt(HEAD_DIM)
    device = lax.axis_index("seq")
    placed = inverse_of(sequence_source)
    own_places = lax.dynamic_slice_in_dim(placed, device * row_count, row_count)
    send_order = jnp.argsort(own_places)
    send_back = inverse_of(send_order)
    own_sources = lax.dynamic_slice_in_dim(sequence_source, device * row_count, row_count)
    arrival_key = own_sources // row_count * row_count + jnp.arange(row_count, dtype=jnp.int32)
    arrival_order = jnp.argsort(arrival_key)
    arrival_place = inverse_of(arrival_order)
    selected = (codes[:, None] == jnp.arange(codebook.shape[0], dtype=jnp.int32)[None, :]) & (
        modality == 1
    )[:, None]
    looked = jnp.dot(selected.astype(jnp.bfloat16), codebook, preferred_element_type=jnp.float32)
    embedded = tokens.astype(jnp.float32) + looked
    unit_one, scale_one = normalize(embedded)
    normed_one = (unit_one * norm1_gain + norm1_shift).astype(jnp.bfloat16)
    projected = jnp.einsum("td,dsc->tsc", normed_one, w_qkv, preferred_element_type=jnp.float32)
    projected = projected.astype(jnp.bfloat16).reshape(row_count, 3 * local_width)
    arrived = lax.all_to_all(projected[send_order], "seq", split_axis=0, concat_axis=0, tiled=True)
    ordered = arrived[arrival_place].reshape(row_count, 3, head_count, HEAD_DIM)
    queries = ordered[:, 0]
    keys_part = ordered[:, 1]
    values_part = ordered[:, 2]
    segment_row = segments[0]
    positions = jnp.arange(row_count, dtype=jnp.int32)
    allowed = (segment_row[:, None] == segment_row[None, :]) & (
        positions[None, :] <= positions[:, None]
    )
    masked = attention_scores(queries, keys_part, allowed, factor)
    peak = jnp.max(masked, axis=-1, keepdims=True)
    weights_exp = jnp.exp(masked - peak)
    total = jnp.sum(weights_exp, axis=-1, keepdims=True)
    log_total = peak + jnp.log(total)
    probs = (weights_exp / total).astype(jnp.bfloat16)
    mixed = jnp.einsum("hqk,khc->qhc", probs, values_part, preferred_element_type=jnp.float32)
    mixed = mixed.astype(jnp.bfloat16).reshape(row_count, local_width)
    returned = lax.all_to_all(mixed[arrival_order], "seq", split_axis=0, concat_axis=0, tiled=True)
    context = returned[send_back]
    attended = lax.psum(jnp.dot(context, w_out, preferred_element_type=jnp.float32), "head")
    hidden_in = embedded + attended
    unit_two, scale_two = normalize(hidden_in)
    normed_two = (unit_two * norm2_gain + norm2_shift).astype(jnp.bfloat16)
    up_value = jnp.dot(normed_two, w_up, preferred_element_type=jnp.float32)
    activated, gelu_pull = jax.vjp(partial(jax.nn.gelu, approximate=False), up_value)
    act_low = activated.astype(jnp.bfloat16)
    branch = lax.psum(
        jnp.dot(act_low, w_down, preferred_element_type=jnp.float32).astype(jnp.bfloat16), "head"
    ).astype(jnp.float32)
    block_output = (hidden_in + branch).astype(jnp.bfloat16)
    down_grad = jnp.einsum("tf,td->fd", act_low, cotangent, preferred_element_type=jnp.float32)
    act_grad = jnp.einsum("td,fd->tf", cotangent, w_down, preferred_element_type=jnp.float32)
    up_bar = gelu_pull(act_grad)[0].astype(jnp.bfloat16)
    up_grad = jnp.einsum("td,tf->df", normed_two, up_bar, preferred_element_type=jnp.float32)
    normed_two_bar = lax.psum(
        jnp.einsum("tf,df->td", up_bar, w_up, preferred_element_type=jnp.float32), "head"
    )
    hidden_part, gain_two_grad, shift_two_grad = norm_back(
        normed_two_bar, unit_two, scale_two, norm2_gain
    )
    hidden_bar = cotangent.astype(jnp.float32) + hidden_part
    hidden_low = hidden_bar.astype(jnp.bfloat16)
    out_grad = jnp.einsum("tc,td->cd", context, hidden_low, preferred_element_type=jnp.float32)
    context_bar = jnp.einsum(
        "td,cd->tc", hidden_low, w_out, preferred_element_type=jnp.float32
    ).astype(jnp.bfloat16)
    came = lax.all_to_all(context_bar[send_order], "seq", split_axis=0, concat_axis=0, tiled=True)
    context_seq = came[arrival_place].reshape(row_count, head_count, HEAD_DIM)
    again = attention_scores(queries, keys_part, allowed, factor)
    probs_again = jnp.exp(again - log_total)
    values_bar = jnp.einsum(
        "hqk,qhc->khc",
        probs_again.astype(jnp.bfloat16),
        context_seq,
        preferred_element_type=jnp.float32,
    )
    probs_bar = jnp.einsum(
        "qhc,khc->hqk", context_seq, values_part, preferred_element_type=jnp.float32
    )
    inner = jnp.sum(probs_again * probs_bar, axis=-1, keepdims=True)
    scores_bar = (probs_again * (probs_bar - inner)).astype(jnp.bfloat16)
    queries_bar = (
        jnp.einsum("hqk,khc->qhc", scores_bar, keys_part, preferred_element_type=jnp.float32)
        * factor
    )
    keys_bar = (
        jnp.einsum("hqk,qhc->khc", scores_bar, queries, preferred_element_type=jnp.float32) * factor
    )
    stacked = (
        jnp.stack([queries_bar, keys_bar, values_bar], axis=1)
        .astype(jnp.bfloat16)
        .reshape(row_count, 3 * local_width)
    )
    went = lax.all_to_all(stacked[arrival_order], "seq", split_axis=0, concat_axis=0, tiled=True)
    qkv_bar = went[send_back].reshape(row_count, 3, local_width)
    qkv_grad = jnp.einsum("td,tsc->dsc", normed_one, qkv_bar, preferred_element_type=jnp.float32)
    normed_one_bar = lax.psum(
        jnp.einsum("tsc,dsc->td", qkv_bar, w_qkv, preferred_element_type=jnp.float32), "head"
    )
    input_part, gain_one_grad, shift_one_grad = norm_back(
        normed_one_bar, unit_one, scale_one, norm1_gain
    )
    input_grad = (hidden_bar + input_part).astype(jnp.bfloat16)
    shares = (
        lax.psum_scatter(qkv_grad, "seq", scatter_dimension=0, tiled=True),
        lax.psum_scatter(out_grad, "seq", scatter_dimension=1, tiled=True),
        lax.psum_scatter(up_grad, "seq", scatter_dimension=0, tiled=True),
        lax.psum_scatter(down_grad, "seq", scatter_dimension=1, tiled=True),
        lax.psum_scatter(gain_one_grad, "seq", scatter_dimension=0, tiled=True),
        lax.psum_scatter(shift_one_grad, "seq", scatter_dimension=0, tiled=True),
        lax.psum_scatter(gain_two_grad, "seq", scatter_dimension=0, tiled=True),
        lax.psum_scatter(shift_two_grad, "seq", scatter_dimension=0, tiled=True),
    )
    return (
        block_output,
        input_grad,
        shares[0],
        shares[1],
        shares[2],
        shares[3],
        shares[4],
        shares[5],
        shares[6],
        shares[7],
    )


def solution(mesh):
    return jax.shard_map(
        local,
        mesh=mesh,
        in_specs=(
            P("seq", None),
            P(),
            P("seq"),
            P("seq"),
            P("seq", None),
            P(),
            P(None, None, "head"),
            P("head", None),
            P(None, "head"),
            P("head", None),
            P(),
            P(),
            P(),
            P(),
            P("seq", None),
        ),
        out_specs=(
            P("seq", None),
            P("seq", None),
            P("seq", None, "head"),
            P("head", "seq"),
            P("seq", "head"),
            P("head", "seq"),
            P("seq"),
            P("seq"),
            P("seq"),
            P("seq"),
        ),
        check_vma=False,
    )
```

profile of v0, /device:TPU:0, one launch (start us, length us, event | category | flops | bytes accessed | tf_op | source)
XLA Modules:
  0.0 1964.6 jit_solution(2835350515329142881)
XLA Ops:
  8.8 30.5 %scatter_custom_fusion = s32[8192]{0:T(1024)S(1)} fusion(s32[8192]{0:T(1024)S(1)} %compare_select_fusion, s32[8192]{0:T(1024)S(1)} %iota.35, s32[]{:T(128)} %constant.49.clone.1), kind=kCustom, calls=%fused_computation.85 | custom fusion | bytes 32772 | tf_op jit(solution)/shard_map/scatter | solution.py:29
  53.3 9.8 convolution_convert_fusion.1
  67.7 9.6 gather_fusion
  94.8 60.5 %all-to-all-done = bf16[8,128,1536]{2,1,0:T(8,128)(2,1)} async-done(((bf16[8,128,1536]{2,1,0:T(8,128)(2,1)}), bf16[8,128,1536]{2,1,0:T(8,128)(2,1)}, u32[]{:S(2)}, u32[]{:S(2)}) %all-to-all-start) | async-done | bytes 3145760 | tf_op jit(solution)/shard_map/all_to_all | solution.py:78
  169.6 10.6 fusion.58
  188.2 10.2 fusion.25
  208.6 11.1 all-reduce.10.cloned.1.call-start
  224.1 10.5 all-to-all-done.1
  246.5 152.0 %all-reduce.10.cloned.1.call-done = f32[1024,2048]{1,0:T(8,128)} async-done(((f32[1024,2048]{1,0:T(8,128)}), f32[1024,2048]{1,0:T(8,128)}) %all-reduce.10.cloned.1.call-update) | async-done | bytes 8388624 | tf_op jit(solution)/shard_map/psum | solution.py:98
  398.5 9.8 fusion.56
  414.1 11.5 fusion.54
  425.6 32.0 %add_convert_fusion.1 = (bf16[1024,2048]{1,0:T(8,128)(2,1)S(1)}, f32[1024,2048]{1,0:T(8,128)}) fusion(f32[1024,2048]{1,0:T(8,128)S(1)} %fusion.54, bf16[1024,2048]{1,0:T(8,128)(2,1)S(1)} %copy-done.6, bf16[2048,2048]{1,0:T(8,128)(2,1)} %param.24), kind=kOutput, calls=%fused_computation.29 | convolution fusion | flops 8740929536 | bytes 33554432 | tf_op jit(solution)/shard_map/td,fd->tf/dot_general | solution.py:110
  459.5 13.6 fusion.60
  483.3 12.6 convolution_convert_fusion
  495.9 130.4 %all-reduce.14.cloned.1.call-done = f32[1024,2048]{1,0:T(8,128)} async-done(((f32[1024,2048]{1,0:T(8,128)}), f32[1024,2048]{1,0:T(8,128)}) %all-reduce.14.cloned.1.call-update) | async-done | bytes 8388624 | tf_op jit(solution)/shard_map/psum | solution.py:113
  634.5 80.4 %all-reduce.12.cloned.1.call-done = bf16[1024,2048]{1,0:T(8,128)(2,1)} async-done(((bf16[1024,2048]{1,0:T(8,128)(2,1)}), bf16[1024,2048]{1,0:T(8,128)(2,1)}) %all-reduce.12.cloned.1.call-update) | async-done | bytes 4194320 | tf_op jit(solution)/shard_map/psum | solution.py:105
  714.9 12.2 multiply_add_fusion
  743.5 25.6 %all-to-all-done.2 = bf16[8,128,512]{2,1,0:T(8,128)(2,1)S(1)} async-done(((bf16[8,128,512]{2,1,0:T(8,128)(2,1)}), bf16[8,128,512]{2,1,0:T(8,128)(2,1)S(1)}, u32[]{:S(2)}, u32[]{:S(2)}) %all-to-all-start.2) | async-done | bytes 1048608 | tf_op jit(solution)/shard_map/all_to_all | solution.py:125
  784.7 10.7 multiply_reduce_fusion
  795.4 11.8 multiply_convert_fusion
  827.8 74.8 %all_to_all.48 = bf16[8,128,1536]{2,1,0:T(8,128)(2,1)} all-to-all(bf16[8,128,1536]{2,1,0:T(8,128)(2,1)} %bitcast.95), channel_id=1, replica_groups=mesh['seq'=8,'head'=4] {'seq'}, dimensions={0} | all-to-all | bytes 6291456 | tf_op jit(solution)/shard_map/all_to_all | solution.py:152
  916.8 11.8 convolution_bitcast_fusion
  938.3 16.4 fusion.53
  954.7 15.5 fusion.61
  970.9 15.4 fusion.50
  988.3 91.8 %all-reduce.16.cloned.1.call-done = f32[1024,2048]{1,0:T(8,128)} async-done(((f32[1024,2048]{1,0:T(8,128)}), f32[1024,2048]{1,0:T(8,128)}) %all-reduce.16.cloned.1.call-update) | async-done | bytes 8388624 | tf_op jit(solution)/shard_map/psum | solution.py:155
  1087.8 38.6 %all-reduce.4 = (f32[2048]{0:T(1024)S(1)}, f32[2048]{0:T(1024)S(1)}, f32[2048]{0:T(1024)S(1)}, f32[2048]{0:T(1024)S(1)}) all-reduce(f32[2048]{0:T(1024)S(1)} %get-tuple-element.16, f32[2048]{0:T(1024)S(1)} %get-tuple-element.21, f32[2048]{0:T(1024)S(1)} %copy-done.31, ...), channel_id=6, replica_groups=mesh['seq'=8,'head'=4] {'seq'}, use_global_device_ids=true, to_apply=%region_25.26.clone | all-reduce | flops 8192 | bytes 65536
  1129.0 11.9 add_convert_fusion
  1140.8 33.0 %reduce-scatter.7.cloned.1.call-done = f32[512,256]{1,0:T(8,128)} async-done(((f32[512,2048]{1,0:T(8,128)}), f32[512,256]{1,0:T(8,128)}) %reduce-scatter.7.cloned.1.call-update) | async-done | bytes 524304 | tf_op jit(solution)/shard_map/reduce_scatter | solution.py:164
  1173.9 285.9 %reduce-scatter.9.cloned.1.call-done = f32[256,2048]{1,0:T(8,128)} async-done(((f32[2048,2048]{1,0:T(8,128)}), f32[256,2048]{1,0:T(8,128)}) %reduce-scatter.9.cloned.1.call-update) | async-done | bytes 2097168 | tf_op jit(solution)/shard_map/reduce_scatter | solution.py:165
  1459.8 286.6 %reduce-scatter.11.cloned.1.call-done = f32[2048,256]{1,0:T(8,128)} async-done(((f32[2048,2048]{1,0:T(8,128)}), f32[2048,256]{1,0:T(8,128)}) %reduce-scatter.11.cloned.1.call-update) | async-done | bytes 2097168 | tf_op jit(solution)/shard_map/reduce_scatter | solution.py:166
  1746.4 210.9 %reduce-scatter.5.cloned.1.call-done = f32[256,3,512]{2,0,1:T(8,128)} async-done(((f32[2048,3,512]{2,0,1:T(8,128)}), f32[256,3,512]{2,0,1:T(8,128)}) %reduce-scatter.5.cloned.1.call-update) | async-done | bytes 1572880 | tf_op jit(solution)/shard_map/reduce_scatter | solution.py:163
  (165 shorter events, 200.8 us)
Async XLA Ops:
  7.2 232.5 %copy-start = (bf16[512,2048]{1,0:T(8,128)(2,1)S(1)}, bf16[512,2048]{1,0:T(8,128)(2,1)}, u32[]{:S(2)}) copy-start(bf16[512,2048]{1,0:T(8,128)(2,1)} %param.22) | copy-start | bytes 6291460
  43.7 24.0 %copy-start.21 = (s32[1024]{0:T(1024)}, s32[1024]{0:T(1024)S(1)}, u32[]{:S(2)}) copy-start(s32[1024]{0:T(1024)S(1)} %get-tuple-element.33) | copy-start | bytes 12292
  52.2 10.8 copy-start.2
  52.3 10.8 copy-start.15
  67.7 26.5 %copy-start.35 = (s32[1,1024]{1,0:T(1,128)S(1)}, s32[1,1024]{1,0:T(1,128)}, u32[]{:S(2)}) copy-start(s32[1,1024]{1,0:T(1,128)} %param.19) | copy-start | bytes 12292
  77.3 78.1 %all-to-all-start = ((bf16[8,128,1536]{2,1,0:T(8,128)(2,1)}), bf16[8,128,1536]{2,1,0:T(8,128)(2,1)}, u32[]{:S(2)}, u32[]{:S(2)}) async-start(bf16[8,128,1536]{2,1,0:T(8,128)(2,1)} %bitcast.94), calls=%async_computation | async-start | bytes 6291456 | tf_op jit(solution)/shard_map/all_to_all | solution.py:78
  89.6 110.2 %copy-start.19 = (s32[1024]{0:T(1024)}, s32[1024]{0:T(1024)S(1)}, u32[]{:S(2)}) copy-start(s32[1024]{0:T(1024)S(1)} %get-tuple-element.34) | copy-start | bytes 12292
  94.2 70.7 %copy-start.23 = (s32[1024]{0:T(1024)}, s32[1024]{0:T(1024)S(1)}, u32[]{:S(2)}) copy-start(s32[1024]{0:T(1024)S(1)} %fusion.43) | copy-start | bytes 12292
  205.0 29.6 %all-to-all-start.1 = ((bf16[8,128,512]{2,1,0:T(8,128)(2,1)}), bf16[8,128,512]{2,1,0:T(8,128)(2,1)S(1)}, u32[]{:S(2)}, u32[]{:S(2)}) async-start(bf16[8,128,512]{2,1,0:T(8,128)(2,1)} %bitcast.98), calls=%async_computation.1 | async-start | bytes 2097152 | tf_op jit(solution)/shard_map/all_to_all | solution.py:96
  208.6 189.9 %all-reduce.10.cloned.1.call-start = ((), (), s32[]{:S(2)}) async-start(), calls=%async_computation.8 | async-start | bytes 16777216 | tf_op jit(solution)/shard_map/psum | solution.py:98
  224.1 22.3 %copy-start.25 = (s32[1024]{0:T(1024)}, s32[1024]{0:T(1024)S(1)}, u32[]{:S(2)}) copy-start(s32[1024]{0:T(1024)S(1)} %fusion.44) | copy-start | bytes 12292
  246.4 379.9 %all-reduce.14.cloned.1.call-start = ((), (), s32[]{:S(2)}) async-start(), calls=%async_computation.10 | async-start | bytes 16777216 | tf_op jit(solution)/shard_map/psum | solution.py:113
  408.3 17.3 copy-start.9
  414.1 11.5 copy-start.17
  414.1 11.5 copy-start.6
  425.6 32.0 %copy-start.5 = (f32[1024,2048]{1,0:T(8,128)}, f32[1024,2048]{1,0:T(8,128)S(1)}, u32[]{:S(2)}) copy-start(f32[1024,2048]{1,0:T(8,128)S(1)} %fusion.54) | copy-start | bytes 25165828
  473.1 241.8 %all-reduce.12.cloned.1.call-start = ((), (), s32[]{:S(2)}) async-start(), calls=%async_computation.9 | async-start | bytes 8388608 | tf_op jit(solution)/shard_map/psum | solution.py:105
  483.3 143.0 %copy-start.10 = (f32[1024]{0:T(1024)S(1)}, f32[1024]{0:T(1024)}, u32[]{:S(2)}) copy-start(f32[1024]{0:T(1024)} %copy-done.9) | copy-start | bytes 12292
  483.3 143.0 %copy-start.18 = (f32[1024]{0:T(1024)S(1)}, f32[1024]{0:T(1024)}, u32[]{:S(2)}) copy-start(f32[1024]{0:T(1024)} %copy-done.17) | copy-start | bytes 12292
  483.3 143.0 %copy-start.30 = (f32[2048]{0:T(1024)S(1)}, f32[2048]{0:T(1024)}, u32[]{:S(2)}) copy-start(f32[2048]{0:T(1024)} %param.27) | copy-start | bytes 24580
  732.8 10.7 copy-start.12
  732.8 10.7 copy-start.14
  732.8 36.3 %copy-start.24 = (s32[1024]{0:T(1024)S(1)}, s32[1024]{0:T(1024)}, u32[]{:S(2)}) copy-start(s32[1024]{0:T(1024)} %copy-done.23) | copy-start | bytes 12292
  737.9 31.2 %all-to-all-start.2 = ((bf16[8,128,512]{2,1,0:T(8,128)(2,1)}), bf16[8,128,512]{2,1,0:T(8,128)(2,1)S(1)}, u32[]{:S(2)}, u32[]{:S(2)}) async-start(bf16[8,128,512]{2,1,0:T(8,128)(2,1)} %bitcast.99), calls=%async_computation.2 | async-start | bytes 2097152 | tf_op jit(solution)/shard_map/all_to_all | solution.py:125
  743.4 336.7 %all-reduce.16.cloned.1.call-start = ((), (), s32[]{:S(2)}) async-start(), calls=%async_computation.11 | async-start | bytes 16777216 | tf_op jit(solution)/shard_map/psum | solution.py:155
  818.2 84.4 %copy-start.26 = (s32[1024]{0:T(1024)S(1)}, s32[1024]{0:T(1024)}, u32[]{:S(2)}) copy-start(s32[1024]{0:T(1024)} %copy-done.25) | copy-start | bytes 12292
  928.7 245.2 %reduce-scatter.7.cloned.1.call-start = ((), (), s32[]{:S(2)}) async-start(), calls=%async_computation.13 | async-start | bytes 4718592 | tf_op jit(solution)/shard_map/reduce_scatter | solution.py:164
  938.2 521.6 %reduce-scatter.9.cloned.1.call-start = ((), (), s32[]{:S(2)}) async-start(), calls=%async_computation.14 | async-start | bytes 18874368 | tf_op jit(solution)/shard_map/reduce_scatter | solution.py:165
  954.7 791.7 %reduce-scatter.11.cloned.1.call-start = ((), (), s32[]{:S(2)}) async-start(), calls=%async_computation.15 | async-start | bytes 18874368 | tf_op jit(solution)/shard_map/reduce_scatter | solution.py:166
  970.3 987.0 %reduce-scatter.5.cloned.1.call-start = ((), (), s32[]{:S(2)}) async-start(), calls=%async_computation.12 | async-start | bytes 14155776 | tf_op jit(solution)/shard_map/reduce_scatter | solution.py:163
  988.2 99.5 %copy-start.31 = (f32[2048]{0:T(1024)S(1)}, f32[2048]{0:T(1024)}, u32[]{:S(2)}) copy-start(f32[2048]{0:T(1024)} %get-tuple-element.14) | copy-start | bytes 24580
  988.3 99.5 %copy-start.32 = (f32[2048]{0:T(1024)S(1)}, f32[2048]{0:T(1024)}, u32[]{:S(2)}) copy-start(f32[2048]{0:T(1024)} %get-tuple-element.20) | copy-start | bytes 24580
  (23 other events, 105.9 us)
Sparse Core Ops, SparseCore 0:
  246.6 151.9 all-reduce.9
  473.2 153.0 all-reduce.13
  629.2 85.6 all-reduce.11
  928.8 151.3 all-reduce.15
  1084.6 89.2 reduce-scatter.6
  1178.1 281.6 reduce-scatter.8
  1464.6 281.6 reduce-scatter.10
  1750.5 206.6 reduce-scatter.4
where the time goes:
time: 1970 us; the launch traced here: 1960 us
  waiting for transfers between devices  1370 us (70%)
  matrix products  209 us (11%)
  local copies, waits for them, and re-layouts  134 us (7%)
  blocking collectives  113 us (6%)
  other arithmetic  96.8 us (5%)
  starting transfers between devices  27.9 us (1%)
    reduce_scatter x1, waiting for transfers between devices, local(): lax.psum_scatter(down_grad, 'seq', scatter_dimension=1, tiled=True)  287 us
    reduce_scatter x1, waiting for transfers between devices, local(): lax.psum_scatter(up_grad, 'seq', scatter_dimension=0, tiled=True)  286 us
    reduce_scatter x1, waiting for transfers between devices, local(): lax.psum_scatter(qkv_grad, 'seq', scatter_dimension=0, tiled=True)  211 us
    psum x1, waiting for transfers between devices, local(): lax.psum(jnp.dot(context, w_out, preferred_element_type=jnp.float32), 'he...  152 us
    psum x1, waiting for transfers between devices, local(): lax.psum(jnp.einsum('tf,df->td', up_bar, w_up, preferred_element_type=jnp...  130 us
    psum x1, waiting for transfers between devices, local(): lax.psum(jnp.einsum('tsc,dsc->td', qkv_bar, w_qkv, preferred_element_type...  91.8 us
    psum x1, waiting for transfers between devices, local(): lax.psum(jnp.dot(act_low, w_down, preferred_element_type=jnp.float32).ast...  80.4 us
    all_to_all x1, blocking collectives, local(): lax.all_to_all(stacked[arrival_order], 'seq', split_axis=0, concat_axis=0...  74.8 us
  transfers between devices with their start and end apart: 11, of which 11 were waited for; matrix products, arithmetic and copies ran while one was open for 6% of the time, Pallas kernels for 0%

commit v1 on v0

v1 whole, which is shorter than its diff:
```python
from functools import partial
import math

import jax
import jax.numpy as jnp
from jax import lax
from jax.experimental import pallas as pl
from jax.experimental.pallas import tpu as pltpu
from jax.sharding import PartitionSpec as P

HEAD_DIM = 128
F32 = jnp.float32
BF16 = jnp.bfloat16
MIB = 1 << 20


def params(limit=40):
    return pltpu.CompilerParams(vmem_limit_bytes=limit * MIB)


def cost(flops, moved, special=0):
    return pl.CostEstimate(flops=int(flops), bytes_accessed=int(moved), transcendentals=int(special))


def dot(a, b, contract=((1,), (0,))):
    return lax.dot_general(a, b, (contract, ((), ())), preferred_element_type=F32)


NT = ((1,), (1,))
TN = ((0,), (0,))


def matmul(a, b, transposed=False, start=0, rows=None, tile_m=512, tile_n=512, out=BF16):
    rows = rows or a.shape[0]
    depth = a.shape[1]
    width = b.shape[0] if transposed else b.shape[1]
    tile_m, tile_n = min(tile_m, rows), min(tile_n, width)
    first = start // tile_m

    def body(a_ref, b_ref, o_ref):
        o_ref[...] = dot(a_ref[...], b_ref[...], NT if transposed else ((1,), (0,))).astype(out)

    return pl.pallas_call(
        body,
        grid=(rows // tile_m, width // tile_n),
        in_specs=[
            pl.BlockSpec((tile_m, depth), lambda i, j: (i + first, 0)),
            pl.BlockSpec((tile_n, depth), lambda i, j: (j, 0))
            if transposed
            else pl.BlockSpec((depth, tile_n), lambda i, j: (0, j)),
        ],
        out_specs=pl.BlockSpec((tile_m, tile_n), lambda i, j: (i, j)),
        out_shape=jax.ShapeDtypeStruct((rows, width), out),
        compiler_params=params(),
        cost_estimate=cost(2 * rows * width * depth, 2 * (rows * depth + width * depth + rows * width)),
    )(a, b)


def project(a, w3):
    rows, depth = a.shape
    width = w3.shape[2]

    def body(a_ref, w_ref, o_ref):
        o_ref[0] = dot(a_ref[...], w_ref[0]).astype(BF16)

    return pl.pallas_call(
        body,
        grid=(3,),
        in_specs=[
            pl.BlockSpec((rows, depth), lambda s: (0, 0)),
            pl.BlockSpec((1, depth, width), lambda s: (s, 0, 0)),
        ],
        out_specs=pl.BlockSpec((1, rows, width), lambda s: (s, 0, 0)),
        out_shape=jax.ShapeDtypeStruct((3, rows, width), BF16),
        compiler_params=params(),
        cost_estimate=cost(6 * rows * width * depth, 2 * (rows * depth + 3 * width * (depth + rows))),
    )(a, w3)


def project_back(g3, w3, start, rows, tile_n=512):
    width, depth = g3.shape[2], w3.shape[1]
    first = start // rows

    def body(g_ref, w_ref, o_ref):
        total = dot(g_ref[0], w_ref[0], NT)
        total += dot(g_ref[1], w_ref[1], NT)
        total += dot(g_ref[2], w_ref[2], NT)
        o_ref[...] = total.astype(BF16)

    return pl.pallas_call(
        body,
        grid=(depth // tile_n,),
        in_specs=[
            pl.BlockSpec((3, rows, width), lambda j: (0, first, 0)),
            pl.BlockSpec((3, tile_n, width), lambda j: (0, j, 0)),
        ],
        out_specs=pl.BlockSpec((rows, tile_n), lambda j: (0, j)),
        out_shape=jax.ShapeDtypeStruct((rows, depth), BF16),
        compiler_params=params(),
        cost_estimate=cost(6 * rows * width * depth, 2 * (rows * depth + 3 * width * (depth + rows))),
    )(g3, w3)


def mlp(normed, cot, w_up, w_down, tile=256):
    rows, depth = normed.shape
    width = w_up.shape[1]

    def body(n_ref, c_ref, u_ref, d_ref, act_ref, bar_ref):
        up = dot(n_ref[...], u_ref[...])
        grad = dot(c_ref[...], d_ref[...], NT)
        bell = jnp.exp(up * up * -0.5)
        t = 1.0 / (1.0 + (0.3275911 / math.sqrt(2.0)) * jnp.abs(up))
        poly = t * (
            0.127414796 + t * (-0.142248368 + t * (0.7107068705 + t * (-0.7265760135 + t * 0.5307027145)))
        )
        tail = poly * bell
        phi = jnp.where(up < 0.0, tail, 1.0 - tail)
        act_ref[...] = (up * phi).astype(BF16)
        slope = phi + up * bell * (1.0 / math.sqrt(2.0 * math.pi))
        bar_ref[...] = (slope * grad).astype(BF16)

    return pl.pallas_call(
        body,
        grid=(width // tile,),
        in_specs=[
            pl.BlockSpec((rows, depth), lambda j: (0, 0)),
            pl.BlockSpec((rows, depth), lambda j: (0, 0)),
            pl.BlockSpec((depth, tile), lambda j: (0, j)),
            pl.BlockSpec((tile, depth), lambda j: (j, 0)),
        ],
        out_specs=[pl.BlockSpec((rows, tile), lambda j: (0, j))] * 2,
        out_shape=[jax.ShapeDtypeStruct((rows, width), BF16)] * 2,
        compiler_params=params(),
        cost_estimate=cost(
            4 * rows * width * depth, 4 * (rows * depth + depth * width + rows * width), rows * width
        ),
    )(normed, cot, w_up, w_down)


def attend(qkv, pos_col, start_col, pos_row, tile=256):
    _, rows, width = qkv.shape
    heads = width // HEAD_DIM
    factor = 1.0 / math.sqrt(HEAD_DIM)

    def body(q_ref, kv_ref, pc_ref, sc_ref, pr_ref, o_ref):
        keys = pr_ref[...]
        seen = (keys <= pc_ref[...]) & (keys >= sc_ref[...])
        bias = jnp.where(seen, 0.0, -1e30)
        for head in range(heads):
            cols = slice(head * HEAD_DIM, (head + 1) * HEAD_DIM)
            scores = dot(q_ref[0, :, cols], kv_ref[1, :, cols], NT) * factor + bias
            peak = jnp.max(scores, axis=-1, keepdims=True)
            grown = jnp.exp(scores - peak)
            total = jnp.sum(grown, axis=-1, keepdims=True)
            probs = (grown * (1.0 / total)).astype(BF16)
            o_ref[:, cols] = dot(probs, kv_ref[2, :, cols]).astype(BF16)

    return pl.pallas_call(
        body,
        grid=(rows // tile,),
        in_specs=[
            pl.BlockSpec((1, tile, width), lambda i: (0, i, 0)),
            pl.BlockSpec((3, rows, width), lambda i: (0, 0, 0)),
            pl.BlockSpec((tile, 1), lambda i: (i, 0)),
            pl.BlockSpec((tile, 1), lambda i: (i, 0)),
            pl.BlockSpec((1, rows), lambda i: (0, 0)),
        ],
        out_specs=pl.BlockSpec((tile, width), lambda i: (i, 0)),
        out_shape=jax.ShapeDtypeStruct((rows, width), BF16),
        compiler_params=params(),
        cost_estimate=cost(8 * rows * rows * width, 10 * rows * width, heads * rows * rows),
    )(qkv, qkv, pos_col, start_col, pos_row)


def attend_back(qkv, bar, pos_col, pos_row, start_row, tile=256):
    _, rows, width = qkv.shape
    heads = width // HEAD_DIM
    factor = 1.0 / math.sqrt(HEAD_DIM)

    def body(q_ref, kv_ref, g_ref, pc_ref, pr_ref, sr_ref, o_ref, dk, dv):
        step = pl.program_id(0)
        keys = pc_ref[...]
        seen = (keys <= pr_ref[...]) & (keys >= sr_ref[...])
        bias = jnp.where(seen, 0.0, -1e30)

        @pl.when(step == 0)
        def _():
            dk[...] = jnp.zeros_like(dk)
            dv[...] = jnp.zeros_like(dv)

        for head in range(heads):
            cols = slice(head * HEAD_DIM, (head + 1) * HEAD_DIM)
            q, k, v, g = q_ref[0, :, cols], kv_ref[1, :, cols], kv_ref[2, :, cols], g_ref[:, cols]
            scores = dot(k, q, NT) * factor + bias
            peak = jnp.max(scores, axis=0, keepdims=True)
            grown = jnp.exp(scores - peak)
            probs = grown * (1.0 / jnp.sum(grown, axis=0, keepdims=True))
            dv[:, cols] += dot(probs.astype(BF16), g)
            probs_bar = dot(v, g, NT)
            inner = jnp.sum(probs * probs_bar, axis=0, keepdims=True)
            scores_bar = (probs * (probs_bar - inner)).astype(BF16)
            dk[:, cols] += dot(scores_bar, q)
            dq = dot(scores_bar, k, TN) * factor
            o_ref[0, pl.ds(pl.multiple_of(step * tile, tile), tile), cols] = dq.astype(BF16)

        @pl.when(step == pl.num_programs(0) - 1)
        def _():
            o_ref[1] = (dk[...] * factor).astype(BF16)
            o_ref[2] = dv[...].astype(BF16)

    return pl.pallas_call(
        body,
        grid=(rows // tile,),
        in_specs=[
            pl.BlockSpec((1, tile, width), lambda i: (0, i, 0)),
            pl.BlockSpec((3, rows, width), lambda i: (0, 0, 0)),
            pl.BlockSpec((tile, width), lambda i: (i, 0)),
            pl.BlockSpec((rows, 1), lambda i: (0, 0)),
            pl.BlockSpec((1, tile), lambda i: (0, i)),
            pl.BlockSpec((1, tile), lambda i: (0, i)),
        ],
        out_specs=pl.BlockSpec((3, rows, width), lambda i: (0, 0, 0)),
        out_shape=jax.ShapeDtypeStruct((3, rows, width), BF16),
        scratch_shapes=[pltpu.VMEM((rows, width), F32)] * 2,
        compiler_params=params(),
        cost_estimate=cost(16 * rows * rows * width, 16 * rows * width, heads * rows * rows),
    )(qkv, qkv, bar, pos_col, pos_row, start_row)


def weight_grad(ids, left, right, received=None):
    count = ids.shape[0]
    rows, depth = left.shape
    block = depth // (2 * count)
    if block % 128:
        picked = jnp.take(left.reshape(rows, 2 * count, block), ids, axis=1).reshape(rows, depth // 2)
        wide = depth // 256
        padded = jnp.concatenate([picked, picked], axis=1)
        if received is not None:
            received = received.reshape(wide, 128, -1)
        result = weight_grad(jnp.arange(wide, dtype=jnp.int32), padded, right, received)
        return result.reshape(count, block, -1)
    if right.ndim == 2:
        right = right[None]
    parts, _, width = right.shape

    def body(ids_ref, l_ref, r_ref, *rest):
        o_ref = rest[-1]
        for part in range(parts):
            cols = slice(part * width, (part + 1) * width)
            total = dot(l_ref[...], r_ref[part], TN)
            if received is not None:
                total += rest[0][0, :, cols].astype(F32)
            o_ref[0, :, cols] = total.astype(BF16)

    specs = [
        pl.BlockSpec((rows, block), lambda j, ids: (0, ids[j])),
        pl.BlockSpec((parts, rows, width), lambda j, ids: (0, 0, 0)),
    ]
    result = pl.BlockSpec((1, block, parts * width), lambda j, ids: (j, 0, 0))
    more = []
    if received is not None:
        specs.append(result)
        more.append(received)
    return pl.pallas_call(
        body,
        grid_spec=pltpu.PrefetchScalarGridSpec(
            num_scalar_prefetch=1, grid=(count,), in_specs=specs, out_specs=result
        ),
        out_shape=jax.ShapeDtypeStruct((count, block, parts * width), BF16),
        compiler_params=params(),
        cost_estimate=cost(
            rows * depth * parts * width, rows * depth + 2 * rows * parts * width + 2 * depth * parts * width
        ),
    )(ids, left, right, *more)


def normalize(values):
    centre = values - jnp.mean(values, axis=-1, keepdims=True)
    scaling = lax.rsqrt(jnp.mean(centre * centre, axis=-1, keepdims=True) + 1e-05)
    return (centre * scaling, scaling)


def norm_back(upstream, unit, scaling, gain):
    scaled = upstream * gain
    inner = (
        scaled
        - jnp.mean(scaled, axis=-1, keepdims=True)
        - unit * jnp.mean(scaled * unit, axis=-1, keepdims=True)
    )
    return (scaling * inner, jnp.sum(upstream * unit, axis=0), jnp.sum(upstream, axis=0))


def local(
    n_seq,
    n_head,
    tokens,
    codebook,
    codes,
    modality,
    segments,
    sequence_source,
    w_qkv,
    w_out,
    w_up,
    w_down,
    norm1_gain,
    norm1_shift,
    norm2_gain,
    norm2_shift,
    cotangent,
):
    rows, depth = tokens.shape
    me, own = lax.axis_index("seq"), lax.axis_index("head")
    share = rows // n_seq // n_head
    slice_rows = rows // n_head
    half = rows // 2
    w3 = jnp.transpose(w_qkv, (1, 0, 2))

    def swap(x, flip, axis="head"):
        size = n_head if axis == "head" else n_seq
        return lax.ppermute(x, axis, [(i, i ^ flip) for i in range(size)])

    def gather(x):
        core, across = swap(x, 1), swap(x, 2)
        return jnp.concatenate([x, core], axis=0), jnp.concatenate([across, swap(across, 1)], axis=0)

    def scatter_sum(high, low):
        passed = high[:slice_rows].astype(F32) + swap(high[slice_rows:], 1).astype(F32)
        across = swap(passed.astype(BF16), 2)
        near = low[:slice_rows].astype(F32) + swap(low[slice_rows:], 1).astype(F32)
        return near + across.astype(F32)

    def exchange(x):
        return lax.all_to_all(x, "seq", split_axis=0, concat_axis=0, tiled=True)

    source = sequence_source.reshape(n_seq, rows)
    places = jnp.arange(rows, dtype=jnp.int32)
    groups = source // rows
    offsets = source % rows
    leaving = groups == me
    coming = lax.dynamic_index_in_dim(groups, me, 0) == jnp.arange(n_seq, dtype=jnp.int32)[:, None]
    upper = (places[:, None] <= places[None, :]).astype(BF16)
    counts = jnp.dot(
        jnp.concatenate([leaving, coming], axis=0).astype(BF16), upper, preferred_element_type=F32
    ).astype(jnp.int32)
    leaving_rank = jnp.where(leaving, counts[:n_seq] - 1, -1)
    coming_rank = jnp.where(coming, counts[n_seq:] - 1, -1)
    lanes = jnp.arange(share, dtype=jnp.int32)

    def listed(rank, value, blocks):
        wanted = (own ^ jnp.asarray(blocks, jnp.int32))[:, None] * share + lanes[None, :]
        hit = rank[None, :, None, :] == wanted[:, None, :, None]
        return jnp.sum(jnp.where(hit, value[None, :, None, :], 0), axis=-1).reshape(-1)

    sent = listed(leaving_rank, offsets, [0])
    pick = (sent[:, None] == places[None, :]).astype(BF16)
    code = jnp.where(modality == 1, codes, -1)
    sent_code = jnp.sum(jnp.where(sent[:, None] == places[None, :], code[None, :], 0), axis=-1)
    pick_code = (
        sent_code[:, None] == jnp.arange(codebook.shape[0], dtype=jnp.int32)[None, :]
    ).astype(BF16)
    leaving_embedded = (
        jnp.dot(pick, tokens, preferred_element_type=F32)
        + jnp.dot(pick_code, codebook, preferred_element_type=F32)
    ).astype(BF16)
    leaving_cot = jnp.dot(pick, cotangent, preferred_element_type=F32).astype(BF16)

    embedded = exchange(leaving_embedded).astype(F32)
    cot_slice = exchange(leaving_cot)

    every = list(range(n_head))
    sent_all = listed(leaving_rank, offsets, every)
    segment_row = segments[0]
    begin = jnp.sum((segment_row[:, None] < segment_row[None, :]).astype(jnp.int32), axis=0)
    packed = listed(coming_rank, jnp.broadcast_to(begin * rows + places, (n_seq, rows)), every)
    position, start = packed % rows, packed // rows
    back = (places[:, None] == sent_all[None, :]).astype(BF16)

    unit_one, scale_one = normalize(embedded)
    normed_one = jnp.concatenate(gather((unit_one * norm1_gain + norm1_shift).astype(BF16)), axis=0)
    qkv = project(normed_one, w3)
    mixed = attend(qkv, position[:, None], start[:, None], position[None, :])
    attended = scatter_sum(
        matmul(mixed, w_out, start=half, rows=half), matmul(mixed, w_out, start=0, rows=half)
    )
    hidden_in = embedded + attended
    unit_two, scale_two = normalize(hidden_in)
    normed_low, normed_high = gather((unit_two * norm2_gain + norm2_shift).astype(BF16))
    cot_low, cot_high = gather(cot_slice)
    act_low, bar_low = mlp(normed_low, cot_low, w_up, w_down)
    act_high, bar_high = mlp(normed_high, cot_high, w_up, w_down)

    normed_two_bar = scatter_sum(
        matmul(bar_high, w_up, transposed=True), matmul(bar_low, w_up, transposed=True)
    )
    normed_two = jnp.concatenate([normed_low, normed_high], axis=0)
    cot_all = jnp.concatenate([cot_low, cot_high], axis=0)
    act = jnp.concatenate([act_low, act_high], axis=0)
    up_bar = jnp.concatenate([bar_low, bar_high], axis=0)

    steps = 2 * jnp.arange(n_seq // 2, dtype=jnp.int32)
    mine, others = me ^ steps, me ^ 1 ^ steps

    def reduce_grad(left, right):
        passed = swap(weight_grad(others, left, right), 1, "seq")
        mine_sum = weight_grad(mine, left, right, passed)
        total = mine_sum[0].astype(F32)
        for j in range(1, n_seq // 2):
            total = total + swap(mine_sum[j], 2 * j, "seq").astype(F32)
        return total

    down_grad = reduce_grad(cot_all, act).T
    up_grad = reduce_grad(normed_two, up_bar)

    branch = scatter_sum(matmul(act_high, w_down), matmul(act_low, w_down))
    output_slice = (hidden_in + branch).astype(BF16)

    def send_home(x):
        return jnp.dot(
            back, jnp.concatenate(gather(exchange(x)), axis=0), preferred_element_type=F32
        ).astype(BF16)

    block_output = send_home(output_slice)

    hidden_part, gain_two, shift_two = norm_back(normed_two_bar, unit_two, scale_two, norm2_gain)
    hidden_bar = cot_slice.astype(F32) + hidden_part
    hidden_low = jnp.concatenate(gather(hidden_bar.astype(BF16)), axis=0)
    context_bar = matmul(hidden_low, w_out, transposed=True)
    out_grad = reduce_grad(hidden_low, mixed).T
    qkv_bar = attend_back(qkv, context_bar, position[:, None], position[None, :], start[None, :])
    normed_one_bar = scatter_sum(
        project_back(qkv_bar, w3, half, half), project_back(qkv_bar, w3, 0, half)
    )
    qkv_grad = reduce_grad(normed_one, qkv_bar)
    qkv_grad = jnp.transpose(qkv_grad.reshape(depth // n_seq, 3, -1), (0, 1, 2))
    input_part, gain_one, shift_one = norm_back(normed_one_bar, unit_one, scale_one, norm1_gain)
    input_grad = send_home((hidden_bar + input_part).astype(BF16))

    vectors = jnp.stack([gain_one, shift_one, gain_two, shift_two])
    vectors = vectors + swap(vectors, 1)
    vectors = vectors + swap(vectors, 2)
    vectors = jnp.transpose(vectors.reshape(4, n_seq, depth // n_seq), (1, 0, 2))
    vectors = jnp.sum(exchange(vectors), axis=0)
    return (
        block_output,
        input_grad,
        qkv_grad,
        out_grad,
        up_grad,
        down_grad,
        vectors[0],
        vectors[1],
        vectors[2],
        vectors[3],
    )


def solution(mesh):
    return jax.shard_map(
        partial(local, mesh.shape["seq"], mesh.shape["head"]),
        mesh=mesh,
        in_specs=(
            P("seq", None),
            P(),
            P("seq"),
            P("seq"),
            P("seq", None),
            P(),
            P(None, None, "head"),
            P("head", None),
            P(None, "head"),
            P("head", None),
            P(),
            P(),
            P(),
            P(),
            P("seq", None),
        ),
        out_specs=(
            P("seq", None),
            P("seq", None),
            P("seq", None, "head"),
            P("head", "seq"),
            P("seq", "head"),
            P("head", "seq"),
            P("seq"),
            P("seq"),
            P("seq"),
            P("seq"),
        ),
        check_vma=False,
    )
```

time: 1970 us -> 873 us (0.44)
  waiting for transfers between devices: 1370 us -> 423 us
  matrix products: 209 us -> 22.7 us
  Pallas kernels: 0 us -> 154 us
  blocking collectives: 113 us -> 33 us
  starting transfers between devices: 27.9 us -> 106 us
  local copies, waits for them, and re-layouts: 134 us -> 62.7 us
  other arithmetic: 96.8 us -> 64.2 us
    reduce_scatter x4 -> x0, waiting for transfers between devices: 816 us -> none  [the longest x1 287 us: local(): lax.psum_scatter(down_grad, 'seq', scatter_dimension=1, tiled=True)]
    psum x4 -> x0, waiting for transfers between devices: 455 us -> none  [the longest x1 152 us: local(): lax.psum(jnp.dot(context, w_out, preferred_element_type=jnp.float32), 'he...]
    ppermute x0 -> x48, waiting for transfers between devices: none -> 406 us  [swap(): return lax.ppermute(x, axis, [(i, i ^ flip) for i in range(size)])]
    dot_general x19 -> x6, matrix products: 209 us -> 22.7 us  [the longest x2 15.1 us: send_home(): jnp.dot(back, jnp.concatenate(gather(exchange(x)), axis=0), preferred_ele...]
    pallas_call x0 -> x22, Pallas kernels: none -> 154 us  [the longest x8 47.6 us: weight_grad(): pl.pallas_call(body, grid_spec=pltpu.PrefetchScalarGridSpec(num_scalar_pr...]
    ppermute x0 -> x48, starting transfers between devices: none -> 87.9 us  [swap(): return lax.ppermute(x, axis, [(i, i ^ flip) for i in range(size)])]
    all_to_all x3 -> x4, waiting for transfers between devices: 96.6 us -> 17.1 us  [exchange(): return lax.all_to_all(x, 'seq', split_axis=0, concat_axis=0, tiled=True)]
    gather x10 -> x0, local copies, waits for them, and re-layouts: 68 us -> none  [the longest x2 14.2 us: local(): qkv_bar = went[send_back].reshape(row_count, 3, local_width)]
  transfers between devices with their start and end apart: 11 -> 52, of which waited for: 11 -> 19; matrix products, arithmetic and copies ran while one was open for 6% -> 9% of each run, Pallas kernels for 0% -> 13%
where the time goes in v1:
time: 873 us; the launch traced here: 868 us
  waiting for transfers between devices  423 us (48%)
  Pallas kernels  154 us (18%)
  starting transfers between devices  106 us (12%)
  other arithmetic  64.2 us (7%)
  local copies, waits for them, and re-layouts  62.7 us (7%)
  blocking collectives  33 us (4%)
  matrix products  22.7 us (3%)
    ppermute x48, waiting for transfers between devices, swap(): return lax.ppermute(x, axis, [(i, i ^ flip) for i in range(size)])  406 us
    ppermute x48, starting transfers between devices, swap(): return lax.ppermute(x, axis, [(i, i ^ flip) for i in range(size)])  87.9 us
    pallas_call x8, Pallas kernels, weight_grad(): pl.pallas_call(body, grid_spec=pltpu.PrefetchScalarGridSpec(num_scalar_pr...  47.6 us
    unnamed x117, local copies, waits for them, and re-layouts  44.9 us
    all_to_all x1, blocking collectives, exchange(): return lax.all_to_all(x, 'seq', split_axis=0, concat_axis=0, tiled=True)  33 us
    pallas_call x2, Pallas kernels, mlp(): pl.pallas_call(body, grid=(width // tile,), in_specs=[pl.BlockSpec((rows,...  29.3 us
    pallas_call x7, Pallas kernels, matmul(): pl.pallas_call(body, grid=(rows // tile_m, width // tile_n), in_specs=[pl...  29.2 us
    pallas_call x1, Pallas kernels, attend_back(): pl.pallas_call(body, grid=(rows // tile,), in_specs=[pl.BlockSpec((1, til...  20.5 us
  transfers between devices with their start and end apart: 52, of which 19 were waited for; matrix products, arithmetic and copies ran while one was open for 9% of the time, Pallas kernels for 13%

profile of v1, /device:TPU:0, one launch (start us, length us, event | category | flops | bytes accessed | tf_op | source)
XLA Modules:
  0.0 867.9 jit_solution(11109407473760966309)
XLA Ops:
  8.3 33.0 %all_to_all.50 = bf16[8,32,2048]{2,1,0:T(8,128)(2,1)S(1)} all-to-all(bf16[8,32,2048]{2,1,0:T(8,128)(2,1)S(1)} %bitcast.120), channel_id=1, replica_groups=mesh['seq'=8,'head'=4] {'seq'}, dimensions={0} | all-to-all | bytes 2097152 | tf_op jit(solution)/shard_map/all_to_all | solution.py:334
  45.7 22.0 %collective-permute-done.1 = bf16[256,2048]{1,0:T(8,128)(2,1)} collective-permute-done((bf16[256,2048]{1,0:T(8,128)(2,1)}, bf16[256,2048]{1,0:T(8,128)(2,1)}, u32[]{:S(2)}, u32[]{:S(2)}) %collective-permute-start.1) | collective-permute-done | bytes 1048608 | tf_op jit(solution)/shard_map/ppermute | solution.py:321
  75.7 7.0 shard_map.249.q_ref.kv_ref
  82.7 11.0 %shard_map.250.a_ref = bf16[1024,512]{1,0:T(8,128)(2,1)S(1)} custom-call(bf16[3,1024,512]{2,1,0:T(8,128)(2,1)S(1)} %shard_map.249.q_ref.kv_ref, bf16[3,1024,512]{2,1,0:T(8,128)(2,1)S(1)} %shard_map.249.q_ref.kv_ref, s32[1024,1]{1,0:T(8,128)S(1)} %get-tuple-element.90.pc_ref, s32[1024,1]{1,0:T(8,128)S(1)} %get-tuple-element.89.sc_ref, ...), custom_call_target="tpu_custom_call" | custom-call | flops 4294967296 | bytes 5242880 | tf_op jit(solution)/shard_map/pallas_call | solution.py:158
  113.3 17.1 %all-to-all-done.1 = bf16[8,32,2048]{2,1,0:T(8,128)(2,1)} async-done(((bf16[8,32,2048]{2,1,0:T(8,128)(2,1)}), bf16[8,32,2048]{2,1,0:T(8,128)(2,1)}, u32[]{:S(2)}, u32[]{:S(2)}) %all-to-all-start.1) | async-done | bytes 1048608 | tf_op jit(solution)/shard_map/all_to_all | solution.py:334
  131.9 6.2 collective-permute-done.5
  144.5 16.0 %collective-permute-done.11 = bf16[256,2048]{1,0:T(8,128)(2,1)} collective-permute-done((bf16[256,2048]{1,0:T(8,128)(2,1)}, bf16[256,2048]{1,0:T(8,128)(2,1)}, u32[]{:S(2)}, u32[]{:S(2)}) %collective-permute-start.11) | collective-permute-done | bytes 1048608 | tf_op jit(solution)/shard_map/ppermute | solution.py:321
  161.0 21.6 %collective-permute-done.9 = bf16[256,2048]{1,0:T(8,128)(2,1)} collective-permute-done((bf16[256,2048]{1,0:T(8,128)(2,1)}, bf16[256,2048]{1,0:T(8,128)(2,1)}, u32[]{:S(2)}, u32[]{:S(2)}) %collective-permute-start.9) | collective-permute-done | bytes 1048608 | tf_op jit(solution)/shard_map/ppermute | solution.py:321
  193.2 14.7 %shard_map.255 = (bf16[512,2048]{1,0:T(8,128)(2,1)S(1)}, bf16[512,2048]{1,0:T(8,128)(2,1)S(1)}) custom-call(bf16[512,2048]{1,0:T(8,128)(2,1)S(1)} %pad_maximum_fusion.6.n_ref, bf16[512,2048]{1,0:T(8,128)(2,1)S(1)} %pad_maximum_fusion.7.c_ref, bf16[2048,2048]{1,0:T(8,128)(2,1)} %b_ref.12, bf16[2048,2048]{1,0:T(8,128)(2,1)} %b_ref.10), custom_call_target="tpu_custom_call" | custom-call | flops 8589934592 | bytes 25165824 | tf_op jit(solution)/shard_map/pallas_call | solution.py:122
  219.0 14.7 %shard_map.253 = (bf16[512,2048]{1,0:T(8,128)(2,1)S(1)}, bf16[512,2048]{1,0:T(8,128)(2,1)S(1)}) custom-call(bf16[512,2048]{1,0:T(8,128)(2,1)S(1)} %pad_maximum_fusion.4.n_ref, bf16[512,2048]{1,0:T(8,128)(2,1)S(1)} %pad_maximum_fusion.5.c_ref, bf16[2048,2048]{1,0:T(8,128)(2,1)} %b_ref.12, bf16[2048,2048]{1,0:T(8,128)(2,1)} %b_ref.10), custom_call_target="tpu_custom_call" | custom-call | flops 8589934592 | bytes 25165824 | tf_op jit(solution)/shard_map/pallas_call | solution.py:122
  265.0 6.2 shard_map.254
  274.6 11.8 %collective-permute-done.20 = bf16[256,2048]{1,0:T(8,128)(2,1)} collective-permute-done((bf16[256,2048]{1,0:T(8,128)(2,1)}, bf16[256,2048]{1,0:T(8,128)(2,1)}, u32[]{:S(2)}, u32[]{:S(2)}) %collective-permute-start.20) | collective-permute-done | bytes 1048608 | tf_op jit(solution)/shard_map/ppermute | solution.py:321
  289.2 19.2 %collective-permute-done.14 = bf16[256,2048]{1,0:T(8,128)(2,1)S(1)} collective-permute-done((bf16[256,2048]{1,0:T(8,128)(2,1)S(1)}, bf16[256,2048]{1,0:T(8,128)(2,1)S(1)}, u32[]{:S(2)}, u32[]{:S(2)}) %collective-permute-start.14) | collective-permute-done | bytes 1048608 | tf_op jit(solution)/shard_map/ppermute | solution.py:321
  314.4 7.1 shard_map.269
  325.5 12.5 %collective-permute-done.22 = bf16[256,2048]{1,0:T(8,128)(2,1)} collective-permute-done((bf16[256,2048]{1,0:T(8,128)(2,1)}, bf16[256,2048]{1,0:T(8,128)(2,1)}, u32[]{:S(2)}, u32[]{:S(2)}) %collective-permute-start.22) | collective-permute-done | bytes 1048608 | tf_op jit(solution)/shard_map/ppermute | solution.py:321
  338.5 7.0 shard_map.267
  357.9 20.5 %shard_map.260.g_ref.r_ref = bf16[3,1024,512]{2,1,0:T(8,128)(2,1)S(1)} custom-call(bf16[3,1024,512]{2,1,0:T(8,128)(2,1)S(1)} %copy-done.37, bf16[3,1024,512]{2,1,0:T(8,128)(2,1)S(1)} %copy-done.37, bf16[1024,512]{1,0:T(8,128)(2,1)S(1)} %shard_map.259.g_ref, s32[1024,1]{1,0:T(8,128)S(1)} %copy-done.29, s32[1,1024]{1,0:T(1,128)S(1)} %and_select_fusion.1.pr_ref, ...), custom_call_target="tpu_custom_call" | custom-call | flops 8589934592 | bytes 8388608 | tf_op jit(solution)/shard_map/pallas_call | solution.py:211
  410.6 13.1 %collective-permute-done.42.rest_0_ = bf16[4,256,2048]{2,1,0:T(8,128)(2,1)} collective-permute-done((bf16[4,256,2048]{2,1,0:T(8,128)(2,1)}, bf16[4,256,2048]{2,1,0:T(8,128)(2,1)}, u32[]{:S(2)}, u32[]{:S(2)}) %collective-permute-start.42) | collective-permute-done | bytes 4194336 | tf_op jit(solution)/shard_map/ppermute | solution.py:321
  425.8 7.2 shard_map.270
  440.7 72.9 %collective-permute-done.38.rest_0_ = bf16[4,256,2048]{2,1,0:T(8,128)(2,1)} collective-permute-done((bf16[4,256,2048]{2,1,0:T(8,128)(2,1)}, bf16[4,256,2048]{2,1,0:T(8,128)(2,1)}, u32[]{:S(2)}, u32[]{:S(2)}) %collective-permute-start.38) | collective-permute-done | bytes 4194336 | tf_op jit(solution)/shard_map/ppermute | solution.py:321
  514.1 7.4 shard_map.268
  524.5 14.4 %collective-permute-done.34.rest_0_ = bf16[4,256,512]{2,1,0:T(8,128)(2,1)} collective-permute-done((bf16[4,256,512]{2,1,0:T(8,128)(2,1)S(1)}, bf16[4,256,512]{2,1,0:T(8,128)(2,1)}, u32[]{:S(2)}, u32[]{:S(2)}) %collective-permute-start.34) | collective-permute-done | bytes 1048608 | tf_op jit(solution)/shard_map/ppermute | solution.py:321
  554.0 13.0 %collective-permute-done.45 = bf16[256,2048]{1,0:T(8,128)(2,1)} collective-permute-done((bf16[256,2048]{1,0:T(8,128)(2,1)S(1)}, bf16[256,2048]{1,0:T(8,128)(2,1)}, u32[]{:S(2)}, u32[]{:S(2)}) %collective-permute-start.45) | collective-permute-done | bytes 1048608 | tf_op jit(solution)/shard_map/ppermute | solution.py:321
  567.0 47.9 %collective-permute-start.40 = (bf16[256,2048]{1,0:T(8,128)(2,1)}, bf16[256,2048]{1,0:T(8,128)(2,1)}, u32[]{:S(2)}, u32[]{:S(2)}) collective-permute-start(bf16[256,2048]{1,0:T(8,128)(2,1)} %get-tuple-element.81), channel_id=1, source_target_pairs={{0,16},{4,20},{8,24},{12,28},{16,0},{20,4},{24,8},{28,12},{1,17},{... | collective-permute-start | bytes 3145736 | tf_op jit(solution)/shard_map/ppermute | solution.py:321
  622.5 64.6 %collective-permute-done.44 = bf16[256,2048]{1,0:T(8,128)(2,1)} collective-permute-done((bf16[256,2048]{1,0:T(8,128)(2,1)}, bf16[256,2048]{1,0:T(8,128)(2,1)}, u32[]{:S(2)}, u32[]{:S(2)}) %collective-permute-start.44) | collective-permute-done | bytes 1048608 | tf_op jit(solution)/shard_map/ppermute | solution.py:321
  695.3 42.4 %collective-permute-done.40 = bf16[256,2048]{1,0:T(8,128)(2,1)} collective-permute-done((bf16[256,2048]{1,0:T(8,128)(2,1)}, bf16[256,2048]{1,0:T(8,128)(2,1)}, u32[]{:S(2)}, u32[]{:S(2)}) %collective-permute-start.40) | collective-permute-done | bytes 1048608 | tf_op jit(solution)/shard_map/ppermute | solution.py:321
  746.0 18.6 %collective-permute-done.36 = bf16[256,512]{1,0:T(8,128)(2,1)S(1)} collective-permute-done((bf16[256,512]{1,0:T(8,128)(2,1)S(1)}, bf16[256,512]{1,0:T(8,128)(2,1)S(1)}, u32[]{:S(2)}, u32[]{:S(2)}) %collective-permute-start.36) | collective-permute-done | bytes 262176 | tf_op jit(solution)/shard_map/ppermute | solution.py:321
  790.1 7.5 fusion.20
  798.2 7.5 collective-permute-done.31
  805.7 17.8 %collective-permute-done.33 = bf16[256,1536]{1,0:T(8,128)(2,1)} collective-permute-done((bf16[256,1536]{1,0:T(8,128)(2,1)}, bf16[256,1536]{1,0:T(8,128)(2,1)}, u32[]{:S(2)}, u32[]{:S(2)}) %collective-permute-start.33) | collective-permute-done | bytes 786464 | tf_op jit(solution)/shard_map/ppermute | solution.py:321
  823.5 29.9 %collective-permute-done.32 = bf16[256,1536]{1,0:T(8,128)(2,1)} collective-permute-done((bf16[256,1536]{1,0:T(8,128)(2,1)}, bf16[256,1536]{1,0:T(8,128)(2,1)}, u32[]{:S(2)}, u32[]{:S(2)}) %collective-permute-start.32) | collective-permute-done | bytes 786464 | tf_op jit(solution)/shard_map/ppermute | solution.py:321
  860.1 7.5 fusion.17
  (298 shorter events, 246.7 us)
Async XLA Ops:
  99.7 30.7 %all-to-all-start.1 = ((bf16[8,32,2048]{2,1,0:T(8,128)(2,1)}), bf16[8,32,2048]{2,1,0:T(8,128)(2,1)}, u32[]{:S(2)}, u32[]{:S(2)}) async-start(bf16[8,32,2048]{2,1,0:T(8,128)(2,1)} %bitcast.119), calls=%async_computation.1 | async-start | bytes 2097152 | tf_op jit(solution)/shard_map/all_to_all | solution.py:334
  130.4 30.1 %collective-permute-start.11 = (bf16[256,2048]{1,0:T(8,128)(2,1)}, bf16[256,2048]{1,0:T(8,128)(2,1)}, u32[]{:S(2)}, u32[]{:S(2)}) collective-permute-start(bf16[256,2048]{1,0:T(8,128)(2,1)} %bitcast.6), channel_id=1, source_target_pairs={{0,2},{1,3},{2,0},{3,1},{4,6},{5,7},{6,4},{7,5},{8,10},{9,11},{10,... | collective-permute-start | bytes 3145736 | tf_op jit(solution)/shard_map/ppermute | solution.py:321
  143.0 39.6 %collective-permute-start.9 = (bf16[256,2048]{1,0:T(8,128)(2,1)}, bf16[256,2048]{1,0:T(8,128)(2,1)}, u32[]{:S(2)}, u32[]{:S(2)}) collective-permute-start(bf16[256,2048]{1,0:T(8,128)(2,1)} %add_convert_fusion.4), channel_id=1, source_target_pairs={{0,2},{1,3},{2,0},{3,1},{4,6},{5,7},{6,4},{7,5},{8,10},{9,11},{10,... | collective-permute-start | bytes 3145736 | tf_op jit(solution)/shard_map/ppermute | solution.py:321
  144.5 38.1 %collective-permute-start.7 = (bf16[256,2048]{1,0:T(8,128)(2,1)}, bf16[256,2048]{1,0:T(8,128)(2,1)}, u32[]{:S(2)}, u32[]{:S(2)}) collective-permute-start(bf16[256,2048]{1,0:T(8,128)(2,1)} %bitcast.6), channel_id=1, source_target_pairs={{0,1},{1,0},{2,3},{3,2},{4,5},{5,4},{6,7},{7,6},{8,9},{9,8},{10,11... | collective-permute-start | bytes 3145736 | tf_op jit(solution)/shard_map/ppermute | solution.py:321
  160.5 28.1 %collective-permute-start.6 = (bf16[256,2048]{1,0:T(8,128)(2,1)}, bf16[256,2048]{1,0:T(8,128)(2,1)S(1)}, u32[]{:S(2)}, u32[]{:S(2)}) collective-permute-start(bf16[256,2048]{1,0:T(8,128)(2,1)} %add_convert_fusion.4), channel_id=1, source_target_pairs={{0,1},{1,0},{2,3},{3,2},{4,5},{5,4},{6,7},{7,6},{8,9},{9,8},{10,11... | collective-permute-start | bytes 3145736 | tf_op jit(solution)/shard_map/ppermute | solution.py:321
  218.5 38.8 %collective-permute-start.19 = (bf16[256,2048]{1,0:T(8,128)(2,1)}, bf16[256,2048]{1,0:T(8,128)(2,1)}, u32[]{:S(2)}, u32[]{:S(2)}) collective-permute-start(bf16[256,2048]{1,0:T(8,128)(2,1)} %slice.165), channel_id=1, source_target_pairs={{0,1},{1,0},{2,3},{3,2},{4,5},{5,4},{6,7},{7,6},{8,9},{9,8},{10,11... | collective-permute-start | bytes 3145736 | tf_op jit(solution)/shard_map/ppermute | solution.py:321
  273.4 35.0 %collective-permute-start.14 = (bf16[256,2048]{1,0:T(8,128)(2,1)S(1)}, bf16[256,2048]{1,0:T(8,128)(2,1)S(1)}, u32[]{:S(2)}, u32[]{:S(2)}) collective-permute-start(bf16[256,2048]{1,0:T(8,128)(2,1)S(1)} %add_convert_fusion.3), channel_id=1, source_target_pairs={{0,2},{1,3},{2,0},{3,1},{4,6},{5,7},{6,4},{7,5},{8,10},{9,11},{10,... | collective-permute-start | bytes 3145736 | tf_op jit(solution)/shard_map/ppermute | solution.py:321
  321.5 102.2 %collective-permute-start.42 = (bf16[4,256,2048]{2,1,0:T(8,128)(2,1)}, bf16[4,256,2048]{2,1,0:T(8,128)(2,1)}, u32[]{:S(2)}, u32[]{:S(2)}) collective-permute-start(bf16[4,256,2048]{2,1,0:T(8,128)(2,1)} %shard_map.269), channel_id=1, source_target_pairs={{0,4},{4,0},{8,12},{12,8},{16,20},{20,16},{24,28},{28,24},{1,5},{5... | collective-permute-start | bytes 12582920 | tf_op jit(solution)/shard_map/ppermute | solution.py:321
  345.5 168.1 %collective-permute-start.38 = (bf16[4,256,2048]{2,1,0:T(8,128)(2,1)}, bf16[4,256,2048]{2,1,0:T(8,128)(2,1)}, u32[]{:S(2)}, u32[]{:S(2)}) collective-permute-start(bf16[4,256,2048]{2,1,0:T(8,128)(2,1)} %shard_map.267), channel_id=1, source_target_pairs={{0,4},{4,0},{8,12},{12,8},{16,20},{20,16},{24,28},{28,24},{1,5},{5... | collective-permute-start | bytes 12582920 | tf_op jit(solution)/shard_map/ppermute | solution.py:321
  347.6 270.6 %all-to-all-start.2 = ((bf16[8,32,2048]{2,1,0:T(8,128)(2,1)}), bf16[8,32,2048]{2,1,0:T(8,128)(2,1)}, u32[]{:S(2)}, u32[]{:S(2)}) async-start(bf16[8,32,2048]{2,1,0:T(8,128)(2,1)} %bitcast.7), calls=%async_computation.2 | async-start | bytes 2097152 | tf_op jit(solution)/shard_map/all_to_all | solution.py:334
  386.9 49.7 %collective-permute-start.25 = (bf16[256,2048]{1,0:T(8,128)(2,1)}, bf16[256,2048]{1,0:T(8,128)(2,1)}, u32[]{:S(2)}, u32[]{:S(2)}) collective-permute-start(bf16[256,2048]{1,0:T(8,128)(2,1)} %slice.169), channel_id=1, source_target_pairs={{0,1},{1,0},{2,3},{3,2},{4,5},{5,4},{6,7},{7,6},{8,9},{9,8},{10,11... | collective-permute-start | bytes 3145736 | tf_op jit(solution)/shard_map/ppermute | solution.py:321
  407.2 131.7 %collective-permute-start.34 = (bf16[4,256,512]{2,1,0:T(8,128)(2,1)S(1)}, bf16[4,256,512]{2,1,0:T(8,128)(2,1)}, u32[]{:S(2)}, u32[]{:S(2)}) collective-permute-start(bf16[4,256,512]{2,1,0:T(8,128)(2,1)S(1)} %shard_map.265), channel_id=1, source_target_pairs={{0,4},{4,0},{8,12},{12,8},{16,20},{20,16},{24,28},{28,24},{1,5},{5... | collective-permute-start | bytes 3145736 | tf_op jit(solution)/shard_map/ppermute | solution.py:321
  410.3 136.7 %collective-permute-start.24 = (bf16[256,2048]{1,0:T(8,128)(2,1)}, bf16[256,2048]{1,0:T(8,128)(2,1)S(1)}, u32[]{:S(2)}, u32[]{:S(2)}) collective-permute-start(bf16[256,2048]{1,0:T(8,128)(2,1)} %slice.167), channel_id=1, source_target_pairs={{0,1},{1,0},{2,3},{3,2},{4,5},{5,4},{6,7},{7,6},{8,9},{9,8},{10,11... | collective-permute-start | bytes 3145736 | tf_op jit(solution)/shard_map/ppermute | solution.py:321
  423.7 348.0 %collective-permute-start.30 = (bf16[4,256,1536]{2,1,0:T(8,128)(2,1)}, bf16[4,256,1536]{2,1,0:T(8,128)(2,1)}, u32[]{:S(2)}, u32[]{:S(2)}) collective-permute-start(bf16[4,256,1536]{2,1,0:T(8,128)(2,1)} %shard_map.263), channel_id=1, source_target_pairs={{0,4},{4,0},{8,12},{12,8},{16,20},{20,16},{24,28},{28,24},{1,5},{5... | collective-permute-start | bytes 9437192 | tf_op jit(solution)/shard_map/ppermute | solution.py:321
  436.6 114.0 %collective-permute-start.43 = (bf16[256,2048]{1,0:T(8,128)(2,1)}, bf16[256,2048]{1,0:T(8,128)(2,1)}, u32[]{:S(2)}, u32[]{:S(2)}) collective-permute-start(bf16[256,2048]{1,0:T(8,128)(2,1)} %get-tuple-element.76), channel_id=1, source_target_pairs={{0,8},{4,12},{8,0},{12,4},{16,24},{20,28},{24,16},{28,20},{1,9},{5... | collective-permute-start | bytes 3145736 | tf_op jit(solution)/shard_map/ppermute | solution.py:321
  513.6 33.4 %collective-permute-start.26 = (bf16[256,2048]{1,0:T(8,128)(2,1)}, bf16[256,2048]{1,0:T(8,128)(2,1)}, u32[]{:S(2)}, u32[]{:S(2)}) collective-permute-start(bf16[256,2048]{1,0:T(8,128)(2,1)} %add_convert_fusion), channel_id=1, source_target_pairs={{0,2},{1,3},{2,0},{3,1},{4,6},{5,7},{6,4},{7,5},{8,10},{9,11},{10,... | collective-permute-start | bytes 3145736 | tf_op jit(solution)/shard_map/ppermute | solution.py:321
  538.9 28.1 %collective-permute-start.45 = (bf16[256,2048]{1,0:T(8,128)(2,1)S(1)}, bf16[256,2048]{1,0:T(8,128)(2,1)}, u32[]{:S(2)}, u32[]{:S(2)}) collective-permute-start(bf16[256,2048]{1,0:T(8,128)(2,1)S(1)} %copy-done.47), channel_id=1, source_target_pairs={{0,24},{4,28},{8,16},{12,20},{16,8},{20,12},{24,0},{28,4},{1,25},{... | collective-permute-start | bytes 3145736 | tf_op jit(solution)/shard_map/ppermute | solution.py:321
  547.0 140.2 %collective-permute-start.44 = (bf16[256,2048]{1,0:T(8,128)(2,1)}, bf16[256,2048]{1,0:T(8,128)(2,1)}, u32[]{:S(2)}, u32[]{:S(2)}) collective-permute-start(bf16[256,2048]{1,0:T(8,128)(2,1)} %get-tuple-element.78), channel_id=1, source_target_pairs={{0,16},{4,20},{8,24},{12,28},{16,0},{20,4},{24,8},{28,12},{1,17},{... | collective-permute-start | bytes 3145736 | tf_op jit(solution)/shard_map/ppermute | solution.py:321
  547.1 144.9 %collective-permute-start.39 = (bf16[256,2048]{1,0:T(8,128)(2,1)}, bf16[256,2048]{1,0:T(8,128)(2,1)}, u32[]{:S(2)}, u32[]{:S(2)}) collective-permute-start(bf16[256,2048]{1,0:T(8,128)(2,1)} %get-tuple-element.79), channel_id=1, source_target_pairs={{0,8},{4,12},{8,0},{12,4},{16,24},{20,28},{24,16},{28,20},{1,9},{5... | collective-permute-start | bytes 3145736 | tf_op jit(solution)/shard_map/ppermute | solution.py:321
  550.6 141.8 %collective-permute-start.41 = (bf16[256,2048]{1,0:T(8,128)(2,1)}, bf16[256,2048]{1,0:T(8,128)(2,1)}, u32[]{:S(2)}, u32[]{:S(2)}) collective-permute-start(bf16[256,2048]{1,0:T(8,128)(2,1)} %get-tuple-element.80), channel_id=1, source_target_pairs={{0,24},{4,28},{8,16},{12,20},{16,8},{20,12},{24,0},{28,4},{1,25},{... | collective-permute-start | bytes 3145736 | tf_op jit(solution)/shard_map/ppermute | solution.py:321
  567.0 170.7 %collective-permute-start.40 = (bf16[256,2048]{1,0:T(8,128)(2,1)}, bf16[256,2048]{1,0:T(8,128)(2,1)}, u32[]{:S(2)}, u32[]{:S(2)}) collective-permute-start(bf16[256,2048]{1,0:T(8,128)(2,1)} %get-tuple-element.81), channel_id=1, source_target_pairs={{0,16},{4,20},{8,24},{12,28},{16,0},{20,4},{24,8},{28,12},{1,17},{... | collective-permute-start | bytes 3145736 | tf_op jit(solution)/shard_map/ppermute | solution.py:321
  618.2 147.5 %all-to-all-start.3 = ((bf16[8,32,2048]{2,1,0:T(8,128)(2,1)}), bf16[8,32,2048]{2,1,0:T(8,128)(2,1)}, u32[]{:S(2)}, u32[]{:S(2)}) async-start(bf16[8,32,2048]{2,1,0:T(8,128)(2,1)} %bitcast.118), calls=%async_computation.3 | async-start | bytes 2097152 | tf_op jit(solution)/shard_map/all_to_all | solution.py:334
  687.1 57.7 %collective-permute-start.16 = (bf16[256,2048]{1,0:T(8,128)(2,1)}, bf16[256,2048]{1,0:T(8,128)(2,1)}, u32[]{:S(2)}, u32[]{:S(2)}) collective-permute-start(bf16[256,2048]{1,0:T(8,128)(2,1)} %bitcast.8), channel_id=1, source_target_pairs={{0,2},{1,3},{2,0},{3,1},{4,6},{5,7},{6,4},{7,5},{8,10},{9,11},{10,... | collective-permute-start | bytes 3145736 | tf_op jit(solution)/shard_map/ppermute | solution.py:321
  691.9 53.5 %collective-permute-start.35 = (bf16[256,512]{1,0:T(8,128)(2,1)S(1)}, bf16[256,512]{1,0:T(8,128)(2,1)S(1)}, u32[]{:S(2)}, u32[]{:S(2)}) collective-permute-start(bf16[256,512]{1,0:T(8,128)(2,1)S(1)} %get-tuple-element.86), channel_id=1, source_target_pairs={{0,8},{4,12},{8,0},{12,4},{16,24},{20,28},{24,16},{28,20},{1,9},{5... | collective-permute-start | bytes 786440 | tf_op jit(solution)/shard_map/ppermute | solution.py:321
  692.4 53.1 %collective-permute-start.37 = (bf16[256,512]{1,0:T(8,128)(2,1)S(1)}, bf16[256,512]{1,0:T(8,128)(2,1)S(1)}, u32[]{:S(2)}, u32[]{:S(2)}) collective-permute-start(bf16[256,512]{1,0:T(8,128)(2,1)S(1)} %get-tuple-element.87), channel_id=1, source_target_pairs={{0,24},{4,28},{8,16},{12,20},{16,8},{20,12},{24,0},{28,4},{1,25},{... | collective-permute-start | bytes 786440 | tf_op jit(solution)/shard_map/ppermute | solution.py:321
  744.8 43.0 %collective-permute-start.15 = (bf16[256,2048]{1,0:T(8,128)(2,1)}, bf16[256,2048]{1,0:T(8,128)(2,1)}, u32[]{:S(2)}, u32[]{:S(2)}) collective-permute-start(bf16[256,2048]{1,0:T(8,128)(2,1)} %bitcast.8), channel_id=1, source_target_pairs={{0,1},{1,0},{2,3},{3,2},{4,5},{5,4},{6,7},{7,6},{8,9},{9,8},{10,11... | collective-permute-start | bytes 3145736 | tf_op jit(solution)/shard_map/ppermute | solution.py:321
  745.4 42.5 %collective-permute-start.17 = (bf16[256,2048]{1,0:T(8,128)(2,1)}, bf16[256,2048]{1,0:T(8,128)(2,1)}, u32[]{:S(2)}, u32[]{:S(2)}) collective-permute-start(bf16[256,2048]{1,0:T(8,128)(2,1)} %collective-permute-done.16), channel_id=1, source_target_pairs={{0,1},{1,0},{2,3},{3,2},{4,5},{5,4},{6,7},{7,6},{8,9},{9,8},{10,11... | collective-permute-start | bytes 3145736 | tf_op jit(solution)/shard_map/ppermute | solution.py:321
  766.9 30.8 %all-to-all-start.4 = ((f32[8,4,256]{2,1,0:T(4,128)}), f32[8,4,256]{2,1,0:T(4,128)S(1)}, u32[]{:S(2)}, u32[]{:S(2)}) async-start(f32[8,4,256]{2,1,0:T(4,128)} %bitcast.38), calls=%async_computation.4 | async-start | bytes 65536 | tf_op jit(solution)/shard_map/all_to_all | solution.py:334
  785.5 38.1 %collective-permute-start.33 = (bf16[256,1536]{1,0:T(8,128)(2,1)}, bf16[256,1536]{1,0:T(8,128)(2,1)}, u32[]{:S(2)}, u32[]{:S(2)}) collective-permute-start(bf16[256,1536]{1,0:T(8,128)(2,1)} %get-tuple-element.83), channel_id=1, source_target_pairs={{0,24},{4,28},{8,16},{12,20},{16,8},{20,12},{24,0},{28,4},{1,25},{... | collective-permute-start | bytes 2359304 | tf_op jit(solution)/shard_map/ppermute | solution.py:321
  787.8 65.6 %collective-permute-start.32 = (bf16[256,1536]{1,0:T(8,128)(2,1)}, bf16[256,1536]{1,0:T(8,128)(2,1)}, u32[]{:S(2)}, u32[]{:S(2)}) collective-permute-start(bf16[256,1536]{1,0:T(8,128)(2,1)} %get-tuple-element.84), channel_id=1, source_target_pairs={{0,16},{4,20},{8,24},{12,28},{16,0},{20,4},{24,8},{28,12},{1,17},{... | collective-permute-start | bytes 2359304 | tf_op jit(solution)/shard_map/ppermute | solution.py:321
  787.8 72.2 %collective-permute-start.27 = (bf16[256,2048]{1,0:T(8,128)(2,1)}, bf16[256,2048]{1,0:T(8,128)(2,1)}, u32[]{:S(2)}, u32[]{:S(2)}) collective-permute-start(bf16[256,2048]{1,0:T(8,128)(2,1)} %bitcast.10), channel_id=1, source_target_pairs={{0,1},{1,0},{2,3},{3,2},{4,5},{5,4},{6,7},{7,6},{8,9},{9,8},{10,11... | collective-permute-start | bytes 3145736 | tf_op jit(solution)/shard_map/ppermute | solution.py:321
  790.1 70.0 %collective-permute-start.29 = (bf16[256,2048]{1,0:T(8,128)(2,1)}, bf16[256,2048]{1,0:T(8,128)(2,1)}, u32[]{:S(2)}, u32[]{:S(2)}) collective-permute-start(bf16[256,2048]{1,0:T(8,128)(2,1)} %collective-permute-done.28), channel_id=1, source_target_pairs={{0,1},{1,0},{2,3},{3,2},{4,5},{5,4},{6,7},{7,6},{8,9},{9,8},{10,11... | collective-permute-start | bytes 3145736 | tf_op jit(solution)/shard_map/ppermute | solution.py:321
  (77 other events, 1222.2 us)

commit v2 on v1

v2 whole, which is shorter than its diff:
```python
from functools import partial
import math

import jax
import jax.numpy as jnp
from jax import lax
from jax.experimental import pallas as pl
from jax.experimental.pallas import tpu as pltpu
from jax.sharding import PartitionSpec as P

HEAD_DIM = 128
F32 = jnp.float32
BF16 = jnp.bfloat16
MIB = 1 << 20
NN = ((1,), (0,))
NT = ((1,), (1,))
TN = ((0,), (0,))


def dot(a, b, contract=NN):
    return lax.dot_general(a, b, (contract, ((), ())), preferred_element_type=F32)


def call(body, grid, ins, outs, scratch=(), flops=0, special=0, after=(), prefetch=None):
    arrays = [array for array, _, _ in ins]
    specs = [pl.BlockSpec(block, index) for _, block, index in ins] + [pl.BlockSpec(memory_space=pl.ANY)] * len(after)
    shapes = [jax.ShapeDtypeStruct(shape, kind) for shape, kind, _, _ in outs]
    n_in, n_pre = len(ins), 0 if prefetch is None else 1

    def wrapped(*refs):
        body(*refs[: n_pre + n_in], *refs[n_pre + n_in + len(after) :])

    moved = sum(a.size * a.dtype.itemsize for a in arrays) + sum(s.size * s.dtype.itemsize for s in shapes)
    out_specs = [pl.BlockSpec(block, index) for _, _, block, index in outs]
    keys = dict(
        out_shape=shapes,
        compiler_params=pltpu.CompilerParams(vmem_limit_bytes=55 * MIB),
        cost_estimate=pl.CostEstimate(flops=0, bytes_accessed=0, transcendentals=0),
    )
    if prefetch is None:
        made = pl.pallas_call(
            wrapped, grid=grid, in_specs=specs, out_specs=out_specs, scratch_shapes=list(scratch), **keys
        )
        return made(*arrays, *after)
    spec = pltpu.PrefetchScalarGridSpec(
        num_scalar_prefetch=1, grid=grid, in_specs=specs, out_specs=out_specs, scratch_shapes=list(scratch)
    )
    return pl.pallas_call(wrapped, grid_spec=spec, **keys)(prefetch, *arrays, *after)


def gate(x, *after):
    def body(*refs):
        pass

    anywhere = pl.BlockSpec(memory_space=pl.ANY)
    return pl.pallas_call(
        body,
        in_specs=[anywhere] * (1 + len(after)),
        out_specs=anywhere,
        out_shape=jax.ShapeDtypeStruct(x.shape, x.dtype),
        input_output_aliases={0: 0},
        cost_estimate=pl.CostEstimate(flops=0, bytes_accessed=0, transcendentals=0),
    )(x, *after)


def block_matmul(picks, b, transposed=False, tile=512, received=None, after=()):
    rows, depth = picks[0][0].shape[0] // picks[0][2], picks[0][0].shape[1]
    width = b.shape[0] if transposed else b.shape[1]

    def body(x_ref, y_ref, b_ref, *rest):
        o_ref, p_ref, both = rest[-3:]

        @pl.when(pl.program_id(0) == 0)
        def _():
            both[:rows] = x_ref[...]
            both[rows:] = y_ref[...]

        result = dot(both[...], b_ref[...], NT if transposed else NN)
        o_ref[...] = result[:rows].astype(BF16)
        second = result[rows:]
        if received is not None:
            second += rest[0][...].astype(F32)
        p_ref[...] = second.astype(BF16)

    side = ((tile, depth), lambda j: (j, 0)) if transposed else ((depth, tile), lambda j: (0, j))
    more = [] if received is None else [(received, (rows, tile), lambda j: (0, j))]
    return call(
        body,
        (width // tile,),
        [(x, (rows, depth), lambda j, n=n: (n, 0)) for x, n, _ in picks] + [(b, *side)] + more,
        [((rows, width), BF16, (rows, tile), lambda j: (0, j))] * 2,
        [pltpu.VMEM((2 * rows, depth), BF16)],
        flops=4 * rows * width * depth,
        after=after,
    )


def project(pair, w3, after=()):
    rows, depth = pair[0].shape
    width = w3.shape[2]

    def body(x_ref, y_ref, w_ref, o_ref, both):
        @pl.when(pl.program_id(0) == 0)
        def _():
            both[:rows] = x_ref[...]
            both[rows:] = y_ref[...]

        o_ref[0] = dot(both[...], w_ref[0]).astype(BF16)

    return call(
        body,
        (3,),
        [(x, (rows, depth), lambda s: (0, 0)) for x in pair]
        + [(w3, (1, depth, width), lambda s: (s, 0, 0))],
        [((3, 2 * rows, width), BF16, (1, 2 * rows, width), lambda s: (s, 0, 0))],
        [pltpu.VMEM((2 * rows, depth), BF16)],
        flops=12 * rows * width * depth,
        after=after,
    )[0]


def project_back(g3, w3, picks, tile=512, received=None, after=()):
    width, depth, rows = g3.shape[2], w3.shape[1], g3.shape[1] // 4

    def body(x_ref, y_ref, w_ref, *rest):
        o_ref, p_ref, both = rest[-3:]

        @pl.when(pl.program_id(0) == 0)
        def _():
            both[:, :rows] = x_ref[...]
            both[:, rows:] = y_ref[...]

        total = dot(both[0], w_ref[0], NT)
        total += dot(both[1], w_ref[1], NT)
        total += dot(both[2], w_ref[2], NT)
        o_ref[...] = total[:rows].astype(BF16)
        second = total[rows:]
        if received is not None:
            second += rest[0][...].astype(F32)
        p_ref[...] = second.astype(BF16)

    more = [] if received is None else [(received, (rows, tile), lambda j: (0, j))]
    return call(
        body,
        (depth // tile,),
        [(g3, (3, rows, width), lambda j, n=n: (0, n, 0)) for n in picks]
        + [(w3, (3, tile, width), lambda j: (0, j, 0))]
        + more,
        [((rows, depth), BF16, (rows, tile), lambda j: (0, j))] * 2,
        [pltpu.VMEM((3, 2 * rows, width), BF16)],
        flops=12 * rows * width * depth,
        after=after,
    )


def mlp(normed, cot, w_up, w_down, tile=512, after=()):
    rows, depth = normed[0].shape
    width = w_up.shape[1]

    def body(n0, n1, c0, c1, u_ref, d_ref, act_ref, bar_ref, n_both, c_both):
        @pl.when(pl.program_id(0) == 0)
        def _():
            n_both[:rows] = n0[...]
            n_both[rows:] = n1[...]
            c_both[:rows] = c0[...]
            c_both[rows:] = c1[...]

        up = dot(n_both[...], u_ref[...])
        grad = dot(c_both[...], d_ref[...], NT)
        bell = jnp.exp(up * up * -0.5)
        t = 1.0 / (1.0 + (0.3275911 / math.sqrt(2.0)) * jnp.abs(up))
        poly = t * (
            0.127414796 + t * (-0.142248368 + t * (0.7107068705 + t * (-0.7265760135 + t * 0.5307027145)))
        )
        tail = poly * bell
        phi = jnp.where(up < 0.0, tail, 1.0 - tail)
        act_ref[...] = (up * phi).astype(BF16)
        slope = phi + up * bell * (1.0 / math.sqrt(2.0 * math.pi))
        bar_ref[...] = (slope * grad).astype(BF16)

    return call(
        body,
        (width // tile,),
        [(x, (rows, depth), lambda j: (0, 0)) for x in (*normed, *cot)]
        + [(w_up, (depth, tile), lambda j: (0, j)), (w_down, (tile, depth), lambda j: (j, 0))],
        [((2 * rows, width), BF16, (2 * rows, tile), lambda j: (0, j))] * 2,
        [pltpu.VMEM((2 * rows, depth), BF16)] * 2,
        flops=8 * rows * width * depth,
        special=4 * rows * width,
        after=after,
    )


def attend(picks, qkv, pos_col, start_col, pos_row, after=()):
    _, half, width = qkv[0].shape
    rows = half // 2
    heads = width // HEAD_DIM
    factor = 1.0 / math.sqrt(HEAD_DIM)

    def body(x_ref, y_ref, low_ref, high_ref, px_ref, py_ref, sx_ref, sy_ref, pr_ref, o_ref, kv, both):
        i = pl.program_id(0)

        @pl.when(i == 0)
        def _():
            kv[:, :half] = low_ref[1:]
            kv[:, half:] = high_ref[1:]
            both[0] = x_ref[0]
            both[1] = y_ref[0]

        keys = pr_ref[...]
        at = jnp.where(i == 0, px_ref[...], py_ref[...])
        since = jnp.where(i == 0, sx_ref[...], sy_ref[...])
        bias = jnp.where((keys <= at) & (keys >= since), 0.0, -1e30)
        for head in range(heads):
            cols = slice(head * HEAD_DIM, (head + 1) * HEAD_DIM)
            scores = dot(both[i, :, cols], kv[0, :, cols], NT) * factor + bias
            peak = jnp.max(scores, axis=-1, keepdims=True)
            grown = jnp.exp(scores - peak)
            total = jnp.sum(grown, axis=-1, keepdims=True)
            o_ref[:, cols] = (dot(grown.astype(BF16), kv[1, :, cols]) * (1.0 / total)).astype(BF16)

    return call(
        body,
        (2,),
        [(qkv[n // 2], (1, rows, width), lambda i, n=n: (0, n % 2, 0)) for n in picks]
        + [
            (qkv[0], (3, half, width), lambda i: (0, 0, 0)),
            (qkv[1], (3, half, width), lambda i: (0, 0, 0)),
        ]
        + [(c, (rows, 1), lambda i, n=n: (n, 0)) for c in (pos_col, start_col) for n in picks]
        + [(pos_row, (1, 2 * half), lambda i: (0, 0))],
        [((half, width), BF16, (rows, width), lambda i: (i, 0))],
        [pltpu.VMEM((2, 2 * half, width), BF16), pltpu.VMEM((2, rows, width), BF16)],
        flops=8 * half * half * width,
        special=2 * heads * half * half,
        after=after,
    )[0]


def attend_back(qkv, bars, pos_col, pos_row, start_row, after=()):
    _, half, width = qkv[0].shape
    rows = 2 * half
    tile = rows // 4
    heads = width // HEAD_DIM
    factor = 1.0 / math.sqrt(HEAD_DIM)

    def body(low_ref, high_ref, g0, g1, g2, g3, pc_ref, pr_ref, sr_ref, o_ref, all_qkv, dk, dv, g_tile):
        step = pl.program_id(0)
        keys = pc_ref[...]
        seen = (keys <= pr_ref[...]) & (keys >= sr_ref[...])
        bias = jnp.where(seen, 0.0, -1e30)

        @pl.when(step == 0)
        def _():
            dk[...] = jnp.zeros_like(dk)
            dv[...] = jnp.zeros_like(dv)
            all_qkv[:, :half] = low_ref[...]
            all_qkv[:, half:] = high_ref[...]

        for number, g_ref in enumerate((g0, g1, g2, g3)):

            @pl.when(step == number)
            def _():
                g_tile[...] = g_ref[...]

        here = pl.ds(pl.multiple_of(step * tile, tile), tile)
        for head in range(heads):
            cols = slice(head * HEAD_DIM, (head + 1) * HEAD_DIM)
            q, k, v, g = all_qkv[0, here, cols], all_qkv[1, :, cols], all_qkv[2, :, cols], g_tile[:, cols]
            scores = dot(k, q, NT) * factor + bias
            peak = jnp.max(scores, axis=0, keepdims=True)
            grown = jnp.exp(scores - peak)
            probs = grown * (1.0 / jnp.sum(grown, axis=0, keepdims=True))
            dv[:, cols] += dot(probs.astype(BF16), g)
            probs_bar = dot(v, g, NT)
            inner = jnp.sum(probs * probs_bar, axis=0, keepdims=True)
            scores_bar = (probs * (probs_bar - inner)).astype(BF16)
            dk[:, cols] += dot(scores_bar, q)
            dq = dot(scores_bar, k, TN) * factor
            o_ref[0, here, cols] = dq.astype(BF16)

        @pl.when(step == pl.num_programs(0) - 1)
        def _():
            o_ref[1] = (dk[...] * factor).astype(BF16)
            o_ref[2] = dv[...].astype(BF16)

    return call(
        body,
        (4,),
        [
            (qkv[0], (3, half, width), lambda i: (0, 0, 0)),
            (qkv[1], (3, half, width), lambda i: (0, 0, 0)),
            *[(bar, (tile, width), lambda i: (0, 0)) for bar in bars],
            (pos_col, (rows, 1), lambda i: (0, 0)),
            (pos_row, (1, tile), lambda i: (0, i)),
            (start_row, (1, tile), lambda i: (0, i)),
        ],
        [((3, rows, width), BF16, (3, rows, width), lambda i: (0, 0, 0))],
        [
            pltpu.VMEM((3, rows, width), BF16),
            pltpu.VMEM((rows, width), F32),
            pltpu.VMEM((rows, width), F32),
            pltpu.VMEM((tile, width), BF16),
        ],
        flops=10 * rows * rows * width,
        special=heads * rows * rows,
        after=after,
    )[0]


def weight_grad(ids, lefts, rights, piece, block, received=None, after=()):
    count = ids.shape[0]
    rights = [r[None] if r.ndim == 2 else r for r in rights]
    part, column, pieces = piece
    width = rights[0].shape[2] // pieces
    halves = count // 2

    def body(ids_ref, *refs):
        left_refs, right_refs = refs[: len(lefts)], refs[len(lefts) : len(lefts) + len(rights)]
        rest = refs[len(lefts) + len(rights) :]
        left = jnp.concatenate([l[...] for l in left_refs], axis=0) if len(lefts) > 1 else left_refs[0][...]
        total, at = None, 0
        for r in right_refs:
            term = dot(left[at : at + r.shape[1]], r[0], TN)
            at += r.shape[1]
            total = term if total is None else total + term
        if received is None:
            rest[0][0] = total.astype(BF16)
            return
        total = (total + rest[0][0].astype(F32)).astype(BF16)
        i = pl.program_id(0)

        @pl.when(i < halves)
        def _():
            rest[1][0] = total

        @pl.when(i >= halves)
        def _():
            rest[2][0] = total

    ins = [(l, (l.shape[0], block), lambda i, ids: (0, ids[i])) for l in lefts]
    ins += [(r, (1, r.shape[1], width), lambda i, ids: (part, 0, column)) for r in rights]
    shape = (1, block, width)
    if received is None:
        outs = [((count, block, width), BF16, shape, lambda i, ids: (i, 0, 0))]
    else:
        ins.append((received, shape, lambda i, ids: (i, 0, 0)))
        outs = [
            ((halves, block, width), BF16, shape, lambda i, ids: (jnp.minimum(i, halves - 1), 0, 0)),
            ((halves, block, width), BF16, shape, lambda i, ids: (jnp.maximum(i - halves, 0), 0, 0)),
        ]
    rows = sum(l.shape[0] for l in lefts)
    result = call(body, (count,), ins, outs, flops=2 * rows * count * block * width, after=after, prefetch=ids)
    return result[0] if received is None else result


def add_halves(kept, received, after=()):
    count, block, width = kept.shape
    shape = (1, block, width)
    halves = count // 2

    def body(k_ref, r_ref, a_ref, b_ref):
        total = (k_ref[...].astype(F32) + r_ref[...].astype(F32)).astype(BF16)
        i = pl.program_id(0)

        @pl.when(i < halves)
        def _():
            a_ref[...] = total

        @pl.when(i >= halves)
        def _():
            b_ref[...] = total

    return call(
        body,
        (count,),
        [(x, shape, lambda i: (i, 0, 0)) for x in (kept, received)],
        [
            ((halves, block, width), BF16, shape, lambda i: (jnp.minimum(i, halves - 1), 0, 0)),
            ((halves, block, width), BF16, shape, lambda i: (jnp.maximum(i - halves, 0), 0, 0)),
        ],
        flops=kept.size,
        after=after,
    )


def add_last(terms, turn, parts=False, after=()):
    _, block, width = terms[0][0].shape
    count = len(terms)

    def body(*refs):
        for n in range(count):
            total = refs[2 * n][0].astype(F32) + refs[2 * n + 1][0].astype(F32)
            if parts:
                refs[-1][n] = total
            elif turn:
                refs[-1][n * width : (n + 1) * width] = total.T
            else:
                refs[-1][:, n * width : (n + 1) * width] = total

    shape = (count, block, width) if parts else (count * width, block) if turn else (block, count * width)
    return call(
        body,
        (1,),
        [(x, (1, block, width), lambda i: (0, 0, 0)) for pair in terms for x in pair],
        [(shape, F32, shape, lambda i: (0,) * len(shape))],
        flops=2 * block * width,
        after=after,
    )[0]


def unit_of(values):
    centre = values - jnp.mean(values, axis=-1, keepdims=True)
    scaling = lax.rsqrt(jnp.mean(centre * centre, axis=-1, keepdims=True) + 1e-05)
    return centre * scaling, scaling


def rowwise(body, rows_in, whole_in, outs, sums=0, tile=128, after=()):
    rows, depth = rows_in[0].shape
    return call(
        body,
        (rows // tile,),
        [(x, (tile, depth), lambda i: (i, 0)) for x in rows_in]
        + [(x, (1, depth), lambda i: (0, 0)) for x in whole_in],
        [((rows, depth), kind, (tile, depth), lambda i: (i, 0)) for kind in outs]
        + [((1, depth), F32, (1, depth), lambda i: (0, 0))] * sums,
        flops=20 * rows * depth,
        after=after,
    )


def norm_forward(values, gain, shift, after=()):
    def body(v_ref, g_ref, s_ref, o_ref):
        unit, _ = unit_of(v_ref[...].astype(F32))
        o_ref[...] = (unit * g_ref[...] + s_ref[...]).astype(BF16)

    return rowwise(body, [values], [gain, shift], [BF16], after=after)[0]


def sum_norm(base, terms, gain, shift, after=()):
    def body(b_ref, x_ref, y_ref, z_ref, g_ref, s_ref, h_ref, o_ref):
        total = x_ref[...].astype(F32) + y_ref[...].astype(F32) + z_ref[...].astype(F32)
        total = b_ref[...].astype(F32) + total
        h_ref[...] = total
        unit, _ = unit_of(total)
        o_ref[...] = (unit * g_ref[...] + s_ref[...]).astype(BF16)

    return rowwise(body, [base, *terms], [gain, shift], [F32, BF16], after=after)


def sum_low(base, terms, after=()):
    def body(b_ref, x_ref, y_ref, z_ref, o_ref):
        total = x_ref[...].astype(F32) + y_ref[...].astype(F32) + z_ref[...].astype(F32)
        o_ref[...] = (b_ref[...].astype(F32) + total).astype(BF16)

    return rowwise(body, [base, *terms], [], [BF16], after=after)[0]


def norm_back(base, values, terms, gain, keep, after=()):
    def body(b_ref, v_ref, x_ref, y_ref, z_ref, g_ref, o_ref, *rest):
        @pl.when(pl.program_id(0) == 0)
        def _():
            rest[-2][...] = jnp.zeros_like(rest[-2])
            rest[-1][...] = jnp.zeros_like(rest[-1])

        upstream = x_ref[...].astype(F32) + y_ref[...].astype(F32) + z_ref[...].astype(F32)
        unit, scaling = unit_of(v_ref[...].astype(F32))
        rest[-2][...] += jnp.sum(upstream * unit, axis=0, keepdims=True)
        rest[-1][...] += jnp.sum(upstream, axis=0, keepdims=True)
        scaled = upstream * g_ref[...]
        inner = (
            scaled
            - jnp.mean(scaled, axis=-1, keepdims=True)
            - unit * jnp.mean(scaled * unit, axis=-1, keepdims=True)
        )
        total = b_ref[...].astype(F32) + scaling * inner
        o_ref[...] = total.astype(BF16)
        if keep:
            rest[0][...] = total

    return rowwise(
        body, [base, values, *terms], [gain], [BF16, F32] if keep else [BF16], sums=2, after=after
    )


def place(index, pair, rows, so_far=None, after=()):
    block, depth = pair[0].shape
    tile = rows // 4

    def body(i_ref, x_ref, y_ref, *rest):
        where = lax.broadcasted_iota(jnp.int32, (tile, block), 0) + pl.program_id(0) * tile
        total = dot((where == i_ref[:, :block]).astype(BF16), x_ref[...])
        total += dot((where == i_ref[:, block:]).astype(BF16), y_ref[...])
        if so_far is not None:
            total += rest[0][...].astype(F32)
        rest[-1][...] = total.astype(BF16)

    more = [] if so_far is None else [(so_far, (tile, depth), lambda i: (i, 0))]
    return call(
        body,
        (rows // tile,),
        [
            (index, (1, 2 * block), lambda i: (0, 0)),
            (pair[0], (block, depth), lambda i: (0, 0)),
            (pair[1], (block, depth), lambda i: (0, 0)),
            *more,
        ],
        [((rows, depth), BF16, (tile, depth), lambda i: (i, 0))],
        flops=4 * rows * block * depth,
        after=after,
    )[0]


def local(
    n_seq,
    n_head,
    tokens,
    codebook,
    codes,
    modality,
    segments,
    sequence_source,
    w_qkv,
    w_out,
    w_up,
    w_down,
    norm1_gain,
    norm1_shift,
    norm2_gain,
    norm2_shift,
    cotangent,
):
    rows, depth = tokens.shape
    me, own = lax.axis_index("seq"), lax.axis_index("head")
    share = rows // n_seq // n_head
    quarter = rows // n_head
    w3 = jnp.transpose(w_qkv, (1, 0, 2))
    gain1, shift1, gain2, shift2 = [v[None] for v in (norm1_gain, norm1_shift, norm2_gain, norm2_shift)]

    def swap(x, flip, axis="head"):
        size = n_head if axis == "head" else n_seq
        return lax.ppermute(x, axis, [(i, i ^ flip) for i in range(size)])

    def exchange(x):
        return lax.all_to_all(x, "seq", split_axis=0, concat_axis=0, tiled=True)

    source = sequence_source.reshape(n_seq, rows)
    places = jnp.arange(rows, dtype=jnp.int32)
    groups = source // rows
    offsets = source % rows
    leaving = groups == me
    coming = lax.dynamic_index_in_dim(groups, me, 0) == jnp.arange(n_seq, dtype=jnp.int32)[:, None]
    upper = (places[:, None] <= places[None, :]).astype(BF16)
    counts = jnp.dot(
        jnp.concatenate([leaving, coming], axis=0).astype(BF16), upper, preferred_element_type=F32
    ).astype(jnp.int32)
    leaving_rank = jnp.where(leaving, counts[:n_seq] - 1, -1)
    coming_rank = jnp.where(coming, counts[n_seq:] - 1, -1)
    lanes = jnp.arange(share, dtype=jnp.int32)

    def listed(rank, value, blocks):
        wanted = (own ^ jnp.asarray(blocks, jnp.int32))[:, None] * share + lanes[None, :]
        hit = rank[None, :, None, :] == wanted[:, None, :, None]
        return jnp.sum(jnp.where(hit, value[None, :, None, :], 0), axis=-1).reshape(-1)

    sent = listed(leaving_rank, offsets, [0])
    pick = (sent[:, None] == places[None, :]).astype(BF16)
    code = jnp.where(modality == 1, codes, -1)
    sent_code = jnp.sum(jnp.where(sent[:, None] == places[None, :], code[None, :], 0), axis=-1)
    pick_code = (
        sent_code[:, None] == jnp.arange(codebook.shape[0], dtype=jnp.int32)[None, :]
    ).astype(BF16)
    leaving_embedded = (
        jnp.dot(pick, tokens, preferred_element_type=F32)
        + jnp.dot(pick_code, codebook, preferred_element_type=F32)
    ).astype(BF16)
    embedded = exchange(leaving_embedded)

    sent_across = listed(leaving_rank, offsets, [2])
    pick_across = (sent_across[:, None] == places[None, :]).astype(BF16)
    leaving_cot = jnp.concatenate(
        [
            jnp.dot(p, cotangent, preferred_element_type=F32).astype(BF16).reshape(n_seq, share, depth)
            for p in (pick, pick_across)
        ],
        axis=1,
    )
    came = exchange(leaving_cot)
    cot0, cot2 = [came[:, i * share : (i + 1) * share].reshape(quarter, depth) for i in range(2)]
    cot1, cot3 = swap(cot0, 1), swap(cot2, 1)

    sent_all = listed(leaving_rank, offsets, list(range(n_head)))
    segment_row = segments[0]
    begin = jnp.sum((segment_row[:, None] < segment_row[None, :]).astype(jnp.int32), axis=0)
    packed = listed(
        coming_rank, jnp.broadcast_to(begin * rows + places, (n_seq, rows)), list(range(n_head))
    )
    position, start = packed % rows, packed // rows
    pos_col, start_col, pos_row, start_row = position[:, None], start[:, None], position[None], start[None]

    n0 = norm_forward(embedded, gain1, shift1)
    n2 = swap(n0, 2)
    n1 = swap(n0, 1)
    qkv_low = project((n0, n1), w3)
    n2 = gate(n2, qkv_low)
    n3 = swap(n2, 1)
    qkv = (qkv_low, project((n2, n3), w3))
    mixed_out = attend((1, 3), qkv, pos_col, start_col, pos_row)
    a1, a3 = block_matmul(((mixed_out, 0, 2), (mixed_out, 1, 2)), w_out)
    mixed_in = attend((0, 2), qkv, pos_col, start_col, pos_row, after=(a1,))
    a0, passed = block_matmul(((mixed_in, 0, 2), (mixed_in, 1, 2)), w_out, received=swap(a3, 1))
    hidden_in, m0 = sum_norm(embedded, (a0, swap(a1, 1), swap(passed, 2)), gain2, shift2)

    m2 = swap(m0, 2)
    m1 = swap(m0, 1)
    act_low, bar_low = mlp((m0, m1), (cot0, cot1), w_up, w_down)
    m2 = gate(m2, act_low)
    m3 = swap(m2, 1)
    act_high, bar_high = mlp((m2, m3), (cot2, cot3), w_up, w_down)
    bars_out, bars_in = ((bar_low, 1, 2), (bar_high, 1, 2)), ((bar_low, 0, 2), (bar_high, 0, 2))
    acts_out, acts_in = ((act_low, 1, 2), (act_high, 1, 2)), ((act_low, 0, 2), (act_high, 0, 2))

    bits = n_seq.bit_length() - 1
    block = depth // n_seq

    def keep_order(order):
        kept = [0]
        for bit in reversed(order[1:]):
            kept = [k | 1 << bit for k in kept] + kept
        return jnp.asarray(kept, jnp.int32)

    def columns(blocks, ids):
        if block % 128 == 0:
            return blocks, ids, block
        picked = [jnp.take(b.reshape(-1, n_seq, block), ids, axis=1).reshape(b.shape[0], -1) for b in blocks]
        return picked, jnp.arange(n_seq // 2 * block // 128, dtype=jnp.int32), 128

    def first_term(grad, after=()):
        order, lefts, rights, piece = grad
        ids = me ^ (1 << order[0]) ^ keep_order(order)
        blocks, ids, size = columns(lefts, ids)
        made = weight_grad(ids, blocks, rights, piece, size, after=after)
        return swap(made, 1 << order[0], "seq"), made

    def second_term(grad, received, after=()):
        order, lefts, rights, piece = grad
        blocks, ids, size = columns(lefts, me ^ keep_order(order))
        send, keep = weight_grad(ids, blocks, rights, piece, size, received, after=after)
        send, keep = [x.reshape(n_seq // 4, block, x.shape[2]) for x in (send, keep)]
        return swap(send, 1 << order[1], "seq"), keep

    def next_terms(grad, received, keep, after=()):
        for bit in grad[0][2:]:
            send, keep = add_halves(keep, received, after=after)
            received = swap(send, 1 << bit, "seq")
        return received, keep

    straight = list(range(bits))
    turned = [1, 0] + straight[2:]
    cots = (cot0, cot1, cot2, cot3)
    normed_one, normed_two = (n0, n1, n2, n3), (m0, m1, m2, m3)

    acts, bars = (act_low, act_high), (bar_low, bar_high)
    down, up = (straight, cots, acts, (0, 0, 1)), (turned, normed_two, bars, (0, 0, 1))

    down_got, made = first_term(down)
    up_got, made = first_term(up, after=(made,))
    t1, t3 = block_matmul(bars_out, w_up, transposed=True, after=(made,))
    b1, b3 = block_matmul(acts_out, w_down, after=(t1,))
    t0, passed = block_matmul(bars_in, w_up, transposed=True, received=swap(t3, 1), after=(b1,))
    h0, hidden_bar, gain_two, shift_two = norm_back(
        cot0, hidden_in, (t0, swap(t1, 1), swap(passed, 2)), gain2, True
    )
    h2 = swap(h0, 2)
    h1 = swap(h0, 1)

    g0, g1 = block_matmul(((h0, 0, 1), (h1, 0, 1)), w_out, transposed=True)
    b0, branch_passed = block_matmul(acts_in, w_down, received=swap(b3, 1), after=(g0,))
    h2 = gate(h2, branch_passed)
    h3 = swap(h2, 1)
    down_got, down_keep = second_term(down, down_got, after=(h2,))
    g2, g3 = block_matmul(((h2, 0, 1), (h3, 0, 1)), w_out, transposed=True, after=(down_keep, up_got))
    out = (straight, (h1, h3, h0, h2), (mixed_out, mixed_in), (0, 0, 1))
    out_got, made = first_term(out, after=(g2,))
    up_got, up_keep = second_term(up, up_got, after=(made,))
    output_slice = sum_low(hidden_in, (b0, swap(b1, 1), swap(branch_passed, 2)), after=(up_keep,))
    output_home = exchange(output_slice)
    qkv_bar = attend_back(qkv, (g0, g1, g2, g3), pos_col, pos_row, start_row, after=(output_slice,))
    q_grad, k_grad, v_grad = [(straight, normed_one, (qkv_bar,), (n, 0, 1)) for n in range(3)]
    u1, u3 = project_back(qkv_bar, w3, (1, 3), after=(out_got, down_got))
    q_got, made = first_term(q_grad, after=(u1, output_home))
    u0, passed = project_back(qkv_bar, w3, (0, 2), received=swap(u3, 1), after=(made,))
    k_got, made = first_term(k_grad, after=(passed, up_got))
    v_got, made = first_term(v_grad, after=(made,))
    out_got, out_keep = second_term(out, out_got, after=(made,))
    down_got, down_keep = next_terms(down, down_got, down_keep, after=(out_keep,))
    input_slice, gain_one, shift_one = norm_back(
        hidden_bar, embedded, (u0, swap(u1, 1), swap(passed, 2)), gain1, False, after=(down_keep, q_got)
    )
    input_home = exchange(input_slice)
    vectors = jnp.concatenate([gain_one, shift_one, gain_two, shift_two], axis=0)
    vectors = vectors + swap(vectors, 1)
    vectors = vectors + swap(vectors, 2)
    vectors = jnp.transpose(vectors.reshape(4, n_seq, block), (1, 0, 2))
    vectors = jnp.sum(exchange(vectors), axis=0)

    where = [sent_all[None, : 2 * quarter], sent_all[None, 2 * quarter :]]
    x0, x1, x2 = output_home, swap(output_home, 1), swap(output_home, 2)
    up_got, up_keep = next_terms(up, up_got, up_keep, after=(input_slice,))
    q_got, q_keep = second_term(q_grad, q_got, after=(up_keep,))
    first = place(where[0], (x0, x1), rows, after=(q_keep, down_got))
    out_got, out_keep = next_terms(out, out_got, out_keep, after=(first,))
    k_got, k_keep = second_term(k_grad, k_got, after=(out_keep,))
    q_got, q_keep = next_terms(q_grad, q_got, q_keep, after=(k_keep, v_got))
    x2 = gate(x2, q_keep)
    down_grad = add_last([(down_got, down_keep)], True, after=(x2,))
    block_output = place(where[1], (x2, swap(x2, 1)), rows, first, after=(down_grad,))
    y0, y1, y2 = input_home, swap(input_home, 1), swap(input_home, 2)
    v_got, v_keep = second_term(v_grad, v_got, after=(block_output, up_got))
    first = place(where[0], (y0, y1), rows, after=(v_keep,))
    k_got, k_keep = next_terms(k_grad, k_got, k_keep, after=(first,))
    y2 = gate(y2, k_keep, out_got, q_got)
    up_grad = add_last([(up_got, up_keep)], False, after=(y2,))
    input_grad = place(where[1], (y2, swap(y2, 1)), rows, first, after=(up_grad,))
    v_got, v_keep = next_terms(v_grad, v_got, v_keep, after=(input_grad,))
    out_grad = add_last([(out_got, out_keep)], True, after=(v_keep,))
    qkv_grad = add_last(
        [(q_got, q_keep), (k_got, k_keep), (v_got, v_keep)], False, True, after=(out_grad,)
    )
    qkv_grad = jnp.transpose(qkv_grad, (1, 0, 2))

    return (
        block_output,
        input_grad,
        qkv_grad,
        out_grad,
        up_grad,
        down_grad,
        vectors[0],
        vectors[1],
        vectors[2],
        vectors[3],
    )


def solution(mesh):
    return jax.shard_map(
        partial(local, mesh.shape["seq"], mesh.shape["head"]),
        mesh=mesh,
        in_specs=(
            P("seq", None),
            P(),
            P("seq"),
            P("seq"),
            P("seq", None),
            P(),
            P(None, None, "head"),
            P("head", None),
            P(None, "head"),
            P("head", None),
            P(),
            P(),
            P(),
            P(),
            P("seq", None),
        ),
        out_specs=(
            P("seq", None),
            P("seq", None),
            P("seq", None, "head"),
            P("head", "seq"),
            P("seq", "head"),
            P("head", "seq"),
            P("seq"),
            P("seq"),
            P("seq"),
            P("seq"),
        ),
        check_vma=False,
    )
```

time: 873 us -> 623 us (0.71)
  waiting for transfers between devices: 423 us -> 186 us
  Pallas kernels: 154 us -> 315 us
  other arithmetic: 64.2 us -> 10.1 us
  starting transfers between devices: 106 us -> 59.6 us
  local copies, waits for them, and re-layouts: 62.7 us -> 29.6 us
  blocking collectives: 33 us -> 0 us
  matrix products: 22.7 us -> 13.3 us
    ppermute x48 -> x49, waiting for transfers between devices: 406 us -> 167 us  [swap(): return lax.ppermute(x, axis, [(i, i ^ flip) for i in range(size)])]
    pallas_call x22 -> x53, Pallas kernels: 154 us -> 315 us  [the longest x36 226 us: call(): return made(*arrays, *after)]
    ppermute x48 -> x49, starting transfers between devices: 87.9 us -> 36.3 us  [swap(): return lax.ppermute(x, axis, [(i, i ^ flip) for i in range(size)])]
    all_to_all x1 -> x0, blocking collectives: 33 us -> none  [exchange(): return lax.all_to_all(x, 'seq', split_axis=0, concat_axis=0, tiled=True)]
    unnamed x117 -> x106, local copies, waits for them, and re-layouts: 44.9 us -> 24.3 us
    convert_element_type x8 -> x0, other arithmetic: 20.4 us -> none  [the longest x4 9.75 us: scatter_sum(): across = swap(passed.astype(BF16), 2)]
    concatenate x8 -> x2, other arithmetic: 16.5 us -> 3.16 us  [the longest x1 3.12 us: local(): jnp.concatenate([jnp.dot(p, cotangent, preferred_element_type=F32).astype...]
    dot_general x3 -> x2, matrix products: 17.3 us -> 6.91 us  [local(): jnp.dot(p, cotangent, preferred_element_type=F32).astype(BF16)]
  transfers between devices with their start and end apart: 52 -> 54, of which waited for: 19 -> 17; matrix products, arithmetic and copies ran while one was open for 9% -> 3% of each run, Pallas kernels for 13% -> 46%
where the time goes in v2:
time: 623 us; the launch traced here: 615 us
  Pallas kernels  315 us (51%)
  waiting for transfers between devices  186 us (30%)
  starting transfers between devices  59.6 us (10%)
  local copies, waits for them, and re-layouts  29.6 us (5%)
  matrix products  13.3 us (2%)
  other arithmetic  10.1 us (2%)
    pallas_call x36, Pallas kernels, call(): return made(*arrays, *after)  226 us
    ppermute x49, waiting for transfers between devices, swap(): return lax.ppermute(x, axis, [(i, i ^ flip) for i in range(size)])  167 us
    pallas_call x12, Pallas kernels, call(): pl.pallas_call(wrapped, grid_spec=spec, **keys)(prefetch, *arrays, *after)  88.7 us
    ppermute x49, starting transfers between devices, swap(): return lax.ppermute(x, axis, [(i, i ^ flip) for i in range(size)])  36.3 us
    unnamed x106, local copies, waits for them, and re-layouts  24.3 us
    all_to_all x5, starting transfers between devices, exchange(): return lax.all_to_all(x, 'seq', split_axis=0, concat_axis=0, tiled=True)  23.3 us
    all_to_all x5, waiting for transfers between devices, exchange(): return lax.all_to_all(x, 'seq', split_axis=0, concat_axis=0, tiled=True)  18.8 us
  transfers between devices with their start and end apart: 54, of which 17 were waited for; matrix products, arithmetic and copies ran while one was open for 3% of the time, Pallas kernels for 46%

profile of v2, /device:TPU:0, one launch (start us, length us, event | category | flops | bytes accessed | tf_op | source)
XLA Modules:
  0.0 615.0 jit_solution(12571677800897196422)
XLA Ops:
  8.8 7.3 %all-to-all-start = ((bf16[8,32,2048]{2,1,0:T(8,128)(2,1)}), bf16[8,32,2048]{2,1,0:T(8,128)(2,1)S(1)}, u32[]{:S(2)}, u32[]{:S(2)}) async-start(bf16[8,32,2048]{2,1,0:T(8,128)(2,1)} %bitcast.1), calls=%async_computation | async-start | bytes 2097152 | tf_op jit(solution)/shard_map/all_to_all | solution.py:545
  23.1 18.8 %all-to-all-done = bf16[8,32,2048]{2,1,0:T(8,128)(2,1)S(1)} async-done(((bf16[8,32,2048]{2,1,0:T(8,128)(2,1)}), bf16[8,32,2048]{2,1,0:T(8,128)(2,1)S(1)}, u32[]{:S(2)}, u32[]{:S(2)}) %all-to-all-start) | async-done | bytes 1048608 | tf_op jit(solution)/shard_map/all_to_all | solution.py:545
  56.2 7.4 %shard_map.367.refs_1_.refs_0_.refs_2_ = bf16[3,512,512]{2,1,0:T(8,128)(2,1)} custom-call(bf16[256,2048]{1,0:T(8,128)(2,1)} %shard_map.366.refs_0_.refs_1_, bf16[256,2048]{1,0:T(8,128)(2,1)} %copy-done.1, bf16[3,2048,512]{2,1,0:T(8,128)(2,1)} %bitcast.35), custom_call_target="tpu_custom_call" | custom-call | tf_op jit(solution)/shard_map/pallas_call | solution.py:44
  63.6 7.7 %collective-permute-done.1.refs_0_ = bf16[256,2048]{1,0:T(8,128)(2,1)S(1)} collective-permute-done((bf16[256,2048]{1,0:T(8,128)(2,1)}, bf16[256,2048]{1,0:T(8,128)(2,1)S(1)}, u32[]{:S(2)}, u32[]{:S(2)}) %collective-permute-start.1) | collective-permute-done | bytes 1048608 | tf_op jit(solution)/shard_map/ppermute | solution.py:542
  78.0 7.4 %shard_map.369.refs_1_.refs_3_ = bf16[3,512,512]{2,1,0:T(8,128)(2,1)} custom-call(bf16[256,2048]{1,0:T(8,128)(2,1)} %shard_map.368.refs_0_.refs_3_, bf16[256,2048]{1,0:T(8,128)(2,1)} %copy-done.2, bf16[3,2048,512]{2,1,0:T(8,128)(2,1)} %bitcast.36), custom_call_target="tpu_custom_call" | custom-call | tf_op jit(solution)/shard_map/pallas_call | solution.py:44
  85.4 7.6 %shard_map.370.refs_0_.refs_1_ = bf16[512,512]{1,0:T(8,128)(2,1)} custom-call(bf16[3,512,512]{2,1,0:T(8,128)(2,1)} %shard_map.367.refs_1_.refs_0_.refs_2_, bf16[3,512,512]{2,1,0:T(8,128)(2,1)} %shard_map.369.refs_1_.refs_3_, bf16[3,512,512]{2,1,0:T(8,128)(2,1)} %shard_map.367.refs_1_.refs_0_.refs_2_, bf16[3,512,512]{2,1,0:T(8,128)(2,1)} %shard_map.369.refs_1_.refs_3_, ...), custom_call_target="tpu_custom_call" | custom-call | tf_op jit(solution)/shard_map/pallas_call | solution.py:44
  98.2 7.7 %shard_map.372.refs_0_.refs_1_ = bf16[512,512]{1,0:T(8,128)(2,1)} custom-call(bf16[3,512,512]{2,1,0:T(8,128)(2,1)} %shard_map.367.refs_1_.refs_0_.refs_2_, bf16[3,512,512]{2,1,0:T(8,128)(2,1)} %shard_map.369.refs_1_.refs_3_, bf16[3,512,512]{2,1,0:T(8,128)(2,1)} %shard_map.367.refs_1_.refs_0_.refs_2_, bf16[3,512,512]{2,1,0:T(8,128)(2,1)} %shard_map.369.refs_1_.refs_3_, ...), custom_call_target="tpu_custom_call" | custom-call | tf_op jit(solution)/shard_map/pallas_call | solution.py:44
  115.2 22.3 %collective-permute-done.5.refs_3_ = bf16[256,2048]{1,0:T(8,128)(2,1)} collective-permute-done((bf16[256,2048]{1,0:T(8,128)(2,1)}, bf16[256,2048]{1,0:T(8,128)(2,1)}, u32[]{:S(2)}, u32[]{:S(2)}) %collective-permute-start.5) | collective-permute-done | bytes 1048608 | tf_op jit(solution)/shard_map/ppermute | solution.py:542
  145.2 15.1 %shard_map.375 = (bf16[512,2048]{1,0:T(8,128)(2,1)}, bf16[512,2048]{1,0:T(8,128)(2,1)}) custom-call(bf16[256,2048]{1,0:T(8,128)(2,1)} %get-tuple-element.72.refs_0_.refs_1_, bf16[256,2048]{1,0:T(8,128)(2,1)} %copy-done.8, bf16[256,2048]{1,0:T(8,128)(2,1)} %bitcast.48, bf16[256,2048]{1,0:T(8,128)(2,1)} %copy-done.9, bf16[2048,2048]{1,0:T(8,128)(2,1)} %refs_2_.12, ...), custom_call_target="tpu_custom_call" | custom-call | tf_op jit(solution)/shard_map/pallas_call | solution.py:44
  160.3 6.8 %collective-permute-done.8.refs_0_ = bf16[256,2048]{1,0:T(8,128)(2,1)S(1)} collective-permute-done((bf16[256,2048]{1,0:T(8,128)(2,1)}, bf16[256,2048]{1,0:T(8,128)(2,1)S(1)}, u32[]{:S(2)}, u32[]{:S(2)}) %collective-permute-start.8) | collective-permute-done | bytes 1048608 | tf_op jit(solution)/shard_map/ppermute | solution.py:542
  172.0 14.8 %shard_map.377 = (bf16[512,2048]{1,0:T(8,128)(2,1)}, bf16[512,2048]{1,0:T(8,128)(2,1)}) custom-call(bf16[256,2048]{1,0:T(8,128)(2,1)} %shard_map.376.refs_0_.refs_3_, bf16[256,2048]{1,0:T(8,128)(2,1)} %copy-done.10, bf16[256,2048]{1,0:T(8,128)(2,1)} %bitcast.56, bf16[256,2048]{1,0:T(8,128)(2,1)} %collective-permute-done.10.refs_3_.refs_4_, ...), custom_call_target="tpu_custom_call" | custom-call | tf_op jit(solution)/shard_map/pallas_call | solution.py:44
  186.8 9.7 %shard_map.378.refs_7_ = bf16[4,256,2048]{2,1,0:T(8,128)(2,1)} custom-call(s32[4]{0:T(128)} %get-tuple-element.145.refs_0_, bf16[256,2048]{1,0:T(8,128)(2,1)} %bitcast.49, bf16[256,2048]{1,0:T(8,128)(2,1)} %copy-done.9, bf16[256,2048]{1,0:T(8,128)(2,1)} %bitcast.57, bf16[256,2048]{1,0:T(8,128)(2,1)} %collective-permute-done.10.refs_3_.refs_4_, ...), custom_call_target="tpu_custom_call" | custom-call | tf_op jit(solution)/shard_map/pallas_call | solution.py:48
  198.5 9.6 %shard_map.379.refs_3_ = bf16[4,256,2048]{2,1,0:T(8,128)(2,1)} custom-call(s32[4]{0:T(128)} %get-tuple-element.147.refs_0_, bf16[256,2048]{1,0:T(8,128)(2,1)} %get-tuple-element.72.refs_0_.refs_1_, bf16[256,2048]{1,0:T(8,128)(2,1)} %copy-done.8, bf16[256,2048]{1,0:T(8,128)(2,1)} %shard_map.376.refs_0_.refs_3_, bf16[256,2048]{1,0:T(8,128)(2,1)} %copy-done.10, ...), custom_call_target="tpu_custom_call" | custom-call | tf_op jit(solution)/shard_map/pallas_call | solution.py:48
  208.1 8.8 %shard_map.380 = (bf16[256,2048]{1,0:T(8,128)(2,1)}, bf16[256,2048]{1,0:T(8,128)(2,1)}) custom-call(bf16[512,2048]{1,0:T(8,128)(2,1)} %get-tuple-element.75.refs_0_, bf16[512,2048]{1,0:T(8,128)(2,1)} %get-tuple-element.76.refs_1_, bf16[2048,2048]{1,0:T(8,128)(2,1)} %refs_2_.12, bf16[4,256,2048]{2,1,0:T(8,128)(2,1)} %shard_map.379.refs_3_), custom_call_target="tpu_custom_call" | custom-call | tf_op jit(solution)/shard_map/pallas_call | solution.py:44
  216.9 8.8 %shard_map.381 = (bf16[256,2048]{1,0:T(8,128)(2,1)}, bf16[256,2048]{1,0:T(8,128)(2,1)}) custom-call(bf16[512,2048]{1,0:T(8,128)(2,1)} %get-tuple-element.73.refs_1_.refs_0_, bf16[512,2048]{1,0:T(8,128)(2,1)} %get-tuple-element.74.refs_1_, bf16[2048,2048]{1,0:T(8,128)(2,1)} %refs_2_.14, bf16[256,2048]{1,0:T(8,128)(2,1)} %get-tuple-element.77.refs_3_), custom_call_target="tpu_custom_call" | custom-call | tf_op jit(solution)/shard_map/pallas_call | solution.py:44
  227.2 8.9 %shard_map.382 = (bf16[256,2048]{1,0:T(8,128)(2,1)}, bf16[256,2048]{1,0:T(8,128)(2,1)}) custom-call(bf16[512,2048]{1,0:T(8,128)(2,1)} %get-tuple-element.75.refs_0_, bf16[512,2048]{1,0:T(8,128)(2,1)} %get-tuple-element.76.refs_1_, bf16[2048,2048]{1,0:T(8,128)(2,1)} %refs_2_.12, bf16[256,2048]{1,0:T(8,128)(2,1)} %copy-done.22, ...), custom_call_target="tpu_custom_call" | custom-call | tf_op jit(solution)/shard_map/pallas_call | solution.py:44
  237.6 23.8 %collective-permute-done.14.refs_4_ = bf16[256,2048]{1,0:T(8,128)(2,1)S(1)} collective-permute-done((bf16[256,2048]{1,0:T(8,128)(2,1)}, bf16[256,2048]{1,0:T(8,128)(2,1)S(1)}, u32[]{:S(2)}, u32[]{:S(2)}) %collective-permute-start.14) | collective-permute-done | bytes 1048608 | tf_op jit(solution)/shard_map/ppermute | solution.py:542
  278.1 8.8 %shard_map.385 = (bf16[256,2048]{1,0:T(8,128)(2,1)}, bf16[256,2048]{1,0:T(8,128)(2,1)}) custom-call(bf16[512,2048]{1,0:T(8,128)(2,1)} %get-tuple-element.73.refs_1_.refs_0_, bf16[512,2048]{1,0:T(8,128)(2,1)} %get-tuple-element.74.refs_1_, bf16[2048,2048]{1,0:T(8,128)(2,1)} %refs_2_.14, bf16[256,2048]{1,0:T(8,128)(2,1)} %copy-done.36, ...), custom_call_target="tpu_custom_call" | custom-call | tf_op jit(solution)/shard_map/pallas_call | solution.py:44
  287.0 7.3 %collective-permute-done.19.refs_0_ = bf16[256,2048]{1,0:T(8,128)(2,1)S(1)} collective-permute-done((bf16[256,2048]{1,0:T(8,128)(2,1)}, bf16[256,2048]{1,0:T(8,128)(2,1)S(1)}, u32[]{:S(2)}, u32[]{:S(2)}) %collective-permute-start.19) | collective-permute-done | bytes 1048608 | tf_op jit(solution)/shard_map/ppermute | solution.py:542
  295.3 11.2 %shard_map.387 = (bf16[2,256,2048]{2,1,0:T(8,128)(2,1)}, bf16[2,256,2048]{2,1,0:T(8,128)(2,1)}) custom-call(s32[4]{0:T(128)} %get-tuple-element.144.refs_0_, bf16[256,2048]{1,0:T(8,128)(2,1)} %bitcast.51, bf16[256,2048]{1,0:T(8,128)(2,1)} %copy-done.9, bf16[256,2048]{1,0:T(8,128)(2,1)} %bitcast.58, ...), custom_call_target="tpu_custom_call" | custom-call | tf_op jit(solution)/shard_map/pallas_call | solution.py:48
  321.8 11.1 %shard_map.390 = (bf16[2,256,2048]{2,1,0:T(8,128)(2,1)}, bf16[2,256,2048]{2,1,0:T(8,128)(2,1)}) custom-call(s32[4]{0:T(128)} %get-tuple-element.146.refs_0_, bf16[256,2048]{1,0:T(8,128)(2,1)} %get-tuple-element.72.refs_0_.refs_1_, bf16[256,2048]{1,0:T(8,128)(2,1)} %copy-done.8, bf16[256,2048]{1,0:T(8,128)(2,1)} %shard_map.376.refs_0_.refs_3_, ...), custom_call_target="tpu_custom_call" | custom-call | tf_op jit(solution)/shard_map/pallas_call | solution.py:48
  344.4 24.6 %shard_map.392.refs_0_.refs_1_.refs_5_ = bf16[3,1024,512]{2,1,0:T(8,128)(2,1)} custom-call(bf16[3,512,512]{2,1,0:T(8,128)(2,1)} %shard_map.367.refs_1_.refs_0_.refs_2_, bf16[3,512,512]{2,1,0:T(8,128)(2,1)} %shard_map.369.refs_1_.refs_3_, bf16[256,512]{1,0:T(8,128)(2,1)} %get-tuple-element.84.refs_4_.refs_2_, bf16[256,512]{1,0:T(8,128)(2,1)} %get-tuple-element.90.refs_3_, ...), custom_call_target="tpu_custom_call" | custom-call | tf_op jit(solution)/shard_map/pallas_call | solution.py:44
  369.0 7.4 %shard_map.393 = (bf16[256,2048]{1,0:T(8,128)(2,1)}, bf16[256,2048]{1,0:T(8,128)(2,1)}) custom-call(bf16[3,1024,512]{2,1,0:T(8,128)(2,1)} %shard_map.392.refs_0_.refs_1_.refs_5_, bf16[3,1024,512]{2,1,0:T(8,128)(2,1)} %shard_map.392.refs_0_.refs_1_.refs_5_, bf16[3,2048,512]{2,1,0:T(8,128)(2,1)} %bitcast.37, ...), custom_call_target="tpu_custom_call" | custom-call | tf_op jit(solution)/shard_map/pallas_call | solution.py:44
  383.7 7.6 %shard_map.395 = (bf16[256,2048]{1,0:T(8,128)(2,1)}, bf16[256,2048]{1,0:T(8,128)(2,1)}) custom-call(bf16[3,1024,512]{2,1,0:T(8,128)(2,1)} %shard_map.392.refs_0_.refs_1_.refs_5_, bf16[3,1024,512]{2,1,0:T(8,128)(2,1)} %shard_map.392.refs_0_.refs_1_.refs_5_, bf16[3,2048,512]{2,1,0:T(8,128)(2,1)} %bitcast.38, ...), custom_call_target="tpu_custom_call" | custom-call | tf_op jit(solution)/shard_map/pallas_call | solution.py:44
  392.8 10.9 %collective-permute-done.26.refs_7_.refs_1_ = bf16[2,256,2048]{2,1,0:T(8,128)(2,1)S(1)} collective-permute-done((bf16[2,256,2048]{2,1,0:T(8,128)(2,1)}, bf16[2,256,2048]{2,1,0:T(8,128)(2,1)S(1)}, u32[]{:S(2)}, u32[]{:S(2)}) %collective-permute-start.26) | collective-permute-done | bytes 2097184 | tf_op jit(solution)/shard_map/ppermute | solution.py:542
  416.3 6.1 shard_map.398
  447.8 6.1 shard_map.402
  453.9 30.6 %collective-permute-done.34.refs_4_.refs_0_ = bf16[1,256,2048]{2,1,0:T(8,128)(2,1)S(1)} collective-permute-done((bf16[1,256,2048]{2,1,0:T(8,128)(2,1)}, bf16[1,256,2048]{2,1,0:T(8,128)(2,1)S(1)}, u32[]{:S(2)}, u32[]{:S(2)}) %collective-permute-start.34) | collective-permute-done | bytes 1048608 | tf_op jit(solution)/shard_map/ppermute | solution.py:542
  511.1 29.7 %collective-permute-done.40.refs_8_.refs_0_ = bf16[1,256,2048]{2,1,0:T(8,128)(2,1)S(1)} collective-permute-done((bf16[1,256,2048]{2,1,0:T(8,128)(2,1)}, bf16[1,256,2048]{2,1,0:T(8,128)(2,1)S(1)}, u32[]{:S(2)}, u32[]{:S(2)}) %collective-permute-start.40) | collective-permute-done | bytes 1048608 | tf_op jit(solution)/shard_map/ppermute | solution.py:542
  547.8 6.7 %shard_map.409.refs_7_ = bf16[1024,2048]{1,0:T(8,128)(2,1)} custom-call(s32[1,512]{1,0:T(1,128)} %broadcast_in_dim.129.refs_0_, bf16[256,2048]{1,0:T(8,128)(2,1)} %shard_map.407.refs_2_.refs_1_, bf16[256,2048]{1,0:T(8,128)(2,1)} %collective-permute-done.36.refs_2_, bf16[1024,2048]{1,0:T(8,128)(2,1)} %shard_map.403.refs_2_.refs_3_, ...), custom_call_target="tpu_custom_call" | custom-call | tf_op jit(solution)/shard_map/pallas_call | solution.py:44
  588.2 6.7 %shard_map.415.refs_2_ = bf16[1024,2048]{1,0:T(8,128)(2,1)} custom-call(s32[1,512]{1,0:T(1,128)} %broadcast_in_dim.129.refs_0_, bf16[256,2048]{1,0:T(8,128)(2,1)} %shard_map.413.refs_2_.refs_1_, bf16[256,2048]{1,0:T(8,128)(2,1)} %copy-done.32, bf16[1024,2048]{1,0:T(8,128)(2,1)} %shard_map.411.refs_2_.refs_3_, f32[256,2048]{1,0:T(8,128)} %shard_map.414.refs_4_), custom_call_target="tpu_custom_call" | custom-call | tf_op jit(solution)/shard_map/pallas_call | solution.py:44
  600.6 10.9 %collective-permute-done.46.refs_4_ = bf16[1,256,512]{2,1,0:T(8,128)(2,1)S(1)} collective-permute-done((bf16[1,256,512]{2,1,0:T(8,128)(2,1)}, bf16[1,256,512]{2,1,0:T(8,128)(2,1)S(1)}, u32[]{:S(2)}, u32[]{:S(2)}) %collective-permute-start.46) | collective-permute-done | bytes 262176 | tf_op jit(solution)/shard_map/ppermute | solution.py:542
  (273 shorter events, 235.4 us)
Async XLA Ops:
  8.8 33.0 %all-to-all-start = ((bf16[8,32,2048]{2,1,0:T(8,128)(2,1)}), bf16[8,32,2048]{2,1,0:T(8,128)(2,1)S(1)}, u32[]{:S(2)}, u32[]{:S(2)}) async-start(bf16[8,32,2048]{2,1,0:T(8,128)(2,1)} %bitcast.1), calls=%async_computation | async-start | bytes 2097152 | tf_op jit(solution)/shard_map/all_to_all | solution.py:545
  45.5 25.8 %collective-permute-start.1 = (bf16[256,2048]{1,0:T(8,128)(2,1)}, bf16[256,2048]{1,0:T(8,128)(2,1)S(1)}, u32[]{:S(2)}, u32[]{:S(2)}) collective-permute-start(bf16[256,2048]{1,0:T(8,128)(2,1)} %shard_map.366.refs_0_.refs_1_), channel_id=1, source_target_pairs={{0,2},{1,3},{2,0},{3,1},{4,6},{5,7},{6,4},{7,5},{8,10},{9,11},{10,... | collective-permute-start | bytes 3145736 | tf_op jit(solution)/shard_map/ppermute | solution.py:542
  50.2 63.0 %all-to-all-start.1 = ((bf16[8,64,2048]{2,1,0:T(8,128)(2,1)}), bf16[8,64,2048]{2,1,0:T(8,128)(2,1)}, u32[]{:S(2)}, u32[]{:S(2)}) async-start(bf16[8,64,2048]{2,1,0:T(8,128)(2,1)} %pad_maximum_fusion), calls=%async_computation.1 | async-start | bytes 4194304 | tf_op jit(solution)/shard_map/all_to_all | solution.py:545
  111.6 25.8 %collective-permute-start.5 = (bf16[256,2048]{1,0:T(8,128)(2,1)}, bf16[256,2048]{1,0:T(8,128)(2,1)}, u32[]{:S(2)}, u32[]{:S(2)}) collective-permute-start(bf16[256,2048]{1,0:T(8,128)(2,1)} %get-tuple-element.70), channel_id=1, source_target_pairs={{0,2},{1,3},{2,0},{3,1},{4,6},{5,7},{6,4},{7,5},{8,10},{9,11},{10,... | collective-permute-start | bytes 3145736 | tf_op jit(solution)/shard_map/ppermute | solution.py:542
  114.9 28.2 %collective-permute-start.7 = (bf16[256,2048]{1,0:T(8,128)(2,1)S(1)}, bf16[256,2048]{1,0:T(8,128)(2,1)S(1)}, u32[]{:S(2)}, u32[]{:S(2)}) collective-permute-start(bf16[256,2048]{1,0:T(8,128)(2,1)S(1)} %bitcast.47), channel_id=1, source_target_pairs={{0,1},{1,0},{2,3},{3,2},{4,5},{5,4},{6,7},{7,6},{8,9},{9,8},{10,11... | collective-permute-start | bytes 3145736 | tf_op jit(solution)/shard_map/ppermute | solution.py:542
  141.4 25.8 %collective-permute-start.8 = (bf16[256,2048]{1,0:T(8,128)(2,1)}, bf16[256,2048]{1,0:T(8,128)(2,1)S(1)}, u32[]{:S(2)}, u32[]{:S(2)}) collective-permute-start(bf16[256,2048]{1,0:T(8,128)(2,1)} %get-tuple-element.72.refs_0_.refs_1_), channel_id=1, source_target_pairs={{0,2},{1,3},{2,0},{3,1},{4,6},{5,7},{6,4},{7,5},{8,10},{9,11},{10,... | collective-permute-start | bytes 3145736 | tf_op jit(solution)/shard_map/ppermute | solution.py:542
  142.9 25.7 %collective-permute-start.10 = (bf16[256,2048]{1,0:T(8,128)(2,1)S(1)}, bf16[256,2048]{1,0:T(8,128)(2,1)}, u32[]{:S(2)}, u32[]{:S(2)}) collective-permute-start(bf16[256,2048]{1,0:T(8,128)(2,1)S(1)} %bitcast.55), channel_id=1, source_target_pairs={{0,1},{1,0},{2,3},{3,2},{4,5},{5,4},{6,7},{7,6},{8,9},{9,8},{10,11... | collective-permute-start | bytes 3145736 | tf_op jit(solution)/shard_map/ppermute | solution.py:542
  196.5 98.8 %collective-permute-start.21 = (bf16[4,256,2048]{2,1,0:T(8,128)(2,1)}, bf16[4,256,2048]{2,1,0:T(8,128)(2,1)}, u32[]{:S(2)}, u32[]{:S(2)}) collective-permute-start(bf16[4,256,2048]{2,1,0:T(8,128)(2,1)} %shard_map.378.refs_7_), channel_id=1, source_target_pairs={{0,4},{4,0},{8,12},{12,8},{16,20},{20,16},{24,28},{28,24},{1,5},{5... | collective-permute-start | bytes 12582920 | tf_op jit(solution)/shard_map/ppermute | solution.py:542
  216.9 93.4 %collective-permute-start.18 = (bf16[4,256,2048]{2,1,0:T(8,128)(2,1)}, bf16[4,256,2048]{2,1,0:T(8,128)(2,1)}, u32[]{:S(2)}, u32[]{:S(2)}) collective-permute-start(bf16[4,256,2048]{2,1,0:T(8,128)(2,1)} %shard_map.379.refs_3_), channel_id=1, source_target_pairs={{0,8},{4,12},{8,0},{12,4},{16,24},{20,28},{24,16},{28,20},{1,9},{5... | collective-permute-start | bytes 12582920 | tf_op jit(solution)/shard_map/ppermute | solution.py:542
  268.9 25.4 %collective-permute-start.19 = (bf16[256,2048]{1,0:T(8,128)(2,1)}, bf16[256,2048]{1,0:T(8,128)(2,1)S(1)}, u32[]{:S(2)}, u32[]{:S(2)}) collective-permute-start(bf16[256,2048]{1,0:T(8,128)(2,1)} %get-tuple-element.83.refs_0_.refs_3_), channel_id=1, source_target_pairs={{0,2},{1,3},{2,0},{3,1},{4,6},{5,7},{6,4},{7,5},{8,10},{9,11},{10,... | collective-permute-start | bytes 3145736 | tf_op jit(solution)/shard_map/ppermute | solution.py:542
  306.5 62.5 %collective-permute-start.24 = (bf16[2,256,2048]{2,1,0:T(8,128)(2,1)}, bf16[2,256,2048]{2,1,0:T(8,128)(2,1)}, u32[]{:S(2)}, u32[]{:S(2)}) collective-permute-start(bf16[2,256,2048]{2,1,0:T(8,128)(2,1)} %get-tuple-element.92), channel_id=1, source_target_pairs={{0,8},{4,12},{8,0},{12,4},{16,24},{20,28},{24,16},{28,20},{1,9},{5... | collective-permute-start | bytes 6291464 | tf_op jit(solution)/shard_map/ppermute | solution.py:542
  308.8 25.4 %collective-permute-start.17 = (bf16[256,2048]{1,0:T(8,128)(2,1)S(1)}, bf16[256,2048]{1,0:T(8,128)(2,1)S(1)}, u32[]{:S(2)}, u32[]{:S(2)}) collective-permute-start(bf16[256,2048]{1,0:T(8,128)(2,1)S(1)} %copy-done.23), channel_id=1, source_target_pairs={{0,2},{1,3},{2,0},{3,1},{4,6},{5,7},{6,4},{7,5},{8,10},{9,11},{10,... | collective-permute-start | bytes 3145736 | tf_op jit(solution)/shard_map/ppermute | solution.py:542
  321.2 47.8 %collective-permute-start.23 = (bf16[4,256,512]{2,1,0:T(8,128)(2,1)}, bf16[4,256,512]{2,1,0:T(8,128)(2,1)}, u32[]{:S(2)}, u32[]{:S(2)}) collective-permute-start(bf16[4,256,512]{2,1,0:T(8,128)(2,1)} %shard_map.389.refs_8_), channel_id=1, source_target_pairs={{0,4},{4,0},{8,12},{12,8},{16,20},{20,16},{24,28},{28,24},{1,5},{5... | collective-permute-start | bytes 3145736 | tf_op jit(solution)/shard_map/ppermute | solution.py:542
  338.6 38.3 %all-to-all-start.2 = ((bf16[8,32,2048]{2,1,0:T(8,128)(2,1)}), bf16[8,32,2048]{2,1,0:T(8,128)(2,1)S(1)}, u32[]{:S(2)}, u32[]{:S(2)}) async-start(bf16[8,32,2048]{2,1,0:T(8,128)(2,1)} %bitcast.67), calls=%async_computation.2 | async-start | bytes 2097152 | tf_op jit(solution)/shard_map/all_to_all | solution.py:545
  342.3 61.3 %collective-permute-start.26 = (bf16[2,256,2048]{2,1,0:T(8,128)(2,1)}, bf16[2,256,2048]{2,1,0:T(8,128)(2,1)S(1)}, u32[]{:S(2)}, u32[]{:S(2)}) collective-permute-start(bf16[2,256,2048]{2,1,0:T(8,128)(2,1)} %get-tuple-element.94), channel_id=1, source_target_pairs={{0,4},{4,0},{8,12},{12,8},{16,20},{20,16},{24,28},{28,24},{1,5},{5... | collective-permute-start | bytes 6291464 | tf_op jit(solution)/shard_map/ppermute | solution.py:542
  376.4 51.1 %collective-permute-start.28 = (bf16[256,2048]{1,0:T(8,128)(2,1)}, bf16[256,2048]{1,0:T(8,128)(2,1)}, u32[]{:S(2)}, u32[]{:S(2)}) collective-permute-start(bf16[256,2048]{1,0:T(8,128)(2,1)} %get-tuple-element.93.refs_6_), channel_id=1, source_target_pairs={{0,1},{1,0},{2,3},{3,2},{4,5},{5,4},{6,7},{7,6},{8,9},{9,8},{10,11... | collective-permute-start | bytes 3145736 | tf_op jit(solution)/shard_map/ppermute | solution.py:542
  383.6 43.9 %collective-permute-start.25 = (bf16[4,256,512]{2,1,0:T(8,128)(2,1)}, bf16[4,256,512]{2,1,0:T(8,128)(2,1)S(1)}, u32[]{:S(2)}, u32[]{:S(2)}) collective-permute-start(bf16[4,256,512]{2,1,0:T(8,128)(2,1)} %shard_map.394.refs_4_), channel_id=1, source_target_pairs={{0,4},{4,0},{8,12},{12,8},{16,20},{20,16},{24,28},{28,24},{1,5},{5... | collective-permute-start | bytes 3145736 | tf_op jit(solution)/shard_map/ppermute | solution.py:542
  391.3 36.2 %collective-permute-start.29 = (bf16[256,2048]{1,0:T(8,128)(2,1)}, bf16[256,2048]{1,0:T(8,128)(2,1)S(1)}, u32[]{:S(2)}, u32[]{:S(2)}) collective-permute-start(bf16[256,2048]{1,0:T(8,128)(2,1)} %get-tuple-element.98.refs_6_), channel_id=1, source_target_pairs={{0,2},{1,3},{2,0},{3,1},{4,6},{5,7},{6,4},{7,5},{8,10},{9,11},{10,... | collective-permute-start | bytes 3145736 | tf_op jit(solution)/shard_map/ppermute | solution.py:542
  392.8 49.0 %collective-permute-start.33 = (bf16[256,2048]{1,0:T(8,128)(2,1)S(1)}, bf16[256,2048]{1,0:T(8,128)(2,1)}, u32[]{:S(2)}, u32[]{:S(2)}) collective-permute-start(bf16[256,2048]{1,0:T(8,128)(2,1)S(1)} %bitcast.65), channel_id=1, source_target_pairs={{0,1},{1,0},{2,3},{3,2},{4,5},{5,4},{6,7},{7,6},{8,9},{9,8},{10,11... | collective-permute-start | bytes 3145736 | tf_op jit(solution)/shard_map/ppermute | solution.py:542
  426.5 57.9 %collective-permute-start.34 = (bf16[1,256,2048]{2,1,0:T(8,128)(2,1)}, bf16[1,256,2048]{2,1,0:T(8,128)(2,1)S(1)}, u32[]{:S(2)}, u32[]{:S(2)}) collective-permute-start(bf16[1,256,2048]{2,1,0:T(8,128)(2,1)} %get-tuple-element.106), channel_id=1, source_target_pairs={{0,16},{4,20},{8,24},{12,28},{16,0},{20,4},{24,8},{28,12},{1,17},{... | collective-permute-start | bytes 3145736 | tf_op jit(solution)/shard_map/ppermute | solution.py:542
  433.7 76.1 %all-to-all-start.3 = ((bf16[8,32,2048]{2,1,0:T(8,128)(2,1)}), bf16[8,32,2048]{2,1,0:T(8,128)(2,1)}, u32[]{:S(2)}, u32[]{:S(2)}) async-start(bf16[8,32,2048]{2,1,0:T(8,128)(2,1)} %bitcast.68), calls=%async_computation.3 | async-start | bytes 2097152 | tf_op jit(solution)/shard_map/all_to_all | solution.py:545
  438.2 56.8 %collective-permute-start.31 = (bf16[4,256,512]{2,1,0:T(8,128)(2,1)}, bf16[4,256,512]{2,1,0:T(8,128)(2,1)}, u32[]{:S(2)}, u32[]{:S(2)}) collective-permute-start(bf16[4,256,512]{2,1,0:T(8,128)(2,1)} %shard_map.396.refs_6_), channel_id=1, source_target_pairs={{0,4},{4,0},{8,12},{12,8},{16,20},{20,16},{24,28},{28,24},{1,5},{5... | collective-permute-start | bytes 3145736 | tf_op jit(solution)/shard_map/ppermute | solution.py:542
  440.2 60.8 %collective-permute-start.35 = (bf16[4,256,512]{2,1,0:T(8,128)(2,1)}, bf16[4,256,512]{2,1,0:T(8,128)(2,1)}, u32[]{:S(2)}, u32[]{:S(2)}) collective-permute-start(bf16[4,256,512]{2,1,0:T(8,128)(2,1)} %shard_map.397.refs_8_), channel_id=1, source_target_pairs={{0,4},{4,0},{8,12},{12,8},{16,20},{20,16},{24,28},{28,24},{1,5},{5... | collective-permute-start | bytes 3145736 | tf_op jit(solution)/shard_map/ppermute | solution.py:542
  440.3 68.6 %collective-permute-start.22 = (bf16[256,2048]{1,0:T(8,128)(2,1)S(1)}, bf16[256,2048]{1,0:T(8,128)(2,1)S(1)}, u32[]{:S(2)}, u32[]{:S(2)}) collective-permute-start(bf16[256,2048]{1,0:T(8,128)(2,1)S(1)} %bitcast.66), channel_id=1, source_target_pairs={{0,2},{1,3},{2,0},{3,1},{4,6},{5,7},{6,4},{7,5},{8,10},{9,11},{10,... | collective-permute-start | bytes 3145736 | tf_op jit(solution)/shard_map/ppermute | solution.py:542
  441.8 49.3 %collective-permute-start.32 = (bf16[2,256,512]{2,1,0:T(8,128)(2,1)}, bf16[2,256,512]{2,1,0:T(8,128)(2,1)}, u32[]{:S(2)}, u32[]{:S(2)}) collective-permute-start(bf16[2,256,512]{2,1,0:T(8,128)(2,1)} %get-tuple-element.105), channel_id=1, source_target_pairs={{0,8},{4,12},{8,0},{12,4},{16,24},{20,28},{24,16},{28,20},{1,9},{5... | collective-permute-start | bytes 1572872 | tf_op jit(solution)/shard_map/ppermute | solution.py:542
  491.1 49.7 %collective-permute-start.40 = (bf16[1,256,2048]{2,1,0:T(8,128)(2,1)}, bf16[1,256,2048]{2,1,0:T(8,128)(2,1)S(1)}, u32[]{:S(2)}, u32[]{:S(2)}) collective-permute-start(bf16[1,256,2048]{2,1,0:T(8,128)(2,1)} %get-tuple-element.111), channel_id=1, source_target_pairs={{0,16},{4,20},{8,24},{12,28},{16,0},{20,4},{24,8},{28,12},{1,17},{... | collective-permute-start | bytes 3145736 | tf_op jit(solution)/shard_map/ppermute | solution.py:542
  509.9 30.9 %collective-permute-start.36 = (bf16[256,2048]{1,0:T(8,128)(2,1)}, bf16[256,2048]{1,0:T(8,128)(2,1)}, u32[]{:S(2)}, u32[]{:S(2)}) collective-permute-start(bf16[256,2048]{1,0:T(8,128)(2,1)} %shard_map.407.refs_2_.refs_1_), channel_id=1, source_target_pairs={{0,1},{1,0},{2,3},{3,2},{4,5},{5,4},{6,7},{7,6},{8,9},{9,8},{10,11... | collective-permute-start | bytes 3145736 | tf_op jit(solution)/shard_map/ppermute | solution.py:542
  509.9 50.7 %collective-permute-start.39 = (bf16[256,2048]{1,0:T(8,128)(2,1)}, bf16[256,2048]{1,0:T(8,128)(2,1)S(1)}, u32[]{:S(2)}, u32[]{:S(2)}) collective-permute-start(bf16[256,2048]{1,0:T(8,128)(2,1)} %bitcast.22.refs_1_), channel_id=1, source_target_pairs={{0,1},{1,0},{2,3},{3,2},{4,5},{5,4},{6,7},{7,6},{8,9},{9,8},{10,11... | collective-permute-start | bytes 3145736 | tf_op jit(solution)/shard_map/ppermute | solution.py:542
  510.4 59.2 %collective-permute-start.37 = (bf16[256,2048]{1,0:T(8,128)(2,1)}, bf16[256,2048]{1,0:T(8,128)(2,1)S(1)}, u32[]{:S(2)}, u32[]{:S(2)}) collective-permute-start(bf16[256,2048]{1,0:T(8,128)(2,1)} %bitcast.22.refs_1_), channel_id=1, source_target_pairs={{0,2},{1,3},{2,0},{3,1},{4,6},{5,7},{6,4},{7,5},{8,10},{9,11},{10,... | collective-permute-start | bytes 3145736 | tf_op jit(solution)/shard_map/ppermute | solution.py:542
  511.1 56.2 %collective-permute-start.38 = (bf16[2,256,512]{2,1,0:T(8,128)(2,1)}, bf16[2,256,512]{2,1,0:T(8,128)(2,1)}, u32[]{:S(2)}, u32[]{:S(2)}) collective-permute-start(bf16[2,256,512]{2,1,0:T(8,128)(2,1)} %get-tuple-element.110), channel_id=1, source_target_pairs={{0,8},{4,12},{8,0},{12,4},{16,24},{20,28},{24,16},{28,20},{1,9},{5... | collective-permute-start | bytes 1572872 | tf_op jit(solution)/shard_map/ppermute | solution.py:542
  540.8 28.8 %collective-permute-start.41 = (bf16[1,256,512]{2,1,0:T(8,128)(2,1)}, bf16[1,256,512]{2,1,0:T(8,128)(2,1)}, u32[]{:S(2)}, u32[]{:S(2)}) collective-permute-start(bf16[1,256,512]{2,1,0:T(8,128)(2,1)} %get-tuple-element.114), channel_id=1, source_target_pairs={{0,16},{4,20},{8,24},{12,28},{16,0},{20,4},{24,8},{28,12},{1,17},{... | collective-permute-start | bytes 786440 | tf_op jit(solution)/shard_map/ppermute | solution.py:542
  540.8 28.8 %collective-permute-start.42 = (bf16[1,256,512]{2,1,0:T(8,128)(2,1)}, bf16[1,256,512]{2,1,0:T(8,128)(2,1)S(1)}, u32[]{:S(2)}, u32[]{:S(2)}) collective-permute-start(bf16[1,256,512]{2,1,0:T(8,128)(2,1)} %get-tuple-element.115), channel_id=1, source_target_pairs={{0,16},{4,20},{8,24},{12,28},{16,0},{20,4},{24,8},{28,12},{1,17},{... | collective-permute-start | bytes 786440 | tf_op jit(solution)/shard_map/ppermute | solution.py:542
  (75 other events, 586.0 us)

commit v3 on v2

--- a/solution.py
+++ b/solution.py
@@ -509,6 +509,51 @@
         flops=4 * rows * block * depth,
         after=after,
     )[0]
+
+
+PLAN = (
+    "fD",
+    "fU",
+    "KA",
+    "KB",
+    "BA",
+    "NB",
+    "GL",
+    "BB",
+    "GG",
+    "sD",
+    "GH",
+    "fO",
+    "sU",
+    "OS",
+    "AT",
+    "aD",
+    "KA1 O.y",
+    "fQ b2",
+    "KB1 x0",
+    "fK U.z",
+    "fV",
+    "NB1 Q.y",
+    "sO",
+    "aU D.l",
+    "sQ",
+    "OL v",
+    "aO",
+    "sK",
+    "aQ V.y",
+    "sV",
+    "aK",
+    "GX U.l O.l V.z",
+    "DE",
+    "OH",
+    "IL Q.l",
+    "aV K.l",
+    "GY w",
+    "UE",
+    "IH",
+    "OE",
+    "QE",
+)
 
 
 def local(
@@ -661,74 +706,183 @@
     normed_one, normed_two = (n0, n1, n2, n3), (m0, m1, m2, m3)
 
     acts, bars = (act_low, act_high), (bar_low, bar_high)
-    down, up = (straight, cots, acts, (0, 0, 1)), (turned, normed_two, bars, (0, 0, 1))
-
-    down_got, made = first_term(down)
-    up_got, made = first_term(up, after=(made,))
-    t1, t3 = block_matmul(bars_out, w_up, transposed=True, after=(made,))
-    b1, b3 = block_matmul(acts_out, w_down, after=(t1,))
-    t0, passed = block_matmul(bars_in, w_up, transposed=True, received=swap(t3, 1), after=(b1,))
-    h0, hidden_bar, gain_two, shift_two = norm_back(
-        cot0, hidden_in, (t0, swap(t1, 1), swap(passed, 2)), gain2, True
-    )
-    h2 = swap(h0, 2)
-    h1 = swap(h0, 1)
-
-    g0, g1 = block_matmul(((h0, 0, 1), (h1, 0, 1)), w_out, transposed=True)
-    b0, branch_passed = block_matmul(acts_in, w_down, received=swap(b3, 1), after=(g0,))
-    h2 = gate(h2, branch_passed)
-    h3 = swap(h2, 1)
-    down_got, down_keep = second_term(down, down_got, after=(h2,))
-    g2, g3 = block_matmul(((h2, 0, 1), (h3, 0, 1)), w_out, transposed=True, after=(down_keep, up_got))
-    out = (straight, (h1, h3, h0, h2), (mixed_out, mixed_in), (0, 0, 1))
-    out_got, made = first_term(out, after=(g2,))
-    up_got, up_keep = second_term(up, up_got, after=(made,))
-    output_slice = sum_low(hidden_in, (b0, swap(b1, 1), swap(branch_passed, 2)), after=(up_keep,))
-    output_home = exchange(output_slice)
-    qkv_bar = attend_back(qkv, (g0, g1, g2, g3), pos_col, pos_row, start_row, after=(output_slice,))
-    q_grad, k_grad, v_grad = [(straight, normed_one, (qkv_bar,), (n, 0, 1)) for n in range(3)]
-    u1, u3 = project_back(qkv_bar, w3, (1, 3), after=(out_got, down_got))
-    q_got, made = first_term(q_grad, after=(u1, output_home))
-    u0, passed = project_back(qkv_bar, w3, (0, 2), received=swap(u3, 1), after=(made,))
-    k_got, made = first_term(k_grad, after=(passed, up_got))
-    v_got, made = first_term(v_grad, after=(made,))
-    out_got, out_keep = second_term(out, out_got, after=(made,))
-    down_got, down_keep = next_terms(down, down_got, down_keep, after=(out_keep,))
-    input_slice, gain_one, shift_one = norm_back(
-        hidden_bar, embedded, (u0, swap(u1, 1), swap(passed, 2)), gain1, False, after=(down_keep, q_got)
-    )
-    input_home = exchange(input_slice)
-    vectors = jnp.concatenate([gain_one, shift_one, gain_two, shift_two], axis=0)
-    vectors = vectors + swap(vectors, 1)
-    vectors = vectors + swap(vectors, 2)
-    vectors = jnp.transpose(vectors.reshape(4, n_seq, block), (1, 0, 2))
-    vectors = jnp.sum(exchange(vectors), axis=0)
-
+    have = {}
+    grads = {
+        "D": (straight, cots, acts, (0, 0, 1)),
+        "U": (turned, normed_two, bars, (0, 0, 1)),
+    }
     where = [sent_all[None, : 2 * quarter], sent_all[None, 2 * quarter :]]
-    x0, x1, x2 = output_home, swap(output_home, 1), swap(output_home, 2)
-    up_got, up_keep = next_terms(up, up_got, up_keep, after=(input_slice,))
-    q_got, q_keep = second_term(q_grad, q_got, after=(up_keep,))
-    first = place(where[0], (x0, x1), rows, after=(q_keep, down_got))
-    out_got, out_keep = next_terms(out, out_got, out_keep, after=(first,))
-    k_got, k_keep = second_term(k_grad, k_got, after=(out_keep,))
-    q_got, q_keep = next_terms(q_grad, q_got, q_keep, after=(k_keep, v_got))
-    x2 = gate(x2, q_keep)
-    down_grad = add_last([(down_got, down_keep)], True, after=(x2,))
-    block_output = place(where[1], (x2, swap(x2, 1)), rows, first, after=(down_grad,))
-    y0, y1, y2 = input_home, swap(input_home, 1), swap(input_home, 2)
-    v_got, v_keep = second_term(v_grad, v_got, after=(block_output, up_got))
-    first = place(where[0], (y0, y1), rows, after=(v_keep,))
-    k_got, k_keep = next_terms(k_grad, k_got, k_keep, after=(first,))
-    y2 = gate(y2, k_keep, out_got, q_got)
-    up_grad = add_last([(up_got, up_keep)], False, after=(y2,))
-    input_grad = place(where[1], (y2, swap(y2, 1)), rows, first, after=(up_grad,))
-    v_got, v_keep = next_terms(v_grad, v_got, v_keep, after=(input_grad,))
-    out_grad = add_last([(out_got, out_keep)], True, after=(v_keep,))
-    qkv_grad = add_last(
-        [(q_got, q_keep), (k_got, k_keep), (v_got, v_keep)], False, True, after=(out_grad,)
-    )
-    qkv_grad = jnp.transpose(qkv_grad, (1, 0, 2))
-
+
+    def first(name, after):
+        have[name + ".y"], made = first_term(grads[name], after)
+        return made
+
+    def second(name, after):
+        have[name + ".z"], have[name + ".k"] = second_term(grads[name], have[name + ".y"], after)
+        return have[name + ".k"]
+
+    def add(name, after):
+        have[name + ".l"], have[name + ".m"] = next_terms(grads[name], have[name + ".z"], have[name + ".k"], after)
+        return have[name + ".m"]
+
+    def last(name):
+        return have[name + ".l"], have[name + ".m"]
+
+    def near_up(after):
+        t1, t3 = block_matmul(bars_out, w_up, transposed=True, after=after)
+        have["t1"], have["t3"] = swap(t1, 1), swap(t3, 1)
+        return t1
+
+    def near_branch(after):
+        b1, b3 = block_matmul(acts_out, w_down, after=after)
+        have["b1"], have["b3"] = swap(b1, 1), swap(b3, 1)
+        return b1
+
+    def far_up(after):
+        have["t0"], passed = block_matmul(bars_in, w_up, transposed=True, received=have["t3"], after=after)
+        have["t2"] = swap(passed, 2)
+        return passed
+
+    def far_branch(after):
+        have["b0"], passed = block_matmul(acts_in, w_down, received=have["b3"], after=after)
+        have["b2"] = swap(passed, 2)
+        return passed
+
+    def hidden(after):
+        h0, have["hidden_bar"], have["gain_two"], have["shift_two"] = norm_back(
+            cot0, hidden_in, (have["t0"], have["t1"], have["t2"]), gain2, True, after=after
+        )
+        have["h0"], have["h2"], have["h1"] = h0, swap(h0, 2), swap(h0, 1)
+        return h0
+
+    def context_low(after):
+        have["g0"], have["g1"] = block_matmul(
+            ((have["h0"], 0, 1), (have["h1"], 0, 1)), w_out, transposed=True, after=after
+        )
+        return have["g1"]
+
+    def gate_hidden(after):
+        have["h2"] = gate(have["h2"], *after)
+        have["h3"] = swap(have["h2"], 1)
+        grads["O"] = (
+            straight,
+            (have["h1"], have["h3"], have["h0"], have["h2"]),
+            (mixed_out, mixed_in),
+            (0, 0, 1),
+        )
+        return have["h2"]
+
+    def context_high(after):
+        have["g2"], have["g3"] = block_matmul(
+            ((have["h2"], 0, 1), (have["h3"], 0, 1)), w_out, transposed=True, after=after
+        )
+        return have["g3"]
+
+    def output(after):
+        made = sum_low(hidden_in, (have["b0"], have["b1"], have["b2"]), after=after)
+        home = exchange(made)
+        have["x0"], have["x1"], have["x2"] = home, swap(home, 1), swap(home, 2)
+        return made
+
+    def attention(after):
+        made = attend_back(
+            qkv, [have[g] for g in ("g0", "g1", "g2", "g3")], pos_col, pos_row, start_row, after=after
+        )
+        for n, name in enumerate(("Q", "K", "V")):
+            grads[name] = (straight, normed_one, (made,), (n, 0, 1))
+        have["qkv_bar"] = made
+        return made
+
+    def near_input(after):
+        u1, u3 = project_back(have["qkv_bar"], w3, (1, 3), after=after)
+        have["u1"], have["u3"] = swap(u1, 1), swap(u3, 1)
+        return u1
+
+    def far_input(after):
+        have["u0"], passed = project_back(have["qkv_bar"], w3, (0, 2), received=have["u3"], after=after)
+        have["u2"] = swap(passed, 2)
+        return passed
+
+    def inputs(after):
+        made, gain_one, shift_one = norm_back(
+            have["hidden_bar"], embedded, (have["u0"], have["u1"], have["u2"]), gain1, False, after=after
+        )
+        home = exchange(made)
+        have["y0"], have["y1"], have["y2"] = home, swap(home, 1), swap(home, 2)
+        vectors = jnp.concatenate([gain_one, shift_one, have["gain_two"], have["shift_two"]], axis=0)
+        vectors = vectors + swap(vectors, 1)
+        have["v"] = vectors + swap(vectors, 2)
+        have["w"] = exchange(jnp.transpose(have["v"].reshape(4, n_seq, block), (1, 0, 2)))
+        return made
+
+    def place_low(out, x, after):
+        have[out] = place(where[0], (have[x + "0"], have[x + "1"]), rows, after=after)
+        return have[out]
+
+    def gate_across(x, after):
+        have[x + "2"] = gate(have[x + "2"], *after)
+        have[x + "3"] = swap(have[x + "2"], 1)
+        return have[x + "2"]
+
+    def place_high(out, x, after):
+        have[out] = place(where[1], (have[x + "2"], have[x + "3"]), rows, have[out], after=after)
+        return have[out]
+
+    def down_end(after):
+        have["down"] = add_last([last("D")], True, after=after)
+        return have["down"]
+
+    def up_end(after):
+        have["up"] = add_last([last("U")], False, after=after)
+        return have["up"]
+
+    def out_end(after):
+        have["out"] = add_last([last("O")], True, after=after)
+        return have["out"]
+
+    def qkv_end(after):
+        have["qkv"] = add_last([last("Q"), last("K"), last("V")], False, True, after=after)
+        return have["qkv"]
+
+    steps = {
+        "KA": near_up,
+        "BA": near_branch,
+        "KB": far_up,
+        "NB": hidden,
+        "GL": context_low,
+        "BB": far_branch,
+        "GG": gate_hidden,
+        "GH": context_high,
+        "OS": output,
+        "AT": attention,
+        "KA1": near_input,
+        "KB1": far_input,
+        "NB1": inputs,
+        "OL": partial(place_low, "output", "x"),
+        "GX": partial(gate_across, "x"),
+        "OH": partial(place_high, "output", "x"),
+        "IL": partial(place_low, "input", "y"),
+        "GY": partial(gate_across, "y"),
+        "IH": partial(place_high, "input", "y"),
+        "DE": down_end,
+        "UE": up_end,
+        "OE": out_end,
+        "QE": qkv_end,
+    }
+    for name in "DUOQKV":
+        steps["f" + name] = partial(first, name)
+        steps["s" + name] = partial(second, name)
+        steps["a" + name] = partial(add, name)
+    made = None
+    for line in PLAN:
+        step, *arrivals = line.split()
+        after = () if made is None else (made,)
+        made = steps[step](after + tuple(have[a] for a in arrivals))
+
+    block_output, input_grad = have["output"], have["input"]
+    down_grad, up_grad, out_grad = have["down"], have["up"], have["out"]
+    qkv_grad = jnp.transpose(have["qkv"], (1, 0, 2))
+    vectors = jnp.sum(have["w"], axis=0)
     return (
         block_output,
         input_grad,

time: 623 us -> 592 us (0.950)
  waiting for transfers between devices: 186 us -> 151 us
    ppermute x49, waiting for transfers between devices: 167 us -> 132 us  [swap(): return lax.ppermute(x, axis, [(i, i ^ flip) for i in range(size)])]
    unnamed x106 -> x112, local copies, waits for them, and re-layouts: 24.3 us -> 25.2 us
  transfers between devices with their start and end apart: 54 -> 54, of which waited for: 17 -> 22; matrix products, arithmetic and copies ran while one was open for 3% -> 4% of each run, Pallas kernels for 46% -> 49%
where the time goes in v3:
time: 592 us; the launch traced here: 584 us
  Pallas kernels  315 us (53%)
  waiting for transfers between devices  151 us (26%)
  starting transfers between devices  61.7 us (10%)
  local copies, waits for them, and re-layouts  30.4 us (5%)
  matrix products  13.3 us (2%)
  other arithmetic  10.9 us (2%)
    pallas_call x36, Pallas kernels, call(): return made(*arrays, *after)  226 us
    ppermute x49, waiting for transfers between devices, swap(): return lax.ppermute(x, axis, [(i, i ^ flip) for i in range(size)])  132 us
    pallas_call x12, Pallas kernels, call(): pl.pallas_call(wrapped, grid_spec=spec, **keys)(prefetch, *arrays, *after)  88.9 us
    ppermute x49, starting transfers between devices, swap(): return lax.ppermute(x, axis, [(i, i ^ flip) for i in range(size)])  36.4 us
    all_to_all x5, starting transfers between devices, exchange(): return lax.all_to_all(x, 'seq', split_axis=0, concat_axis=0, tiled=True)  25.3 us
    unnamed x112, local copies, waits for them, and re-layouts  25.2 us
    all_to_all x5, waiting for transfers between devices, exchange(): return lax.all_to_all(x, 'seq', split_axis=0, concat_axis=0, tiled=True)  18.8 us
  transfers between devices with their start and end apart: 54, of which 22 were waited for; matrix products, arithmetic and copies ran while one was open for 4% of the time, Pallas kernels for 49%

profile of v3, /device:TPU:0, one launch (start us, length us, event | category | flops | bytes accessed | tf_op | source)
XLA Modules:
  0.0 583.7 jit_solution(12519706375516339305)
XLA Ops:
  8.8 7.3 %all-to-all-start = ((bf16[8,32,2048]{2,1,0:T(8,128)(2,1)}), bf16[8,32,2048]{2,1,0:T(8,128)(2,1)S(1)}, u32[]{:S(2)}, u32[]{:S(2)}) async-start(bf16[8,32,2048]{2,1,0:T(8,128)(2,1)} %bitcast.1), calls=%async_computation | async-start | bytes 2097152 | tf_op jit(solution)/shard_map/all_to_all | solution.py:590
  23.1 18.8 %all-to-all-done = bf16[8,32,2048]{2,1,0:T(8,128)(2,1)S(1)} async-done(((bf16[8,32,2048]{2,1,0:T(8,128)(2,1)}), bf16[8,32,2048]{2,1,0:T(8,128)(2,1)S(1)}, u32[]{:S(2)}, u32[]{:S(2)}) %all-to-all-start) | async-done | bytes 1048608 | tf_op jit(solution)/shard_map/all_to_all | solution.py:590
  56.2 7.4 %shard_map.367.refs_1_.refs_0_.refs_2_ = bf16[3,512,512]{2,1,0:T(8,128)(2,1)} custom-call(bf16[256,2048]{1,0:T(8,128)(2,1)} %shard_map.366.refs_0_.refs_1_, bf16[256,2048]{1,0:T(8,128)(2,1)} %copy-done.1, bf16[3,2048,512]{2,1,0:T(8,128)(2,1)} %bitcast.35), custom_call_target="tpu_custom_call" | custom-call | tf_op jit(solution)/shard_map/pallas_call | solution.py:44
  63.6 7.8 %collective-permute-done.1.refs_0_ = bf16[256,2048]{1,0:T(8,128)(2,1)S(1)} collective-permute-done((bf16[256,2048]{1,0:T(8,128)(2,1)}, bf16[256,2048]{1,0:T(8,128)(2,1)S(1)}, u32[]{:S(2)}, u32[]{:S(2)}) %collective-permute-start.1) | collective-permute-done | bytes 1048608 | tf_op jit(solution)/shard_map/ppermute | solution.py:587
  78.0 7.4 %shard_map.369.refs_1_.refs_3_ = bf16[3,512,512]{2,1,0:T(8,128)(2,1)} custom-call(bf16[256,2048]{1,0:T(8,128)(2,1)} %shard_map.368.refs_0_.refs_3_, bf16[256,2048]{1,0:T(8,128)(2,1)} %copy-done.2, bf16[3,2048,512]{2,1,0:T(8,128)(2,1)} %bitcast.36), custom_call_target="tpu_custom_call" | custom-call | tf_op jit(solution)/shard_map/pallas_call | solution.py:44
  85.4 7.6 %shard_map.370.refs_0_.refs_1_ = bf16[512,512]{1,0:T(8,128)(2,1)} custom-call(bf16[3,512,512]{2,1,0:T(8,128)(2,1)} %shard_map.367.refs_1_.refs_0_.refs_2_, bf16[3,512,512]{2,1,0:T(8,128)(2,1)} %shard_map.369.refs_1_.refs_3_, bf16[3,512,512]{2,1,0:T(8,128)(2,1)} %shard_map.367.refs_1_.refs_0_.refs_2_, bf16[3,512,512]{2,1,0:T(8,128)(2,1)} %shard_map.369.refs_1_.refs_3_, ...), custom_call_target="tpu_custom_call" | custom-call | tf_op jit(solution)/shard_map/pallas_call | solution.py:44
  98.1 7.6 %shard_map.372.refs_0_.refs_1_ = bf16[512,512]{1,0:T(8,128)(2,1)} custom-call(bf16[3,512,512]{2,1,0:T(8,128)(2,1)} %shard_map.367.refs_1_.refs_0_.refs_2_, bf16[3,512,512]{2,1,0:T(8,128)(2,1)} %shard_map.369.refs_1_.refs_3_, bf16[3,512,512]{2,1,0:T(8,128)(2,1)} %shard_map.367.refs_1_.refs_0_.refs_2_, bf16[3,512,512]{2,1,0:T(8,128)(2,1)} %shard_map.369.refs_1_.refs_3_, ...), custom_call_target="tpu_custom_call" | custom-call | tf_op jit(solution)/shard_map/pallas_call | solution.py:44
  115.1 22.3 %collective-permute-done.5.refs_3_ = bf16[256,2048]{1,0:T(8,128)(2,1)} collective-permute-done((bf16[256,2048]{1,0:T(8,128)(2,1)}, bf16[256,2048]{1,0:T(8,128)(2,1)}, u32[]{:S(2)}, u32[]{:S(2)}) %collective-permute-start.5) | collective-permute-done | bytes 1048608 | tf_op jit(solution)/shard_map/ppermute | solution.py:587
  145.1 15.1 %shard_map.375 = (bf16[512,2048]{1,0:T(8,128)(2,1)}, bf16[512,2048]{1,0:T(8,128)(2,1)}) custom-call(bf16[256,2048]{1,0:T(8,128)(2,1)} %get-tuple-element.72.refs_0_.refs_1_, bf16[256,2048]{1,0:T(8,128)(2,1)} %copy-done.8, bf16[256,2048]{1,0:T(8,128)(2,1)} %bitcast.48, bf16[256,2048]{1,0:T(8,128)(2,1)} %copy-done.9, bf16[2048,2048]{1,0:T(8,128)(2,1)} %refs_2_.11, ...), custom_call_target="tpu_custom_call" | custom-call | tf_op jit(solution)/shard_map/pallas_call | solution.py:44
  160.2 6.9 %collective-permute-done.8.refs_0_ = bf16[256,2048]{1,0:T(8,128)(2,1)S(1)} collective-permute-done((bf16[256,2048]{1,0:T(8,128)(2,1)}, bf16[256,2048]{1,0:T(8,128)(2,1)S(1)}, u32[]{:S(2)}, u32[]{:S(2)}) %collective-permute-start.8) | collective-permute-done | bytes 1048608 | tf_op jit(solution)/shard_map/ppermute | solution.py:587
  171.9 14.8 %shard_map.377 = (bf16[512,2048]{1,0:T(8,128)(2,1)}, bf16[512,2048]{1,0:T(8,128)(2,1)}) custom-call(bf16[256,2048]{1,0:T(8,128)(2,1)} %shard_map.376.refs_0_.refs_3_, bf16[256,2048]{1,0:T(8,128)(2,1)} %copy-done.10, bf16[256,2048]{1,0:T(8,128)(2,1)} %bitcast.56, bf16[256,2048]{1,0:T(8,128)(2,1)} %collective-permute-done.10.refs_3_.refs_4_, ...), custom_call_target="tpu_custom_call" | custom-call | tf_op jit(solution)/shard_map/pallas_call | solution.py:44
  186.7 9.7 %shard_map.378.refs_7_ = bf16[4,256,2048]{2,1,0:T(8,128)(2,1)} custom-call(s32[4]{0:T(128)} %get-tuple-element.145.refs_0_, bf16[256,2048]{1,0:T(8,128)(2,1)} %bitcast.49, bf16[256,2048]{1,0:T(8,128)(2,1)} %copy-done.9, bf16[256,2048]{1,0:T(8,128)(2,1)} %bitcast.57, bf16[256,2048]{1,0:T(8,128)(2,1)} %collective-permute-done.10.refs_3_.refs_4_, ...), custom_call_target="tpu_custom_call" | custom-call | tf_op jit(solution)/shard_map/pallas_call | solution.py:48
  198.4 9.6 %shard_map.379.refs_3_ = bf16[4,256,2048]{2,1,0:T(8,128)(2,1)} custom-call(s32[4]{0:T(128)} %get-tuple-element.147.refs_0_, bf16[256,2048]{1,0:T(8,128)(2,1)} %get-tuple-element.72.refs_0_.refs_1_, bf16[256,2048]{1,0:T(8,128)(2,1)} %copy-done.8, bf16[256,2048]{1,0:T(8,128)(2,1)} %shard_map.376.refs_0_.refs_3_, bf16[256,2048]{1,0:T(8,128)(2,1)} %copy-done.10, ...), custom_call_target="tpu_custom_call" | custom-call | tf_op jit(solution)/shard_map/pallas_call | solution.py:48
  208.0 8.8 %shard_map.380 = (bf16[256,2048]{1,0:T(8,128)(2,1)}, bf16[256,2048]{1,0:T(8,128)(2,1)}) custom-call(bf16[512,2048]{1,0:T(8,128)(2,1)} %get-tuple-element.75.refs_0_, bf16[512,2048]{1,0:T(8,128)(2,1)} %get-tuple-element.76.refs_1_, bf16[2048,2048]{1,0:T(8,128)(2,1)} %refs_2_.11, bf16[4,256,2048]{2,1,0:T(8,128)(2,1)} %shard_map.379.refs_3_), custom_call_target="tpu_custom_call" | custom-call | tf_op jit(solution)/shard_map/pallas_call | solution.py:44
  220.6 8.9 %shard_map.381 = (bf16[256,2048]{1,0:T(8,128)(2,1)}, bf16[256,2048]{1,0:T(8,128)(2,1)}) custom-call(bf16[512,2048]{1,0:T(8,128)(2,1)} %get-tuple-element.75.refs_0_, bf16[512,2048]{1,0:T(8,128)(2,1)} %get-tuple-element.76.refs_1_, bf16[2048,2048]{1,0:T(8,128)(2,1)} %refs_2_.11, bf16[256,2048]{1,0:T(8,128)(2,1)} %copy-done.22, ...), custom_call_target="tpu_custom_call" | custom-call | tf_op jit(solution)/shard_map/pallas_call | solution.py:44
  231.0 8.7 %shard_map.382 = (bf16[256,2048]{1,0:T(8,128)(2,1)}, bf16[256,2048]{1,0:T(8,128)(2,1)}) custom-call(bf16[512,2048]{1,0:T(8,128)(2,1)} %get-tuple-element.73.refs_1_.refs_0_, bf16[512,2048]{1,0:T(8,128)(2,1)} %get-tuple-element.74.refs_1_, bf16[2048,2048]{1,0:T(8,128)(2,1)} %refs_2_.14, bf16[256,2048]{1,0:T(8,128)(2,1)} %get-tuple-element.79.refs_3_), custom_call_target="tpu_custom_call" | custom-call | tf_op jit(solution)/shard_map/pallas_call | solution.py:44
  239.7 15.2 %collective-permute-done.14.refs_4_ = bf16[256,2048]{1,0:T(8,128)(2,1)S(1)} collective-permute-done((bf16[256,2048]{1,0:T(8,128)(2,1)}, bf16[256,2048]{1,0:T(8,128)(2,1)S(1)}, u32[]{:S(2)}, u32[]{:S(2)}) %collective-permute-start.14) | collective-permute-done | bytes 1048608 | tf_op jit(solution)/shard_map/ppermute | solution.py:587
  271.6 8.8 %shard_map.385 = (bf16[256,2048]{1,0:T(8,128)(2,1)}, bf16[256,2048]{1,0:T(8,128)(2,1)}) custom-call(bf16[512,2048]{1,0:T(8,128)(2,1)} %get-tuple-element.73.refs_1_.refs_0_, bf16[512,2048]{1,0:T(8,128)(2,1)} %get-tuple-element.74.refs_1_, bf16[2048,2048]{1,0:T(8,128)(2,1)} %refs_2_.14, bf16[256,2048]{1,0:T(8,128)(2,1)} %copy-done.37, ...), custom_call_target="tpu_custom_call" | custom-call | tf_op jit(solution)/shard_map/pallas_call | solution.py:44
  280.4 7.4 %collective-permute-done.19.refs_0_ = bf16[256,2048]{1,0:T(8,128)(2,1)S(1)} collective-permute-done((bf16[256,2048]{1,0:T(8,128)(2,1)}, bf16[256,2048]{1,0:T(8,128)(2,1)S(1)}, u32[]{:S(2)}, u32[]{:S(2)}) %collective-permute-start.19) | collective-permute-done | bytes 1048608 | tf_op jit(solution)/shard_map/ppermute | solution.py:587
  289.4 11.2 %shard_map.387 = (bf16[2,256,2048]{2,1,0:T(8,128)(2,1)}, bf16[2,256,2048]{2,1,0:T(8,128)(2,1)}) custom-call(s32[4]{0:T(128)} %get-tuple-element.144.refs_0_, bf16[256,2048]{1,0:T(8,128)(2,1)} %bitcast.51, bf16[256,2048]{1,0:T(8,128)(2,1)} %copy-done.9, bf16[256,2048]{1,0:T(8,128)(2,1)} %bitcast.58, ...), custom_call_target="tpu_custom_call" | custom-call | tf_op jit(solution)/shard_map/pallas_call | solution.py:48
  314.5 11.1 %shard_map.390 = (bf16[2,256,2048]{2,1,0:T(8,128)(2,1)}, bf16[2,256,2048]{2,1,0:T(8,128)(2,1)}) custom-call(s32[4]{0:T(128)} %get-tuple-element.146.refs_0_, bf16[256,2048]{1,0:T(8,128)(2,1)} %get-tuple-element.72.refs_0_.refs_1_, bf16[256,2048]{1,0:T(8,128)(2,1)} %copy-done.8, bf16[256,2048]{1,0:T(8,128)(2,1)} %shard_map.376.refs_0_.refs_3_, ...), custom_call_target="tpu_custom_call" | custom-call | tf_op jit(solution)/shard_map/pallas_call | solution.py:48
  337.1 24.6 %shard_map.392.refs_2_.refs_0_.refs_1_.refs_5_ = bf16[3,1024,512]{2,1,0:T(8,128)(2,1)} custom-call(bf16[3,512,512]{2,1,0:T(8,128)(2,1)} %shard_map.367.refs_1_.refs_0_.refs_2_, bf16[3,512,512]{2,1,0:T(8,128)(2,1)} %shard_map.369.refs_1_.refs_3_, bf16[256,512]{1,0:T(8,128)(2,1)} %get-tuple-element.90.refs_2_, ...), custom_call_target="tpu_custom_call" | custom-call | tf_op jit(solution)/shard_map/pallas_call | solution.py:44
  370.7 7.4 %shard_map.394 = (bf16[256,2048]{1,0:T(8,128)(2,1)}, bf16[256,2048]{1,0:T(8,128)(2,1)}) custom-call(bf16[3,1024,512]{2,1,0:T(8,128)(2,1)} %shard_map.392.refs_2_.refs_0_.refs_1_.refs_5_, bf16[3,1024,512]{2,1,0:T(8,128)(2,1)} %shard_map.392.refs_2_.refs_0_.refs_1_.refs_5_, bf16[3,2048,512]{2,1,0:T(8,128)(2,1)} %bitcast.37, ...), custom_call_target="tpu_custom_call" | custom-call | tf_op jit(solution)/shard_map/pallas_call | solution.py:44
  385.2 7.6 %shard_map.396 = (bf16[256,2048]{1,0:T(8,128)(2,1)}, bf16[256,2048]{1,0:T(8,128)(2,1)}) custom-call(bf16[3,1024,512]{2,1,0:T(8,128)(2,1)} %shard_map.392.refs_2_.refs_0_.refs_1_.refs_5_, bf16[3,1024,512]{2,1,0:T(8,128)(2,1)} %shard_map.392.refs_2_.refs_0_.refs_1_.refs_5_, bf16[3,2048,512]{2,1,0:T(8,128)(2,1)} %bitcast.38, ...), custom_call_target="tpu_custom_call" | custom-call | tf_op jit(solution)/shard_map/pallas_call | solution.py:44
  408.1 9.1 %collective-permute-done.30.refs_7_.refs_6_ = bf16[4,256,512]{2,1,0:T(8,128)(2,1)} collective-permute-done((bf16[4,256,512]{2,1,0:T(8,128)(2,1)}, bf16[4,256,512]{2,1,0:T(8,128)(2,1)}, u32[]{:S(2)}, u32[]{:S(2)}) %collective-permute-start.30) | collective-permute-done | bytes 1048608 | tf_op jit(solution)/shard_map/ppermute | solution.py:587
  454.0 8.6 %collective-permute-done.31.refs_1_ = bf16[2,256,512]{2,1,0:T(8,128)(2,1)} collective-permute-done((bf16[2,256,512]{2,1,0:T(8,128)(2,1)}, bf16[2,256,512]{2,1,0:T(8,128)(2,1)}, u32[]{:S(2)}, u32[]{:S(2)}) %collective-permute-start.31) | collective-permute-done | bytes 524320 | tf_op jit(solution)/shard_map/ppermute | solution.py:587
  481.0 13.4 %collective-permute-done.37.refs_3_.refs_6_ = bf16[4,256,512]{2,1,0:T(8,128)(2,1)} collective-permute-done((bf16[4,256,512]{2,1,0:T(8,128)(2,1)S(1)}, bf16[4,256,512]{2,1,0:T(8,128)(2,1)}, u32[]{:S(2)}, u32[]{:S(2)}) %collective-permute-start.37) | collective-permute-done | bytes 1048608 | tf_op jit(solution)/shard_map/ppermute | solution.py:587
  496.5 6.2 %shard_map.407 = (bf16[2,256,512]{2,1,0:T(8,128)(2,1)}, bf16[2,256,512]{2,1,0:T(8,128)(2,1)}) custom-call(s32[4]{0:T(128)} %get-tuple-element.144.refs_0_, bf16[256,2048]{1,0:T(8,128)(2,1)} %shard_map.366.refs_0_.refs_1_, bf16[256,2048]{1,0:T(8,128)(2,1)} %copy-done.1, bf16[256,2048]{1,0:T(8,128)(2,1)} %shard_map.368.refs_0_.refs_3_, ...), custom_call_target="tpu_custom_call" | custom-call | tf_op jit(solution)/shard_map/pallas_call | solution.py:48
  506.6 13.7 %collective-permute-done.36.refs_1_ = bf16[2,256,512]{2,1,0:T(8,128)(2,1)S(1)} collective-permute-done((bf16[2,256,512]{2,1,0:T(8,128)(2,1)}, bf16[2,256,512]{2,1,0:T(8,128)(2,1)S(1)}, u32[]{:S(2)}, u32[]{:S(2)}) %collective-permute-start.36) | collective-permute-done | bytes 524320 | tf_op jit(solution)/shard_map/ppermute | solution.py:587
  523.2 8.2 %collective-permute-done.41.refs_4_.refs_1_ = bf16[2,256,512]{2,1,0:T(8,128)(2,1)S(1)} collective-permute-done((bf16[2,256,512]{2,1,0:T(8,128)(2,1)}, bf16[2,256,512]{2,1,0:T(8,128)(2,1)S(1)}, u32[]{:S(2)}, u32[]{:S(2)}) %collective-permute-start.41) | collective-permute-done | bytes 524320 | tf_op jit(solution)/shard_map/ppermute | solution.py:587
  545.1 6.7 %shard_map.411.refs_3_ = bf16[1024,2048]{1,0:T(8,128)(2,1)} custom-call(s32[1,512]{1,0:T(1,128)} %broadcast_in_dim.129.refs_0_, bf16[256,2048]{1,0:T(8,128)(2,1)} %shard_map.409.refs_2_.refs_1_, bf16[256,2048]{1,0:T(8,128)(2,1)} %collective-permute-done.42.refs_2_, bf16[1024,2048]{1,0:T(8,128)(2,1)} %shard_map.403.refs_2_.refs_3_, ...), custom_call_target="tpu_custom_call" | custom-call | tf_op jit(solution)/shard_map/pallas_call | solution.py:44
  571.4 6.7 %shard_map.416.refs_2_ = bf16[1024,2048]{1,0:T(8,128)(2,1)} custom-call(s32[1,512]{1,0:T(1,128)} %broadcast_in_dim.129.refs_0_, bf16[256,2048]{1,0:T(8,128)(2,1)} %shard_map.414.refs_2_.refs_1_, bf16[256,2048]{1,0:T(8,128)(2,1)} %copy-done.36, bf16[1024,2048]{1,0:T(8,128)(2,1)} %shard_map.412.refs_2_.refs_3_, f32[256,2048]{1,0:T(8,128)} %shard_map.415.refs_4_), custom_call_target="tpu_custom_call" | custom-call | tf_op jit(solution)/shard_map/pallas_call | solution.py:44
  (279 shorter events, 247.7 us)
Async XLA Ops:
  8.8 33.0 %all-to-all-start = ((bf16[8,32,2048]{2,1,0:T(8,128)(2,1)}), bf16[8,32,2048]{2,1,0:T(8,128)(2,1)S(1)}, u32[]{:S(2)}, u32[]{:S(2)}) async-start(bf16[8,32,2048]{2,1,0:T(8,128)(2,1)} %bitcast.1), calls=%async_computation | async-start | bytes 2097152 | tf_op jit(solution)/shard_map/all_to_all | solution.py:590
  45.5 25.8 %collective-permute-start.1 = (bf16[256,2048]{1,0:T(8,128)(2,1)}, bf16[256,2048]{1,0:T(8,128)(2,1)S(1)}, u32[]{:S(2)}, u32[]{:S(2)}) collective-permute-start(bf16[256,2048]{1,0:T(8,128)(2,1)} %shard_map.366.refs_0_.refs_1_), channel_id=1, source_target_pairs={{0,2},{1,3},{2,0},{3,1},{4,6},{5,7},{6,4},{7,5},{8,10},{9,11},{10,... | collective-permute-start | bytes 3145736 | tf_op jit(solution)/shard_map/ppermute | solution.py:587
  50.1 62.9 %all-to-all-start.1 = ((bf16[8,64,2048]{2,1,0:T(8,128)(2,1)}), bf16[8,64,2048]{2,1,0:T(8,128)(2,1)}, u32[]{:S(2)}, u32[]{:S(2)}) async-start(bf16[8,64,2048]{2,1,0:T(8,128)(2,1)} %pad_maximum_fusion), calls=%async_computation.1 | async-start | bytes 4194304 | tf_op jit(solution)/shard_map/all_to_all | solution.py:590
  111.6 25.8 %collective-permute-start.5 = (bf16[256,2048]{1,0:T(8,128)(2,1)}, bf16[256,2048]{1,0:T(8,128)(2,1)}, u32[]{:S(2)}, u32[]{:S(2)}) collective-permute-start(bf16[256,2048]{1,0:T(8,128)(2,1)} %get-tuple-element.70), channel_id=1, source_target_pairs={{0,2},{1,3},{2,0},{3,1},{4,6},{5,7},{6,4},{7,5},{8,10},{9,11},{10,... | collective-permute-start | bytes 3145736 | tf_op jit(solution)/shard_map/ppermute | solution.py:587
  114.8 28.2 %collective-permute-start.7 = (bf16[256,2048]{1,0:T(8,128)(2,1)S(1)}, bf16[256,2048]{1,0:T(8,128)(2,1)S(1)}, u32[]{:S(2)}, u32[]{:S(2)}) collective-permute-start(bf16[256,2048]{1,0:T(8,128)(2,1)S(1)} %bitcast.47), channel_id=1, source_target_pairs={{0,1},{1,0},{2,3},{3,2},{4,5},{5,4},{6,7},{7,6},{8,9},{9,8},{10,11... | collective-permute-start | bytes 3145736 | tf_op jit(solution)/shard_map/ppermute | solution.py:587
  141.3 25.8 %collective-permute-start.8 = (bf16[256,2048]{1,0:T(8,128)(2,1)}, bf16[256,2048]{1,0:T(8,128)(2,1)S(1)}, u32[]{:S(2)}, u32[]{:S(2)}) collective-permute-start(bf16[256,2048]{1,0:T(8,128)(2,1)} %get-tuple-element.72.refs_0_.refs_1_), channel_id=1, source_target_pairs={{0,2},{1,3},{2,0},{3,1},{4,6},{5,7},{6,4},{7,5},{8,10},{9,11},{10,... | collective-permute-start | bytes 3145736 | tf_op jit(solution)/shard_map/ppermute | solution.py:587
  142.8 25.7 %collective-permute-start.10 = (bf16[256,2048]{1,0:T(8,128)(2,1)S(1)}, bf16[256,2048]{1,0:T(8,128)(2,1)}, u32[]{:S(2)}, u32[]{:S(2)}) collective-permute-start(bf16[256,2048]{1,0:T(8,128)(2,1)S(1)} %bitcast.55), channel_id=1, source_target_pairs={{0,1},{1,0},{2,3},{3,2},{4,5},{5,4},{6,7},{7,6},{8,9},{9,8},{10,11... | collective-permute-start | bytes 3145736 | tf_op jit(solution)/shard_map/ppermute | solution.py:587
  196.4 92.9 %collective-permute-start.21 = (bf16[4,256,2048]{2,1,0:T(8,128)(2,1)}, bf16[4,256,2048]{2,1,0:T(8,128)(2,1)}, u32[]{:S(2)}, u32[]{:S(2)}) collective-permute-start(bf16[4,256,2048]{2,1,0:T(8,128)(2,1)} %shard_map.378.refs_7_), channel_id=1, source_target_pairs={{0,4},{4,0},{8,12},{12,8},{16,20},{20,16},{24,28},{28,24},{1,5},{5... | collective-permute-start | bytes 12582920 | tf_op jit(solution)/shard_map/ppermute | solution.py:587
  216.8 97.8 %collective-permute-start.18 = (bf16[4,256,2048]{2,1,0:T(8,128)(2,1)}, bf16[4,256,2048]{2,1,0:T(8,128)(2,1)}, u32[]{:S(2)}, u32[]{:S(2)}) collective-permute-start(bf16[4,256,2048]{2,1,0:T(8,128)(2,1)} %shard_map.379.refs_3_), channel_id=1, source_target_pairs={{0,8},{4,12},{8,0},{12,4},{16,24},{20,28},{24,16},{28,20},{1,9},{5... | collective-permute-start | bytes 12582920 | tf_op jit(solution)/shard_map/ppermute | solution.py:587
  229.5 25.4 %collective-permute-start.14 = (bf16[256,2048]{1,0:T(8,128)(2,1)}, bf16[256,2048]{1,0:T(8,128)(2,1)S(1)}, u32[]{:S(2)}, u32[]{:S(2)}) collective-permute-start(bf16[256,2048]{1,0:T(8,128)(2,1)} %get-tuple-element.79.refs_3_), channel_id=1, source_target_pairs={{0,2},{1,3},{2,0},{3,1},{4,6},{5,7},{6,4},{7,5},{8,10},{9,11},{10,... | collective-permute-start | bytes 3145736 | tf_op jit(solution)/shard_map/ppermute | solution.py:587
  262.4 25.4 %collective-permute-start.19 = (bf16[256,2048]{1,0:T(8,128)(2,1)}, bf16[256,2048]{1,0:T(8,128)(2,1)S(1)}, u32[]{:S(2)}, u32[]{:S(2)}) collective-permute-start(bf16[256,2048]{1,0:T(8,128)(2,1)} %get-tuple-element.83.refs_0_.refs_3_), channel_id=1, source_target_pairs={{0,2},{1,3},{2,0},{3,1},{4,6},{5,7},{6,4},{7,5},{8,10},{9,11},{10,... | collective-permute-start | bytes 3145736 | tf_op jit(solution)/shard_map/ppermute | solution.py:587
  300.6 66.1 %collective-permute-start.23 = (bf16[2,256,2048]{2,1,0:T(8,128)(2,1)}, bf16[2,256,2048]{2,1,0:T(8,128)(2,1)}, u32[]{:S(2)}, u32[]{:S(2)}) collective-permute-start(bf16[2,256,2048]{2,1,0:T(8,128)(2,1)} %get-tuple-element.92), channel_id=1, source_target_pairs={{0,8},{4,12},{8,0},{12,4},{16,24},{20,28},{24,16},{28,20},{1,9},{5... | collective-permute-start | bytes 6291464 | tf_op jit(solution)/shard_map/ppermute | solution.py:587
  300.7 25.6 %collective-permute-start.17 = (bf16[256,2048]{1,0:T(8,128)(2,1)S(1)}, bf16[256,2048]{1,0:T(8,128)(2,1)S(1)}, u32[]{:S(2)}, u32[]{:S(2)}) collective-permute-start(bf16[256,2048]{1,0:T(8,128)(2,1)S(1)} %copy-done.24), channel_id=1, source_target_pairs={{0,2},{1,3},{2,0},{3,1},{4,6},{5,7},{6,4},{7,5},{8,10},{9,11},{10,... | collective-permute-start | bytes 3145736 | tf_op jit(solution)/shard_map/ppermute | solution.py:587
  313.1 57.6 %collective-permute-start.24 = (bf16[4,256,512]{2,1,0:T(8,128)(2,1)}, bf16[4,256,512]{2,1,0:T(8,128)(2,1)}, u32[]{:S(2)}, u32[]{:S(2)}) collective-permute-start(bf16[4,256,512]{2,1,0:T(8,128)(2,1)} %shard_map.389.refs_8_), channel_id=1, source_target_pairs={{0,4},{4,0},{8,12},{12,8},{16,20},{20,16},{24,28},{28,24},{1,5},{5... | collective-permute-start | bytes 3145736 | tf_op jit(solution)/shard_map/ppermute | solution.py:587
  330.7 53.6 %all-to-all-start.2 = ((bf16[8,32,2048]{2,1,0:T(8,128)(2,1)}), bf16[8,32,2048]{2,1,0:T(8,128)(2,1)S(1)}, u32[]{:S(2)}, u32[]{:S(2)}) async-start(bf16[8,32,2048]{2,1,0:T(8,128)(2,1)} %bitcast.63), calls=%async_computation.2 | async-start | bytes 2097152 | tf_op jit(solution)/shard_map/all_to_all | solution.py:590
  335.0 60.5 %collective-permute-start.26 = (bf16[2,256,2048]{2,1,0:T(8,128)(2,1)}, bf16[2,256,2048]{2,1,0:T(8,128)(2,1)S(1)}, u32[]{:S(2)}, u32[]{:S(2)}) collective-permute-start(bf16[2,256,2048]{2,1,0:T(8,128)(2,1)} %get-tuple-element.97), channel_id=1, source_target_pairs={{0,4},{4,0},{8,12},{12,8},{16,20},{20,16},{24,28},{28,24},{1,5},{5... | collective-permute-start | bytes 6291464 | tf_op jit(solution)/shard_map/ppermute | solution.py:587
  378.1 39.2 %collective-permute-start.28 = (bf16[256,2048]{1,0:T(8,128)(2,1)}, bf16[256,2048]{1,0:T(8,128)(2,1)}, u32[]{:S(2)}, u32[]{:S(2)}) collective-permute-start(bf16[256,2048]{1,0:T(8,128)(2,1)} %get-tuple-element.95.refs_6_), channel_id=1, source_target_pairs={{0,1},{1,0},{2,3},{3,2},{4,5},{5,4},{6,7},{7,6},{8,9},{9,8},{10,11... | collective-permute-start | bytes 3145736 | tf_op jit(solution)/shard_map/ppermute | solution.py:587
  384.3 33.0 %collective-permute-start.30 = (bf16[4,256,512]{2,1,0:T(8,128)(2,1)}, bf16[4,256,512]{2,1,0:T(8,128)(2,1)}, u32[]{:S(2)}, u32[]{:S(2)}) collective-permute-start(bf16[4,256,512]{2,1,0:T(8,128)(2,1)} %shard_map.395.refs_4_), channel_id=1, source_target_pairs={{0,4},{4,0},{8,12},{12,8},{16,20},{20,16},{24,28},{28,24},{1,5},{5... | collective-permute-start | bytes 3145736 | tf_op jit(solution)/shard_map/ppermute | solution.py:587
  394.3 47.4 %collective-permute-start.33 = (bf16[1,256,2048]{2,1,0:T(8,128)(2,1)}, bf16[1,256,2048]{2,1,0:T(8,128)(2,1)S(1)}, u32[]{:S(2)}, u32[]{:S(2)}) collective-permute-start(bf16[1,256,2048]{2,1,0:T(8,128)(2,1)} %get-tuple-element.103), channel_id=1, source_target_pairs={{0,16},{4,20},{8,24},{12,28},{16,0},{20,4},{24,8},{28,12},{1,17},{... | collective-permute-start | bytes 3145736 | tf_op jit(solution)/shard_map/ppermute | solution.py:587
  395.5 57.4 %collective-permute-start.32 = (bf16[256,2048]{1,0:T(8,128)(2,1)}, bf16[256,2048]{1,0:T(8,128)(2,1)}, u32[]{:S(2)}, u32[]{:S(2)}) collective-permute-start(bf16[256,2048]{1,0:T(8,128)(2,1)} %bitcast.65), channel_id=1, source_target_pairs={{0,1},{1,0},{2,3},{3,2},{4,5},{5,4},{6,7},{7,6},{8,9},{9,8},{10,11... | collective-permute-start | bytes 3145736 | tf_op jit(solution)/shard_map/ppermute | solution.py:587
  430.3 32.3 %collective-permute-start.31 = (bf16[2,256,512]{2,1,0:T(8,128)(2,1)}, bf16[2,256,512]{2,1,0:T(8,128)(2,1)}, u32[]{:S(2)}, u32[]{:S(2)}) collective-permute-start(bf16[2,256,512]{2,1,0:T(8,128)(2,1)} %get-tuple-element.102), channel_id=1, source_target_pairs={{0,8},{4,12},{8,0},{12,4},{16,24},{20,28},{24,16},{28,20},{1,9},{5... | collective-permute-start | bytes 1572872 | tf_op jit(solution)/shard_map/ppermute | solution.py:587
  431.4 100.9 %all-to-all-start.3 = ((bf16[8,32,2048]{2,1,0:T(8,128)(2,1)}), bf16[8,32,2048]{2,1,0:T(8,128)(2,1)}, u32[]{:S(2)}, u32[]{:S(2)}) async-start(bf16[8,32,2048]{2,1,0:T(8,128)(2,1)} %bitcast.21), calls=%async_computation.3 | async-start | bytes 2097152 | tf_op jit(solution)/shard_map/all_to_all | solution.py:590
  436.0 36.1 %collective-permute-start.27 = (bf16[4,256,512]{2,1,0:T(8,128)(2,1)}, bf16[4,256,512]{2,1,0:T(8,128)(2,1)}, u32[]{:S(2)}, u32[]{:S(2)}) collective-permute-start(bf16[4,256,512]{2,1,0:T(8,128)(2,1)} %shard_map.397.refs_6_), channel_id=1, source_target_pairs={{0,4},{4,0},{8,12},{12,8},{16,20},{20,16},{24,28},{28,24},{1,5},{5... | collective-permute-start | bytes 3145736 | tf_op jit(solution)/shard_map/ppermute | solution.py:587
  438.1 56.3 %collective-permute-start.37 = (bf16[4,256,512]{2,1,0:T(8,128)(2,1)S(1)}, bf16[4,256,512]{2,1,0:T(8,128)(2,1)}, u32[]{:S(2)}, u32[]{:S(2)}) collective-permute-start(bf16[4,256,512]{2,1,0:T(8,128)(2,1)S(1)} %copy-done.18), channel_id=1, source_target_pairs={{0,4},{4,0},{8,12},{12,8},{16,20},{20,16},{24,28},{28,24},{1,5},{5... | collective-permute-start | bytes 3145736 | tf_op jit(solution)/shard_map/ppermute | solution.py:587
  452.9 70.3 %collective-permute-start.22 = (bf16[256,2048]{1,0:T(8,128)(2,1)S(1)}, bf16[256,2048]{1,0:T(8,128)(2,1)S(1)}, u32[]{:S(2)}, u32[]{:S(2)}) collective-permute-start(bf16[256,2048]{1,0:T(8,128)(2,1)S(1)} %bitcast.67), channel_id=1, source_target_pairs={{0,2},{1,3},{2,0},{3,1},{4,6},{5,7},{6,4},{7,5},{8,10},{9,11},{10,... | collective-permute-start | bytes 3145736 | tf_op jit(solution)/shard_map/ppermute | solution.py:587
  454.0 40.4 %collective-permute-start.38 = (bf16[2,256,512]{2,1,0:T(8,128)(2,1)}, bf16[2,256,512]{2,1,0:T(8,128)(2,1)}, u32[]{:S(2)}, u32[]{:S(2)}) collective-permute-start(bf16[2,256,512]{2,1,0:T(8,128)(2,1)} %get-tuple-element.113), channel_id=1, source_target_pairs={{0,8},{4,12},{8,0},{12,4},{16,24},{20,28},{24,16},{28,20},{1,9},{5... | collective-permute-start | bytes 1572872 | tf_op jit(solution)/shard_map/ppermute | solution.py:587
  462.6 68.8 %collective-permute-start.39 = (bf16[1,256,2048]{2,1,0:T(8,128)(2,1)}, bf16[1,256,2048]{2,1,0:T(8,128)(2,1)}, u32[]{:S(2)}, u32[]{:S(2)}) collective-permute-start(bf16[1,256,2048]{2,1,0:T(8,128)(2,1)} %get-tuple-element.117), channel_id=1, source_target_pairs={{0,16},{4,20},{8,24},{12,28},{16,0},{20,4},{24,8},{28,12},{1,17},{... | collective-permute-start | bytes 3145736 | tf_op jit(solution)/shard_map/ppermute | solution.py:587
  478.2 42.1 %collective-permute-start.36 = (bf16[2,256,512]{2,1,0:T(8,128)(2,1)}, bf16[2,256,512]{2,1,0:T(8,128)(2,1)S(1)}, u32[]{:S(2)}, u32[]{:S(2)}) collective-permute-start(bf16[2,256,512]{2,1,0:T(8,128)(2,1)} %get-tuple-element.112), channel_id=1, source_target_pairs={{0,8},{4,12},{8,0},{12,4},{16,24},{20,28},{24,16},{28,20},{1,9},{5... | collective-permute-start | bytes 1572872 | tf_op jit(solution)/shard_map/ppermute | solution.py:587
  502.7 28.8 %collective-permute-start.41 = (bf16[2,256,512]{2,1,0:T(8,128)(2,1)}, bf16[2,256,512]{2,1,0:T(8,128)(2,1)S(1)}, u32[]{:S(2)}, u32[]{:S(2)}) collective-permute-start(bf16[2,256,512]{2,1,0:T(8,128)(2,1)} %get-tuple-element.119), channel_id=1, source_target_pairs={{0,8},{4,12},{8,0},{12,4},{16,24},{20,28},{24,16},{28,20},{1,9},{5... | collective-permute-start | bytes 1572872 | tf_op jit(solution)/shard_map/ppermute | solution.py:587
  532.8 31.0 %collective-permute-start.43 = (bf16[256,2048]{1,0:T(8,128)(2,1)}, bf16[256,2048]{1,0:T(8,128)(2,1)S(1)}, u32[]{:S(2)}, u32[]{:S(2)}) collective-permute-start(bf16[256,2048]{1,0:T(8,128)(2,1)} %bitcast.22.refs_1_), channel_id=1, source_target_pairs={{0,2},{1,3},{2,0},{3,1},{4,6},{5,7},{6,4},{7,5},{8,10},{9,11},{10,... | collective-permute-start | bytes 3145736 | tf_op jit(solution)/shard_map/ppermute | solution.py:587
  533.9 27.1 %collective-permute-start.46 = (bf16[1,256,512]{2,1,0:T(8,128)(2,1)S(1)}, bf16[1,256,512]{2,1,0:T(8,128)(2,1)S(1)}, u32[]{:S(2)}, u32[]{:S(2)}) collective-permute-start(bf16[1,256,512]{2,1,0:T(8,128)(2,1)S(1)} %copy-done.54), channel_id=1, source_target_pairs={{0,16},{4,20},{8,24},{12,28},{16,0},{20,4},{24,8},{28,12},{1,17},{... | collective-permute-start | bytes 786440 | tf_op jit(solution)/shard_map/ppermute | solution.py:587
  536.2 27.5 %all-to-all-start.4 = ((f32[8,4,256]{2,1,0:T(4,128)}), f32[8,4,256]{2,1,0:T(4,128)S(1)}, u32[]{:S(2)}, u32[]{:S(2)}) async-start(f32[8,4,256]{2,1,0:T(4,128)} %bitcast.24), calls=%async_computation.4 | async-start | bytes 65536 | tf_op jit(solution)/shard_map/all_to_all | solution.py:590
  (78 other events, 624.7 us)

commit v4 on v3

--- a/solution.py
+++ b/solution.py
@@ -197,23 +197,17 @@
     heads = width // HEAD_DIM
     factor = 1.0 / math.sqrt(HEAD_DIM)
 
-    def body(x_ref, y_ref, low_ref, high_ref, px_ref, py_ref, sx_ref, sy_ref, pr_ref, o_ref, kv, both):
-        i = pl.program_id(0)
-
-        @pl.when(i == 0)
-        def _():
-            kv[:, :half] = low_ref[1:]
-            kv[:, half:] = high_ref[1:]
-            both[0] = x_ref[0]
-            both[1] = y_ref[0]
-
+    def body(x_ref, y_ref, low_ref, high_ref, px_ref, py_ref, sx_ref, sy_ref, pr_ref, o_ref, kv):
+        kv[:, :half] = low_ref[1:]
+        kv[:, half:] = high_ref[1:]
         keys = pr_ref[...]
-        at = jnp.where(i == 0, px_ref[...], py_ref[...])
-        since = jnp.where(i == 0, sx_ref[...], sy_ref[...])
+        at = jnp.concatenate([px_ref[...], py_ref[...]], axis=0)
+        since = jnp.concatenate([sx_ref[...], sy_ref[...]], axis=0)
         bias = jnp.where((keys <= at) & (keys >= since), 0.0, -1e30)
         for head in range(heads):
             cols = slice(head * HEAD_DIM, (head + 1) * HEAD_DIM)
-            scores = dot(both[i, :, cols], kv[0, :, cols], NT) * factor + bias
+            q = jnp.concatenate([x_ref[0, :, cols], y_ref[0, :, cols]], axis=0)
+            scores = dot(q, kv[0, :, cols], NT) * factor + bias
             peak = jnp.max(scores, axis=-1, keepdims=True)
             grown = jnp.exp(scores - peak)
             total = jnp.sum(grown, axis=-1, keepdims=True)
@@ -221,7 +215,7 @@
 
     return call(
         body,
-        (2,),
+        (1,),
         [(qkv[n // 2], (1, rows, width), lambda i, n=n: (0, n % 2, 0)) for n in picks]
         + [
             (qkv[0], (3, half, width), lambda i: (0, 0, 0)),
@@ -229,8 +223,8 @@
         ]
         + [(c, (rows, 1), lambda i, n=n: (n, 0)) for c in (pos_col, start_col) for n in picks]
         + [(pos_row, (1, 2 * half), lambda i: (0, 0))],
-        [((half, width), BF16, (rows, width), lambda i: (i, 0))],
-        [pltpu.VMEM((2, 2 * half, width), BF16), pltpu.VMEM((2, rows, width), BF16)],
+        [((half, width), BF16, (half, width), lambda i: (0, 0))],
+        [pltpu.VMEM((2, 2 * half, width), BF16)],
         flops=8 * half * half * width,
         special=2 * heads * half * half,
         after=after,
@@ -240,7 +234,7 @@
 def attend_back(qkv, bars, pos_col, pos_row, start_row, after=()):
     _, half, width = qkv[0].shape
     rows = 2 * half
-    tile = rows // 4
+    tile = rows // 2
     heads = width // HEAD_DIM
     factor = 1.0 / math.sqrt(HEAD_DIM)
 
@@ -257,11 +251,12 @@
             all_qkv[:, :half] = low_ref[...]
             all_qkv[:, half:] = high_ref[...]
 
-        for number, g_ref in enumerate((g0, g1, g2, g3)):
+        for number, (one, two) in enumerate(((g0, g1), (g2, g3))):
 
             @pl.when(step == number)
             def _():
-                g_tile[...] = g_ref[...]
+                g_tile[: tile // 2] = one[...]
+                g_tile[tile // 2 :] = two[...]
 
         here = pl.ds(pl.multiple_of(step * tile, tile), tile)
         for head in range(heads):
@@ -286,11 +281,11 @@
 
     return call(
         body,
-        (4,),
+        (2,),
         [
             (qkv[0], (3, half, width), lambda i: (0, 0, 0)),
             (qkv[1], (3, half, width), lambda i: (0, 0, 0)),
-            *[(bar, (tile, width), lambda i: (0, 0)) for bar in bars],
+            *[(bar, (tile // 2, width), lambda i: (0, 0)) for bar in bars],
             (pos_col, (rows, 1), lambda i: (0, 0)),
             (pos_row, (1, tile), lambda i: (0, i)),
             (start_row, (1, tile), lambda i: (0, i)),
@@ -529,7 +524,7 @@
     "AT",
     "aD",
     "KA1 O.y",
-    "fQ b2",
+    "fQ",
     "KB1 x0",
     "fK U.z",
     "fV",
@@ -651,9 +646,11 @@
     n3 = swap(n2, 1)
     qkv = (qkv_low, project((n2, n3), w3))
     mixed_out = attend((1, 3), qkv, pos_col, start_col, pos_row)
-    a1, a3 = block_matmul(((mixed_out, 0, 2), (mixed_out, 1, 2)), w_out)
+    a1, a3 = block_matmul(((mixed_out, 0, 2), (mixed_out, 1, 2)), w_out, tile=1024)
     mixed_in = attend((0, 2), qkv, pos_col, start_col, pos_row, after=(a1,))
-    a0, passed = block_matmul(((mixed_in, 0, 2), (mixed_in, 1, 2)), w_out, received=swap(a3, 1))
+    a0, passed = block_matmul(
+        ((mixed_in, 0, 2), (mixed_in, 1, 2)), w_out, tile=1024, received=swap(a3, 1)
+    )
     hidden_in, m0 = sum_norm(embedded, (a0, swap(a1, 1), swap(passed, 2)), gain2, shift2)
 
     m2 = swap(m0, 2)

time: 592 us -> 590 us (level)
  transfers between devices with their start and end apart: 54 -> 54, of which waited for: 22 -> 22; matrix products, arithmetic and copies ran while one was open for 4% -> 4% of each run, Pallas kernels for 49% -> 48%
where the time goes in v4:
time: 590 us; the launch traced here: 582 us
  Pallas kernels  311 us (53%)
  waiting for transfers between devices  153 us (26%)
  starting transfers between devices  61.5 us (10%)
  local copies, waits for them, and re-layouts  30.4 us (5%)
  matrix products  13.3 us (2%)
  other arithmetic  10.9 us (2%)
    pallas_call x36, Pallas kernels, call(): return made(*arrays, *after)  222 us
    ppermute x49, waiting for transfers between devices, swap(): return lax.ppermute(x, axis, [(i, i ^ flip) for i in range(size)])  134 us
    pallas_call x12, Pallas kernels, call(): pl.pallas_call(wrapped, grid_spec=spec, **keys)(prefetch, *arrays, *after)  89.5 us
    ppermute x49, starting transfers between devices, swap(): return lax.ppermute(x, axis, [(i, i ^ flip) for i in range(size)])  36.1 us
    all_to_all x5, starting transfers between devices, exchange(): return lax.all_to_all(x, 'seq', split_axis=0, concat_axis=0, tiled=True)  25.4 us
    unnamed x112, local copies, waits for them, and re-layouts  25.2 us
    all_to_all x5, waiting for transfers between devices, exchange(): return lax.all_to_all(x, 'seq', split_axis=0, concat_axis=0, tiled=True)  18.8 us
  transfers between devices with their start and end apart: 54, of which 22 were waited for; matrix products, arithmetic and copies ran while one was open for 4% of the time, Pallas kernels for 48%

profile of v4, /device:TPU:0, one launch (start us, length us, event | category | flops | bytes accessed | tf_op | source)
XLA Modules:
  0.0 581.7 jit_solution(6958529818540930917)
XLA Ops:
  8.8 7.3 %all-to-all-start = ((bf16[8,32,2048]{2,1,0:T(8,128)(2,1)}), bf16[8,32,2048]{2,1,0:T(8,128)(2,1)S(1)}, u32[]{:S(2)}, u32[]{:S(2)}) async-start(bf16[8,32,2048]{2,1,0:T(8,128)(2,1)} %bitcast.1), calls=%async_computation | async-start | bytes 2097152 | tf_op jit(solution)/shard_map/all_to_all | solution.py:585
  23.1 18.8 %all-to-all-done = bf16[8,32,2048]{2,1,0:T(8,128)(2,1)S(1)} async-done(((bf16[8,32,2048]{2,1,0:T(8,128)(2,1)}), bf16[8,32,2048]{2,1,0:T(8,128)(2,1)S(1)}, u32[]{:S(2)}, u32[]{:S(2)}) %all-to-all-start) | async-done | bytes 1048608 | tf_op jit(solution)/shard_map/all_to_all | solution.py:585
  56.3 7.4 %shard_map.367.refs_1_.refs_0_.refs_2_ = bf16[3,512,512]{2,1,0:T(8,128)(2,1)} custom-call(bf16[256,2048]{1,0:T(8,128)(2,1)} %shard_map.366.refs_0_.refs_1_, bf16[256,2048]{1,0:T(8,128)(2,1)} %copy-done.1, bf16[3,2048,512]{2,1,0:T(8,128)(2,1)} %bitcast.35), custom_call_target="tpu_custom_call" | custom-call | tf_op jit(solution)/shard_map/pallas_call | solution.py:44
  63.7 7.6 %collective-permute-done.1.refs_0_ = bf16[256,2048]{1,0:T(8,128)(2,1)S(1)} collective-permute-done((bf16[256,2048]{1,0:T(8,128)(2,1)}, bf16[256,2048]{1,0:T(8,128)(2,1)S(1)}, u32[]{:S(2)}, u32[]{:S(2)}) %collective-permute-start.1) | collective-permute-done | bytes 1048608 | tf_op jit(solution)/shard_map/ppermute | solution.py:582
  78.0 7.4 %shard_map.369.refs_1_.refs_3_ = bf16[3,512,512]{2,1,0:T(8,128)(2,1)} custom-call(bf16[256,2048]{1,0:T(8,128)(2,1)} %shard_map.368.refs_0_.refs_3_, bf16[256,2048]{1,0:T(8,128)(2,1)} %copy-done.2, bf16[3,2048,512]{2,1,0:T(8,128)(2,1)} %bitcast.36), custom_call_target="tpu_custom_call" | custom-call | tf_op jit(solution)/shard_map/pallas_call | solution.py:44
  85.4 6.8 %shard_map.370.refs_0_.refs_1_ = bf16[512,512]{1,0:T(8,128)(2,1)} custom-call(bf16[3,512,512]{2,1,0:T(8,128)(2,1)} %shard_map.367.refs_1_.refs_0_.refs_2_, bf16[3,512,512]{2,1,0:T(8,128)(2,1)} %shard_map.369.refs_1_.refs_3_, bf16[3,512,512]{2,1,0:T(8,128)(2,1)} %shard_map.367.refs_1_.refs_0_.refs_2_, bf16[3,512,512]{2,1,0:T(8,128)(2,1)} %shard_map.369.refs_1_.refs_3_, ...), custom_call_target="tpu_custom_call" | custom-call | tf_op jit(solution)/shard_map/pallas_call | solution.py:44
  97.0 6.9 %shard_map.372.refs_0_.refs_1_ = bf16[512,512]{1,0:T(8,128)(2,1)} custom-call(bf16[3,512,512]{2,1,0:T(8,128)(2,1)} %shard_map.367.refs_1_.refs_0_.refs_2_, bf16[3,512,512]{2,1,0:T(8,128)(2,1)} %shard_map.369.refs_1_.refs_3_, bf16[3,512,512]{2,1,0:T(8,128)(2,1)} %shard_map.367.refs_1_.refs_0_.refs_2_, bf16[3,512,512]{2,1,0:T(8,128)(2,1)} %shard_map.369.refs_1_.refs_3_, ...), custom_call_target="tpu_custom_call" | custom-call | tf_op jit(solution)/shard_map/pallas_call | solution.py:44
  112.4 22.3 %collective-permute-done.5.refs_3_ = bf16[256,2048]{1,0:T(8,128)(2,1)} collective-permute-done((bf16[256,2048]{1,0:T(8,128)(2,1)}, bf16[256,2048]{1,0:T(8,128)(2,1)}, u32[]{:S(2)}, u32[]{:S(2)}) %collective-permute-start.5) | collective-permute-done | bytes 1048608 | tf_op jit(solution)/shard_map/ppermute | solution.py:582
  142.4 14.9 %shard_map.375 = (bf16[512,2048]{1,0:T(8,128)(2,1)}, bf16[512,2048]{1,0:T(8,128)(2,1)}) custom-call(bf16[256,2048]{1,0:T(8,128)(2,1)} %get-tuple-element.72.refs_0_.refs_1_, bf16[256,2048]{1,0:T(8,128)(2,1)} %copy-done.8, bf16[256,2048]{1,0:T(8,128)(2,1)} %bitcast.48, bf16[256,2048]{1,0:T(8,128)(2,1)} %copy-done.9, bf16[2048,2048]{1,0:T(8,128)(2,1)} %refs_2_.11, ...), custom_call_target="tpu_custom_call" | custom-call | tf_op jit(solution)/shard_map/pallas_call | solution.py:44
  157.3 7.1 %collective-permute-done.8.refs_0_ = bf16[256,2048]{1,0:T(8,128)(2,1)S(1)} collective-permute-done((bf16[256,2048]{1,0:T(8,128)(2,1)}, bf16[256,2048]{1,0:T(8,128)(2,1)S(1)}, u32[]{:S(2)}, u32[]{:S(2)}) %collective-permute-start.8) | collective-permute-done | bytes 1048608 | tf_op jit(solution)/shard_map/ppermute | solution.py:582
  169.2 14.8 %shard_map.377 = (bf16[512,2048]{1,0:T(8,128)(2,1)}, bf16[512,2048]{1,0:T(8,128)(2,1)}) custom-call(bf16[256,2048]{1,0:T(8,128)(2,1)} %shard_map.376.refs_0_.refs_3_, bf16[256,2048]{1,0:T(8,128)(2,1)} %copy-done.10, bf16[256,2048]{1,0:T(8,128)(2,1)} %bitcast.56, bf16[256,2048]{1,0:T(8,128)(2,1)} %collective-permute-done.10.refs_3_.refs_4_, ...), custom_call_target="tpu_custom_call" | custom-call | tf_op jit(solution)/shard_map/pallas_call | solution.py:44
  184.0 9.7 %shard_map.378.refs_7_ = bf16[4,256,2048]{2,1,0:T(8,128)(2,1)} custom-call(s32[4]{0:T(128)} %get-tuple-element.145.refs_0_, bf16[256,2048]{1,0:T(8,128)(2,1)} %bitcast.49, bf16[256,2048]{1,0:T(8,128)(2,1)} %copy-done.9, bf16[256,2048]{1,0:T(8,128)(2,1)} %bitcast.57, bf16[256,2048]{1,0:T(8,128)(2,1)} %collective-permute-done.10.refs_3_.refs_4_, ...), custom_call_target="tpu_custom_call" | custom-call | tf_op jit(solution)/shard_map/pallas_call | solution.py:48
  195.6 9.8 %shard_map.379.refs_3_ = bf16[4,256,2048]{2,1,0:T(8,128)(2,1)} custom-call(s32[4]{0:T(128)} %get-tuple-element.147.refs_0_, bf16[256,2048]{1,0:T(8,128)(2,1)} %get-tuple-element.72.refs_0_.refs_1_, bf16[256,2048]{1,0:T(8,128)(2,1)} %copy-done.8, bf16[256,2048]{1,0:T(8,128)(2,1)} %shard_map.376.refs_0_.refs_3_, bf16[256,2048]{1,0:T(8,128)(2,1)} %copy-done.10, ...), custom_call_target="tpu_custom_call" | custom-call | tf_op jit(solution)/shard_map/pallas_call | solution.py:48
  205.4 8.8 %shard_map.380 = (bf16[256,2048]{1,0:T(8,128)(2,1)}, bf16[256,2048]{1,0:T(8,128)(2,1)}) custom-call(bf16[512,2048]{1,0:T(8,128)(2,1)} %get-tuple-element.75.refs_0_, bf16[512,2048]{1,0:T(8,128)(2,1)} %get-tuple-element.76.refs_1_, bf16[2048,2048]{1,0:T(8,128)(2,1)} %refs_2_.11, bf16[4,256,2048]{2,1,0:T(8,128)(2,1)} %shard_map.379.refs_3_), custom_call_target="tpu_custom_call" | custom-call | tf_op jit(solution)/shard_map/pallas_call | solution.py:44
  218.1 8.9 %shard_map.381 = (bf16[256,2048]{1,0:T(8,128)(2,1)}, bf16[256,2048]{1,0:T(8,128)(2,1)}) custom-call(bf16[512,2048]{1,0:T(8,128)(2,1)} %get-tuple-element.75.refs_0_, bf16[512,2048]{1,0:T(8,128)(2,1)} %get-tuple-element.76.refs_1_, bf16[2048,2048]{1,0:T(8,128)(2,1)} %refs_2_.11, bf16[256,2048]{1,0:T(8,128)(2,1)} %copy-done.21, ...), custom_call_target="tpu_custom_call" | custom-call | tf_op jit(solution)/shard_map/pallas_call | solution.py:44
  228.4 8.7 %shard_map.382 = (bf16[256,2048]{1,0:T(8,128)(2,1)}, bf16[256,2048]{1,0:T(8,128)(2,1)}) custom-call(bf16[512,2048]{1,0:T(8,128)(2,1)} %get-tuple-element.73.refs_1_.refs_0_, bf16[512,2048]{1,0:T(8,128)(2,1)} %get-tuple-element.74.refs_1_, bf16[2048,2048]{1,0:T(8,128)(2,1)} %refs_2_.14, bf16[256,2048]{1,0:T(8,128)(2,1)} %get-tuple-element.79.refs_3_), custom_call_target="tpu_custom_call" | custom-call | tf_op jit(solution)/shard_map/pallas_call | solution.py:44
  237.2 15.2 %collective-permute-done.14.refs_4_ = bf16[256,2048]{1,0:T(8,128)(2,1)S(1)} collective-permute-done((bf16[256,2048]{1,0:T(8,128)(2,1)}, bf16[256,2048]{1,0:T(8,128)(2,1)S(1)}, u32[]{:S(2)}, u32[]{:S(2)}) %collective-permute-start.14) | collective-permute-done | bytes 1048608 | tf_op jit(solution)/shard_map/ppermute | solution.py:582
  268.6 8.8 %shard_map.385 = (bf16[256,2048]{1,0:T(8,128)(2,1)}, bf16[256,2048]{1,0:T(8,128)(2,1)}) custom-call(bf16[512,2048]{1,0:T(8,128)(2,1)} %get-tuple-element.73.refs_1_.refs_0_, bf16[512,2048]{1,0:T(8,128)(2,1)} %get-tuple-element.74.refs_1_, bf16[2048,2048]{1,0:T(8,128)(2,1)} %refs_2_.14, bf16[256,2048]{1,0:T(8,128)(2,1)} %copy-done.37, ...), custom_call_target="tpu_custom_call" | custom-call | tf_op jit(solution)/shard_map/pallas_call | solution.py:44
  277.5 7.4 %collective-permute-done.19.refs_0_ = bf16[256,2048]{1,0:T(8,128)(2,1)S(1)} collective-permute-done((bf16[256,2048]{1,0:T(8,128)(2,1)}, bf16[256,2048]{1,0:T(8,128)(2,1)S(1)}, u32[]{:S(2)}, u32[]{:S(2)}) %collective-permute-start.19) | collective-permute-done | bytes 1048608 | tf_op jit(solution)/shard_map/ppermute | solution.py:582
  286.6 11.2 %shard_map.387 = (bf16[2,256,2048]{2,1,0:T(8,128)(2,1)}, bf16[2,256,2048]{2,1,0:T(8,128)(2,1)}) custom-call(s32[4]{0:T(128)} %get-tuple-element.144.refs_0_, bf16[256,2048]{1,0:T(8,128)(2,1)} %bitcast.51, bf16[256,2048]{1,0:T(8,128)(2,1)} %copy-done.9, bf16[256,2048]{1,0:T(8,128)(2,1)} %bitcast.58, ...), custom_call_target="tpu_custom_call" | custom-call | tf_op jit(solution)/shard_map/pallas_call | solution.py:48
  311.8 11.1 %shard_map.390 = (bf16[2,256,2048]{2,1,0:T(8,128)(2,1)}, bf16[2,256,2048]{2,1,0:T(8,128)(2,1)}) custom-call(s32[4]{0:T(128)} %get-tuple-element.146.refs_0_, bf16[256,2048]{1,0:T(8,128)(2,1)} %get-tuple-element.72.refs_0_.refs_1_, bf16[256,2048]{1,0:T(8,128)(2,1)} %copy-done.8, bf16[256,2048]{1,0:T(8,128)(2,1)} %shard_map.376.refs_0_.refs_3_, ...), custom_call_target="tpu_custom_call" | custom-call | tf_op jit(solution)/shard_map/pallas_call | solution.py:48
  334.3 23.6 %shard_map.392.refs_2_.refs_0_.refs_1_.refs_5_ = bf16[3,1024,512]{2,1,0:T(8,128)(2,1)} custom-call(bf16[3,512,512]{2,1,0:T(8,128)(2,1)} %shard_map.367.refs_1_.refs_0_.refs_2_, bf16[3,512,512]{2,1,0:T(8,128)(2,1)} %shard_map.369.refs_1_.refs_3_, bf16[256,512]{1,0:T(8,128)(2,1)} %get-tuple-element.90.refs_2_, ...), custom_call_target="tpu_custom_call" | custom-call | tf_op jit(solution)/shard_map/pallas_call | solution.py:44
  368.1 7.4 %shard_map.394 = (bf16[256,2048]{1,0:T(8,128)(2,1)}, bf16[256,2048]{1,0:T(8,128)(2,1)}) custom-call(bf16[3,1024,512]{2,1,0:T(8,128)(2,1)} %shard_map.392.refs_2_.refs_0_.refs_1_.refs_5_, bf16[3,1024,512]{2,1,0:T(8,128)(2,1)} %shard_map.392.refs_2_.refs_0_.refs_1_.refs_5_, bf16[3,2048,512]{2,1,0:T(8,128)(2,1)} %bitcast.37, ...), custom_call_target="tpu_custom_call" | custom-call | tf_op jit(solution)/shard_map/pallas_call | solution.py:44
  383.1 7.6 %shard_map.396 = (bf16[256,2048]{1,0:T(8,128)(2,1)}, bf16[256,2048]{1,0:T(8,128)(2,1)}) custom-call(bf16[3,1024,512]{2,1,0:T(8,128)(2,1)} %shard_map.392.refs_2_.refs_0_.refs_1_.refs_5_, bf16[3,1024,512]{2,1,0:T(8,128)(2,1)} %shard_map.392.refs_2_.refs_0_.refs_1_.refs_5_, bf16[3,2048,512]{2,1,0:T(8,128)(2,1)} %bitcast.38, ...), custom_call_target="tpu_custom_call" | custom-call | tf_op jit(solution)/shard_map/pallas_call | solution.py:44
  405.4 9.1 %collective-permute-done.30.refs_7_.refs_6_ = bf16[4,256,512]{2,1,0:T(8,128)(2,1)} collective-permute-done((bf16[4,256,512]{2,1,0:T(8,128)(2,1)}, bf16[4,256,512]{2,1,0:T(8,128)(2,1)}, u32[]{:S(2)}, u32[]{:S(2)}) %collective-permute-start.30) | collective-permute-done | bytes 1048608 | tf_op jit(solution)/shard_map/ppermute | solution.py:582
  451.9 8.0 %collective-permute-done.31.refs_1_ = bf16[2,256,512]{2,1,0:T(8,128)(2,1)} collective-permute-done((bf16[2,256,512]{2,1,0:T(8,128)(2,1)}, bf16[2,256,512]{2,1,0:T(8,128)(2,1)}, u32[]{:S(2)}, u32[]{:S(2)}) %collective-permute-start.31) | collective-permute-done | bytes 524320 | tf_op jit(solution)/shard_map/ppermute | solution.py:582
  478.3 13.1 %collective-permute-done.37.refs_3_.refs_6_ = bf16[4,256,512]{2,1,0:T(8,128)(2,1)} collective-permute-done((bf16[4,256,512]{2,1,0:T(8,128)(2,1)S(1)}, bf16[4,256,512]{2,1,0:T(8,128)(2,1)}, u32[]{:S(2)}, u32[]{:S(2)}) %collective-permute-start.37) | collective-permute-done | bytes 1048608 | tf_op jit(solution)/shard_map/ppermute | solution.py:582
  493.5 6.2 %shard_map.407 = (bf16[2,256,512]{2,1,0:T(8,128)(2,1)}, bf16[2,256,512]{2,1,0:T(8,128)(2,1)}) custom-call(s32[4]{0:T(128)} %get-tuple-element.144.refs_0_, bf16[256,2048]{1,0:T(8,128)(2,1)} %shard_map.366.refs_0_.refs_1_, bf16[256,2048]{1,0:T(8,128)(2,1)} %copy-done.1, bf16[256,2048]{1,0:T(8,128)(2,1)} %shard_map.368.refs_0_.refs_3_, ...), custom_call_target="tpu_custom_call" | custom-call | tf_op jit(solution)/shard_map/pallas_call | solution.py:48
  503.7 14.5 %collective-permute-done.36.refs_1_ = bf16[2,256,512]{2,1,0:T(8,128)(2,1)S(1)} collective-permute-done((bf16[2,256,512]{2,1,0:T(8,128)(2,1)}, bf16[2,256,512]{2,1,0:T(8,128)(2,1)S(1)}, u32[]{:S(2)}, u32[]{:S(2)}) %collective-permute-start.36) | collective-permute-done | bytes 524320 | tf_op jit(solution)/shard_map/ppermute | solution.py:582
  521.1 8.2 %collective-permute-done.41.refs_4_.refs_1_ = bf16[2,256,512]{2,1,0:T(8,128)(2,1)S(1)} collective-permute-done((bf16[2,256,512]{2,1,0:T(8,128)(2,1)}, bf16[2,256,512]{2,1,0:T(8,128)(2,1)S(1)}, u32[]{:S(2)}, u32[]{:S(2)}) %collective-permute-start.41) | collective-permute-done | bytes 524320 | tf_op jit(solution)/shard_map/ppermute | solution.py:582
  543.2 6.7 %shard_map.411.refs_3_ = bf16[1024,2048]{1,0:T(8,128)(2,1)} custom-call(s32[1,512]{1,0:T(1,128)} %broadcast_in_dim.129.refs_0_, bf16[256,2048]{1,0:T(8,128)(2,1)} %shard_map.409.refs_2_.refs_1_, bf16[256,2048]{1,0:T(8,128)(2,1)} %collective-permute-done.42.refs_2_, bf16[1024,2048]{1,0:T(8,128)(2,1)} %shard_map.403.refs_2_.refs_3_, ...), custom_call_target="tpu_custom_call" | custom-call | tf_op jit(solution)/shard_map/pallas_call | solution.py:44
  569.4 6.7 %shard_map.416.refs_2_ = bf16[1024,2048]{1,0:T(8,128)(2,1)} custom-call(s32[1,512]{1,0:T(1,128)} %broadcast_in_dim.129.refs_0_, bf16[256,2048]{1,0:T(8,128)(2,1)} %shard_map.414.refs_2_.refs_1_, bf16[256,2048]{1,0:T(8,128)(2,1)} %copy-done.36, bf16[1024,2048]{1,0:T(8,128)(2,1)} %shard_map.412.refs_2_.refs_3_, f32[256,2048]{1,0:T(8,128)} %shard_map.415.refs_4_), custom_call_target="tpu_custom_call" | custom-call | tf_op jit(solution)/shard_map/pallas_call | solution.py:44
  (279 shorter events, 248.3 us)
Async XLA Ops:
  8.8 33.1 %all-to-all-start = ((bf16[8,32,2048]{2,1,0:T(8,128)(2,1)}), bf16[8,32,2048]{2,1,0:T(8,128)(2,1)S(1)}, u32[]{:S(2)}, u32[]{:S(2)}) async-start(bf16[8,32,2048]{2,1,0:T(8,128)(2,1)} %bitcast.1), calls=%async_computation | async-start | bytes 2097152 | tf_op jit(solution)/shard_map/all_to_all | solution.py:585
  45.5 25.8 %collective-permute-start.1 = (bf16[256,2048]{1,0:T(8,128)(2,1)}, bf16[256,2048]{1,0:T(8,128)(2,1)S(1)}, u32[]{:S(2)}, u32[]{:S(2)}) collective-permute-start(bf16[256,2048]{1,0:T(8,128)(2,1)} %shard_map.366.refs_0_.refs_1_), channel_id=1, source_target_pairs={{0,2},{1,3},{2,0},{3,1},{4,6},{5,7},{6,4},{7,5},{8,10},{9,11},{10,... | collective-permute-start | bytes 3145736 | tf_op jit(solution)/shard_map/ppermute | solution.py:582
  50.1 60.2 %all-to-all-start.1 = ((bf16[8,64,2048]{2,1,0:T(8,128)(2,1)}), bf16[8,64,2048]{2,1,0:T(8,128)(2,1)}, u32[]{:S(2)}, u32[]{:S(2)}) async-start(bf16[8,64,2048]{2,1,0:T(8,128)(2,1)} %pad_maximum_fusion), calls=%async_computation.1 | async-start | bytes 4194304 | tf_op jit(solution)/shard_map/all_to_all | solution.py:585
  108.8 25.9 %collective-permute-start.5 = (bf16[256,2048]{1,0:T(8,128)(2,1)}, bf16[256,2048]{1,0:T(8,128)(2,1)}, u32[]{:S(2)}, u32[]{:S(2)}) collective-permute-start(bf16[256,2048]{1,0:T(8,128)(2,1)} %get-tuple-element.70), channel_id=1, source_target_pairs={{0,2},{1,3},{2,0},{3,1},{4,6},{5,7},{6,4},{7,5},{8,10},{9,11},{10,... | collective-permute-start | bytes 3145736 | tf_op jit(solution)/shard_map/ppermute | solution.py:582
  112.1 28.2 %collective-permute-start.7 = (bf16[256,2048]{1,0:T(8,128)(2,1)S(1)}, bf16[256,2048]{1,0:T(8,128)(2,1)S(1)}, u32[]{:S(2)}, u32[]{:S(2)}) collective-permute-start(bf16[256,2048]{1,0:T(8,128)(2,1)S(1)} %bitcast.47), channel_id=1, source_target_pairs={{0,1},{1,0},{2,3},{3,2},{4,5},{5,4},{6,7},{7,6},{8,9},{9,8},{10,11... | collective-permute-start | bytes 3145736 | tf_op jit(solution)/shard_map/ppermute | solution.py:582
  138.6 25.8 %collective-permute-start.8 = (bf16[256,2048]{1,0:T(8,128)(2,1)}, bf16[256,2048]{1,0:T(8,128)(2,1)S(1)}, u32[]{:S(2)}, u32[]{:S(2)}) collective-permute-start(bf16[256,2048]{1,0:T(8,128)(2,1)} %get-tuple-element.72.refs_0_.refs_1_), channel_id=1, source_target_pairs={{0,2},{1,3},{2,0},{3,1},{4,6},{5,7},{6,4},{7,5},{8,10},{9,11},{10,... | collective-permute-start | bytes 3145736 | tf_op jit(solution)/shard_map/ppermute | solution.py:582
  140.1 25.7 %collective-permute-start.10 = (bf16[256,2048]{1,0:T(8,128)(2,1)S(1)}, bf16[256,2048]{1,0:T(8,128)(2,1)}, u32[]{:S(2)}, u32[]{:S(2)}) collective-permute-start(bf16[256,2048]{1,0:T(8,128)(2,1)S(1)} %bitcast.55), channel_id=1, source_target_pairs={{0,1},{1,0},{2,3},{3,2},{4,5},{5,4},{6,7},{7,6},{8,9},{9,8},{10,11... | collective-permute-start | bytes 3145736 | tf_op jit(solution)/shard_map/ppermute | solution.py:582
  193.7 92.9 %collective-permute-start.21 = (bf16[4,256,2048]{2,1,0:T(8,128)(2,1)}, bf16[4,256,2048]{2,1,0:T(8,128)(2,1)}, u32[]{:S(2)}, u32[]{:S(2)}) collective-permute-start(bf16[4,256,2048]{2,1,0:T(8,128)(2,1)} %shard_map.378.refs_7_), channel_id=1, source_target_pairs={{0,4},{4,0},{8,12},{12,8},{16,20},{20,16},{24,28},{28,24},{1,5},{5... | collective-permute-start | bytes 12582920 | tf_op jit(solution)/shard_map/ppermute | solution.py:582
  214.2 97.6 %collective-permute-start.18 = (bf16[4,256,2048]{2,1,0:T(8,128)(2,1)}, bf16[4,256,2048]{2,1,0:T(8,128)(2,1)}, u32[]{:S(2)}, u32[]{:S(2)}) collective-permute-start(bf16[4,256,2048]{2,1,0:T(8,128)(2,1)} %shard_map.379.refs_3_), channel_id=1, source_target_pairs={{0,8},{4,12},{8,0},{12,4},{16,24},{20,28},{24,16},{28,20},{1,9},{5... | collective-permute-start | bytes 12582920 | tf_op jit(solution)/shard_map/ppermute | solution.py:582
  226.9 25.4 %collective-permute-start.14 = (bf16[256,2048]{1,0:T(8,128)(2,1)}, bf16[256,2048]{1,0:T(8,128)(2,1)S(1)}, u32[]{:S(2)}, u32[]{:S(2)}) collective-permute-start(bf16[256,2048]{1,0:T(8,128)(2,1)} %get-tuple-element.79.refs_3_), channel_id=1, source_target_pairs={{0,2},{1,3},{2,0},{3,1},{4,6},{5,7},{6,4},{7,5},{8,10},{9,11},{10,... | collective-permute-start | bytes 3145736 | tf_op jit(solution)/shard_map/ppermute | solution.py:582
  259.5 25.4 %collective-permute-start.19 = (bf16[256,2048]{1,0:T(8,128)(2,1)}, bf16[256,2048]{1,0:T(8,128)(2,1)S(1)}, u32[]{:S(2)}, u32[]{:S(2)}) collective-permute-start(bf16[256,2048]{1,0:T(8,128)(2,1)} %get-tuple-element.83.refs_0_.refs_3_), channel_id=1, source_target_pairs={{0,2},{1,3},{2,0},{3,1},{4,6},{5,7},{6,4},{7,5},{8,10},{9,11},{10,... | collective-permute-start | bytes 3145736 | tf_op jit(solution)/shard_map/ppermute | solution.py:582
  297.8 66.2 %collective-permute-start.23 = (bf16[2,256,2048]{2,1,0:T(8,128)(2,1)}, bf16[2,256,2048]{2,1,0:T(8,128)(2,1)}, u32[]{:S(2)}, u32[]{:S(2)}) collective-permute-start(bf16[2,256,2048]{2,1,0:T(8,128)(2,1)} %get-tuple-element.92), channel_id=1, source_target_pairs={{0,8},{4,12},{8,0},{12,4},{16,24},{20,28},{24,16},{28,20},{1,9},{5... | collective-permute-start | bytes 6291464 | tf_op jit(solution)/shard_map/ppermute | solution.py:582
  297.9 25.6 %collective-permute-start.17 = (bf16[256,2048]{1,0:T(8,128)(2,1)S(1)}, bf16[256,2048]{1,0:T(8,128)(2,1)S(1)}, u32[]{:S(2)}, u32[]{:S(2)}) collective-permute-start(bf16[256,2048]{1,0:T(8,128)(2,1)S(1)} %copy-done.23), channel_id=1, source_target_pairs={{0,2},{1,3},{2,0},{3,1},{4,6},{5,7},{6,4},{7,5},{8,10},{9,11},{10,... | collective-permute-start | bytes 3145736 | tf_op jit(solution)/shard_map/ppermute | solution.py:582
  310.4 57.8 %collective-permute-start.24 = (bf16[4,256,512]{2,1,0:T(8,128)(2,1)}, bf16[4,256,512]{2,1,0:T(8,128)(2,1)}, u32[]{:S(2)}, u32[]{:S(2)}) collective-permute-start(bf16[4,256,512]{2,1,0:T(8,128)(2,1)} %shard_map.389.refs_8_), channel_id=1, source_target_pairs={{0,4},{4,0},{8,12},{12,8},{16,20},{20,16},{24,28},{28,24},{1,5},{5... | collective-permute-start | bytes 3145736 | tf_op jit(solution)/shard_map/ppermute | solution.py:582
  328.0 54.1 %all-to-all-start.2 = ((bf16[8,32,2048]{2,1,0:T(8,128)(2,1)}), bf16[8,32,2048]{2,1,0:T(8,128)(2,1)S(1)}, u32[]{:S(2)}, u32[]{:S(2)}) async-start(bf16[8,32,2048]{2,1,0:T(8,128)(2,1)} %bitcast.63), calls=%async_computation.2 | async-start | bytes 2097152 | tf_op jit(solution)/shard_map/all_to_all | solution.py:585
  332.3 60.5 %collective-permute-start.26 = (bf16[2,256,2048]{2,1,0:T(8,128)(2,1)}, bf16[2,256,2048]{2,1,0:T(8,128)(2,1)S(1)}, u32[]{:S(2)}, u32[]{:S(2)}) collective-permute-start(bf16[2,256,2048]{2,1,0:T(8,128)(2,1)} %get-tuple-element.97), channel_id=1, source_target_pairs={{0,4},{4,0},{8,12},{12,8},{16,20},{20,16},{24,28},{28,24},{1,5},{5... | collective-permute-start | bytes 6291464 | tf_op jit(solution)/shard_map/ppermute | solution.py:582
  375.5 39.0 %collective-permute-start.28 = (bf16[256,2048]{1,0:T(8,128)(2,1)}, bf16[256,2048]{1,0:T(8,128)(2,1)}, u32[]{:S(2)}, u32[]{:S(2)}) collective-permute-start(bf16[256,2048]{1,0:T(8,128)(2,1)} %get-tuple-element.95.refs_6_), channel_id=1, source_target_pairs={{0,1},{1,0},{2,3},{3,2},{4,5},{5,4},{6,7},{7,6},{8,9},{9,8},{10,11... | collective-permute-start | bytes 3145736 | tf_op jit(solution)/shard_map/ppermute | solution.py:582
  382.1 32.4 %collective-permute-start.30 = (bf16[4,256,512]{2,1,0:T(8,128)(2,1)}, bf16[4,256,512]{2,1,0:T(8,128)(2,1)}, u32[]{:S(2)}, u32[]{:S(2)}) collective-permute-start(bf16[4,256,512]{2,1,0:T(8,128)(2,1)} %shard_map.395.refs_4_), channel_id=1, source_target_pairs={{0,4},{4,0},{8,12},{12,8},{16,20},{20,16},{24,28},{28,24},{1,5},{5... | collective-permute-start | bytes 3145736 | tf_op jit(solution)/shard_map/ppermute | solution.py:582
  392.2 47.4 %collective-permute-start.33 = (bf16[1,256,2048]{2,1,0:T(8,128)(2,1)}, bf16[1,256,2048]{2,1,0:T(8,128)(2,1)S(1)}, u32[]{:S(2)}, u32[]{:S(2)}) collective-permute-start(bf16[1,256,2048]{2,1,0:T(8,128)(2,1)} %get-tuple-element.103), channel_id=1, source_target_pairs={{0,16},{4,20},{8,24},{12,28},{16,0},{20,4},{24,8},{28,12},{1,17},{... | collective-permute-start | bytes 3145736 | tf_op jit(solution)/shard_map/ppermute | solution.py:582
  392.8 58.0 %collective-permute-start.32 = (bf16[256,2048]{1,0:T(8,128)(2,1)}, bf16[256,2048]{1,0:T(8,128)(2,1)}, u32[]{:S(2)}, u32[]{:S(2)}) collective-permute-start(bf16[256,2048]{1,0:T(8,128)(2,1)} %bitcast.65), channel_id=1, source_target_pairs={{0,1},{1,0},{2,3},{3,2},{4,5},{5,4},{6,7},{7,6},{8,9},{9,8},{10,11... | collective-permute-start | bytes 3145736 | tf_op jit(solution)/shard_map/ppermute | solution.py:582
  428.2 31.7 %collective-permute-start.31 = (bf16[2,256,512]{2,1,0:T(8,128)(2,1)}, bf16[2,256,512]{2,1,0:T(8,128)(2,1)}, u32[]{:S(2)}, u32[]{:S(2)}) collective-permute-start(bf16[2,256,512]{2,1,0:T(8,128)(2,1)} %get-tuple-element.102), channel_id=1, source_target_pairs={{0,8},{4,12},{8,0},{12,4},{16,24},{20,28},{24,16},{28,20},{1,9},{5... | collective-permute-start | bytes 1572872 | tf_op jit(solution)/shard_map/ppermute | solution.py:582
  428.7 101.4 %all-to-all-start.3 = ((bf16[8,32,2048]{2,1,0:T(8,128)(2,1)}), bf16[8,32,2048]{2,1,0:T(8,128)(2,1)}, u32[]{:S(2)}, u32[]{:S(2)}) async-start(bf16[8,32,2048]{2,1,0:T(8,128)(2,1)} %bitcast.21), calls=%async_computation.3 | async-start | bytes 2097152 | tf_op jit(solution)/shard_map/all_to_all | solution.py:585
  433.1 36.3 %collective-permute-start.27 = (bf16[4,256,512]{2,1,0:T(8,128)(2,1)}, bf16[4,256,512]{2,1,0:T(8,128)(2,1)}, u32[]{:S(2)}, u32[]{:S(2)}) collective-permute-start(bf16[4,256,512]{2,1,0:T(8,128)(2,1)} %shard_map.397.refs_6_), channel_id=1, source_target_pairs={{0,4},{4,0},{8,12},{12,8},{16,20},{20,16},{24,28},{28,24},{1,5},{5... | collective-permute-start | bytes 3145736 | tf_op jit(solution)/shard_map/ppermute | solution.py:582
  435.1 56.4 %collective-permute-start.37 = (bf16[4,256,512]{2,1,0:T(8,128)(2,1)S(1)}, bf16[4,256,512]{2,1,0:T(8,128)(2,1)}, u32[]{:S(2)}, u32[]{:S(2)}) collective-permute-start(bf16[4,256,512]{2,1,0:T(8,128)(2,1)S(1)} %copy-done.18), channel_id=1, source_target_pairs={{0,4},{4,0},{8,12},{12,8},{16,20},{20,16},{24,28},{28,24},{1,5},{5... | collective-permute-start | bytes 3145736 | tf_op jit(solution)/shard_map/ppermute | solution.py:582
  450.8 70.3 %collective-permute-start.22 = (bf16[256,2048]{1,0:T(8,128)(2,1)S(1)}, bf16[256,2048]{1,0:T(8,128)(2,1)S(1)}, u32[]{:S(2)}, u32[]{:S(2)}) collective-permute-start(bf16[256,2048]{1,0:T(8,128)(2,1)S(1)} %bitcast.67), channel_id=1, source_target_pairs={{0,2},{1,3},{2,0},{3,1},{4,6},{5,7},{6,4},{7,5},{8,10},{9,11},{10,... | collective-permute-start | bytes 3145736 | tf_op jit(solution)/shard_map/ppermute | solution.py:582
  451.9 39.5 %collective-permute-start.38 = (bf16[2,256,512]{2,1,0:T(8,128)(2,1)}, bf16[2,256,512]{2,1,0:T(8,128)(2,1)}, u32[]{:S(2)}, u32[]{:S(2)}) collective-permute-start(bf16[2,256,512]{2,1,0:T(8,128)(2,1)} %get-tuple-element.113), channel_id=1, source_target_pairs={{0,8},{4,12},{8,0},{12,4},{16,24},{20,28},{24,16},{28,20},{1,9},{5... | collective-permute-start | bytes 1572872 | tf_op jit(solution)/shard_map/ppermute | solution.py:582
  459.8 69.5 %collective-permute-start.39 = (bf16[1,256,2048]{2,1,0:T(8,128)(2,1)}, bf16[1,256,2048]{2,1,0:T(8,128)(2,1)}, u32[]{:S(2)}, u32[]{:S(2)}) collective-permute-start(bf16[1,256,2048]{2,1,0:T(8,128)(2,1)} %get-tuple-element.117), channel_id=1, source_target_pairs={{0,16},{4,20},{8,24},{12,28},{16,0},{20,4},{24,8},{28,12},{1,17},{... | collective-permute-start | bytes 3145736 | tf_op jit(solution)/shard_map/ppermute | solution.py:582
  475.5 42.7 %collective-permute-start.36 = (bf16[2,256,512]{2,1,0:T(8,128)(2,1)}, bf16[2,256,512]{2,1,0:T(8,128)(2,1)S(1)}, u32[]{:S(2)}, u32[]{:S(2)}) collective-permute-start(bf16[2,256,512]{2,1,0:T(8,128)(2,1)} %get-tuple-element.112), channel_id=1, source_target_pairs={{0,8},{4,12},{8,0},{12,4},{16,24},{20,28},{24,16},{28,20},{1,9},{5... | collective-permute-start | bytes 1572872 | tf_op jit(solution)/shard_map/ppermute | solution.py:582
  499.8 29.6 %collective-permute-start.41 = (bf16[2,256,512]{2,1,0:T(8,128)(2,1)}, bf16[2,256,512]{2,1,0:T(8,128)(2,1)S(1)}, u32[]{:S(2)}, u32[]{:S(2)}) collective-permute-start(bf16[2,256,512]{2,1,0:T(8,128)(2,1)} %get-tuple-element.119), channel_id=1, source_target_pairs={{0,8},{4,12},{8,0},{12,4},{16,24},{20,28},{24,16},{28,20},{1,9},{5... | collective-permute-start | bytes 1572872 | tf_op jit(solution)/shard_map/ppermute | solution.py:582
  530.6 31.0 %collective-permute-start.43 = (bf16[256,2048]{1,0:T(8,128)(2,1)}, bf16[256,2048]{1,0:T(8,128)(2,1)S(1)}, u32[]{:S(2)}, u32[]{:S(2)}) collective-permute-start(bf16[256,2048]{1,0:T(8,128)(2,1)} %bitcast.22.refs_1_), channel_id=1, source_target_pairs={{0,2},{1,3},{2,0},{3,1},{4,6},{5,7},{6,4},{7,5},{8,10},{9,11},{10,... | collective-permute-start | bytes 3145736 | tf_op jit(solution)/shard_map/ppermute | solution.py:582
  531.7 27.1 %collective-permute-start.46 = (bf16[1,256,512]{2,1,0:T(8,128)(2,1)S(1)}, bf16[1,256,512]{2,1,0:T(8,128)(2,1)S(1)}, u32[]{:S(2)}, u32[]{:S(2)}) collective-permute-start(bf16[1,256,512]{2,1,0:T(8,128)(2,1)S(1)} %copy-done.54), channel_id=1, source_target_pairs={{0,16},{4,20},{8,24},{12,28},{16,0},{20,4},{24,8},{28,12},{1,17},{... | collective-permute-start | bytes 786440 | tf_op jit(solution)/shard_map/ppermute | solution.py:582
  534.1 27.5 %all-to-all-start.4 = ((f32[8,4,256]{2,1,0:T(4,128)}), f32[8,4,256]{2,1,0:T(4,128)S(1)}, u32[]{:S(2)}, u32[]{:S(2)}) async-start(f32[8,4,256]{2,1,0:T(4,128)} %bitcast.24), calls=%async_computation.4 | async-start | bytes 65536 | tf_op jit(solution)/shard_map/all_to_all | solution.py:585
  (78 other events, 621.0 us)

commit v5 on v4

--- a/solution.py
+++ b/solution.py
@@ -63,9 +63,10 @@
     )(x, *after)
 
 
-def block_matmul(picks, b, transposed=False, tile=512, received=None, after=()):
+def block_matmul(picks, b, transposed=False, tile=1024, received=None, after=()):
     rows, depth = picks[0][0].shape[0] // picks[0][2], picks[0][0].shape[1]
     width = b.shape[0] if transposed else b.shape[1]
+    tile = min(tile, width)
 
     def body(x_ref, y_ref, b_ref, *rest):
         o_ref, p_ref, both = rest[-3:]
@@ -646,10 +647,10 @@
     n3 = swap(n2, 1)
     qkv = (qkv_low, project((n2, n3), w3))
     mixed_out = attend((1, 3), qkv, pos_col, start_col, pos_row)
-    a1, a3 = block_matmul(((mixed_out, 0, 2), (mixed_out, 1, 2)), w_out, tile=1024)
+    a1, a3 = block_matmul(((mixed_out, 0, 2), (mixed_out, 1, 2)), w_out)
     mixed_in = attend((0, 2), qkv, pos_col, start_col, pos_row, after=(a1,))
     a0, passed = block_matmul(
-        ((mixed_in, 0, 2), (mixed_in, 1, 2)), w_out, tile=1024, received=swap(a3, 1)
+        ((mixed_in, 0, 2), (mixed_in, 1, 2)), w_out, received=swap(a3, 1)
     )
     hidden_in, m0 = sum_norm(embedded, (a0, swap(a1, 1), swap(passed, 2)), gain2, shift2)
 

time: 590 us -> 589 us (level)
  no operation moved by 1% of the time
where the time goes in v5:
time: 589 us; the launch traced here: 582 us
  Pallas kernels  311 us (53%)
  waiting for transfers between devices  153 us (26%)
  starting transfers between devices  61.6 us (10%)
  local copies, waits for them, and re-layouts  30.4 us (5%)
  matrix products  13.3 us (2%)
  other arithmetic  10.9 us (2%)
    pallas_call x36, Pallas kernels, call(): return made(*arrays, *after)  221 us
    ppermute x49, waiting for transfers between devices, swap(): return lax.ppermute(x, axis, [(i, i ^ flip) for i in range(size)])  134 us
    pallas_call x12, Pallas kernels, call(): pl.pallas_call(wrapped, grid_spec=spec, **keys)(prefetch, *arrays, *after)  89.6 us
    ppermute x49, starting transfers between devices, swap(): return lax.ppermute(x, axis, [(i, i ^ flip) for i in range(size)])  36.3 us
    all_to_all x5, starting transfers between devices, exchange(): return lax.all_to_all(x, 'seq', split_axis=0, concat_axis=0, tiled=True)  25.3 us
    unnamed x112, local copies, waits for them, and re-layouts  25.2 us
    all_to_all x5, waiting for transfers between devices, exchange(): return lax.all_to_all(x, 'seq', split_axis=0, concat_axis=0, tiled=True)  18.8 us
  transfers between devices with their start and end apart: 54, of which 22 were waited for; matrix products, arithmetic and copies ran while one was open for 4% of the time, Pallas kernels for 48%

profile of v5, /device:TPU:0, one launch (start us, length us, event | category | flops | bytes accessed | tf_op | source)
XLA Modules:
  0.0 581.5 jit_solution(3362674826362178211)
XLA Ops:
  8.8 7.3 %all-to-all-start = ((bf16[8,32,2048]{2,1,0:T(8,128)(2,1)}), bf16[8,32,2048]{2,1,0:T(8,128)(2,1)S(1)}, u32[]{:S(2)}, u32[]{:S(2)}) async-start(bf16[8,32,2048]{2,1,0:T(8,128)(2,1)} %bitcast.1), calls=%async_computation | async-start | bytes 2097152 | tf_op jit(solution)/shard_map/all_to_all | solution.py:586
  23.1 18.8 %all-to-all-done = bf16[8,32,2048]{2,1,0:T(8,128)(2,1)S(1)} async-done(((bf16[8,32,2048]{2,1,0:T(8,128)(2,1)}), bf16[8,32,2048]{2,1,0:T(8,128)(2,1)S(1)}, u32[]{:S(2)}, u32[]{:S(2)}) %all-to-all-start) | async-done | bytes 1048608 | tf_op jit(solution)/shard_map/all_to_all | solution.py:586
  56.2 7.4 %shard_map.367.refs_1_.refs_0_.refs_2_ = bf16[3,512,512]{2,1,0:T(8,128)(2,1)} custom-call(bf16[256,2048]{1,0:T(8,128)(2,1)} %shard_map.366.refs_0_.refs_1_, bf16[256,2048]{1,0:T(8,128)(2,1)} %copy-done.1, bf16[3,2048,512]{2,1,0:T(8,128)(2,1)} %bitcast.35), custom_call_target="tpu_custom_call" | custom-call | tf_op jit(solution)/shard_map/pallas_call | solution.py:44
  63.6 7.8 %collective-permute-done.1.refs_0_ = bf16[256,2048]{1,0:T(8,128)(2,1)S(1)} collective-permute-done((bf16[256,2048]{1,0:T(8,128)(2,1)}, bf16[256,2048]{1,0:T(8,128)(2,1)S(1)}, u32[]{:S(2)}, u32[]{:S(2)}) %collective-permute-start.1) | collective-permute-done | bytes 1048608 | tf_op jit(solution)/shard_map/ppermute | solution.py:583
  78.0 7.4 %shard_map.369.refs_1_.refs_3_ = bf16[3,512,512]{2,1,0:T(8,128)(2,1)} custom-call(bf16[256,2048]{1,0:T(8,128)(2,1)} %shard_map.368.refs_0_.refs_3_, bf16[256,2048]{1,0:T(8,128)(2,1)} %copy-done.2, bf16[3,2048,512]{2,1,0:T(8,128)(2,1)} %bitcast.36), custom_call_target="tpu_custom_call" | custom-call | tf_op jit(solution)/shard_map/pallas_call | solution.py:44
  85.4 6.8 %shard_map.370.refs_0_.refs_1_ = bf16[512,512]{1,0:T(8,128)(2,1)} custom-call(bf16[3,512,512]{2,1,0:T(8,128)(2,1)} %shard_map.367.refs_1_.refs_0_.refs_2_, bf16[3,512,512]{2,1,0:T(8,128)(2,1)} %shard_map.369.refs_1_.refs_3_, bf16[3,512,512]{2,1,0:T(8,128)(2,1)} %shard_map.367.refs_1_.refs_0_.refs_2_, bf16[3,512,512]{2,1,0:T(8,128)(2,1)} %shard_map.369.refs_1_.refs_3_, ...), custom_call_target="tpu_custom_call" | custom-call | tf_op jit(solution)/shard_map/pallas_call | solution.py:44
  96.7 6.9 %shard_map.372.refs_0_.refs_1_ = bf16[512,512]{1,0:T(8,128)(2,1)} custom-call(bf16[3,512,512]{2,1,0:T(8,128)(2,1)} %shard_map.367.refs_1_.refs_0_.refs_2_, bf16[3,512,512]{2,1,0:T(8,128)(2,1)} %shard_map.369.refs_1_.refs_3_, bf16[3,512,512]{2,1,0:T(8,128)(2,1)} %shard_map.367.refs_1_.refs_0_.refs_2_, bf16[3,512,512]{2,1,0:T(8,128)(2,1)} %shard_map.369.refs_1_.refs_3_, ...), custom_call_target="tpu_custom_call" | custom-call | tf_op jit(solution)/shard_map/pallas_call | solution.py:44
  112.1 22.3 %collective-permute-done.5.refs_3_ = bf16[256,2048]{1,0:T(8,128)(2,1)} collective-permute-done((bf16[256,2048]{1,0:T(8,128)(2,1)}, bf16[256,2048]{1,0:T(8,128)(2,1)}, u32[]{:S(2)}, u32[]{:S(2)}) %collective-permute-start.5) | collective-permute-done | bytes 1048608 | tf_op jit(solution)/shard_map/ppermute | solution.py:583
  142.1 14.9 %shard_map.375 = (bf16[512,2048]{1,0:T(8,128)(2,1)}, bf16[512,2048]{1,0:T(8,128)(2,1)}) custom-call(bf16[256,2048]{1,0:T(8,128)(2,1)} %get-tuple-element.72.refs_0_.refs_1_, bf16[256,2048]{1,0:T(8,128)(2,1)} %copy-done.8, bf16[256,2048]{1,0:T(8,128)(2,1)} %bitcast.48, bf16[256,2048]{1,0:T(8,128)(2,1)} %copy-done.9, bf16[2048,2048]{1,0:T(8,128)(2,1)} %refs_2_.11, ...), custom_call_target="tpu_custom_call" | custom-call | tf_op jit(solution)/shard_map/pallas_call | solution.py:44
  157.0 7.1 %collective-permute-done.8.refs_0_ = bf16[256,2048]{1,0:T(8,128)(2,1)S(1)} collective-permute-done((bf16[256,2048]{1,0:T(8,128)(2,1)}, bf16[256,2048]{1,0:T(8,128)(2,1)S(1)}, u32[]{:S(2)}, u32[]{:S(2)}) %collective-permute-start.8) | collective-permute-done | bytes 1048608 | tf_op jit(solution)/shard_map/ppermute | solution.py:583
  168.9 14.8 %shard_map.377 = (bf16[512,2048]{1,0:T(8,128)(2,1)}, bf16[512,2048]{1,0:T(8,128)(2,1)}) custom-call(bf16[256,2048]{1,0:T(8,128)(2,1)} %shard_map.376.refs_0_.refs_3_, bf16[256,2048]{1,0:T(8,128)(2,1)} %copy-done.10, bf16[256,2048]{1,0:T(8,128)(2,1)} %bitcast.56, bf16[256,2048]{1,0:T(8,128)(2,1)} %collective-permute-done.10.refs_3_.refs_4_, ...), custom_call_target="tpu_custom_call" | custom-call | tf_op jit(solution)/shard_map/pallas_call | solution.py:44
  183.7 9.7 %shard_map.378.refs_7_ = bf16[4,256,2048]{2,1,0:T(8,128)(2,1)} custom-call(s32[4]{0:T(128)} %get-tuple-element.145.refs_0_, bf16[256,2048]{1,0:T(8,128)(2,1)} %bitcast.49, bf16[256,2048]{1,0:T(8,128)(2,1)} %copy-done.9, bf16[256,2048]{1,0:T(8,128)(2,1)} %bitcast.57, bf16[256,2048]{1,0:T(8,128)(2,1)} %collective-permute-done.10.refs_3_.refs_4_, ...), custom_call_target="tpu_custom_call" | custom-call | tf_op jit(solution)/shard_map/pallas_call | solution.py:48
  195.3 10.1 %shard_map.379.refs_3_ = bf16[4,256,2048]{2,1,0:T(8,128)(2,1)} custom-call(s32[4]{0:T(128)} %get-tuple-element.147.refs_0_, bf16[256,2048]{1,0:T(8,128)(2,1)} %get-tuple-element.72.refs_0_.refs_1_, bf16[256,2048]{1,0:T(8,128)(2,1)} %copy-done.8, bf16[256,2048]{1,0:T(8,128)(2,1)} %shard_map.376.refs_0_.refs_3_, bf16[256,2048]{1,0:T(8,128)(2,1)} %copy-done.10, ...), custom_call_target="tpu_custom_call" | custom-call | tf_op jit(solution)/shard_map/pallas_call | solution.py:48
  205.4 8.6 %shard_map.380 = (bf16[256,2048]{1,0:T(8,128)(2,1)}, bf16[256,2048]{1,0:T(8,128)(2,1)}) custom-call(bf16[512,2048]{1,0:T(8,128)(2,1)} %get-tuple-element.75.refs_0_, bf16[512,2048]{1,0:T(8,128)(2,1)} %get-tuple-element.76.refs_1_, bf16[2048,2048]{1,0:T(8,128)(2,1)} %refs_2_.11, bf16[4,256,2048]{2,1,0:T(8,128)(2,1)} %shard_map.379.refs_3_), custom_call_target="tpu_custom_call" | custom-call | tf_op jit(solution)/shard_map/pallas_call | solution.py:44
  217.9 8.8 %shard_map.381 = (bf16[256,2048]{1,0:T(8,128)(2,1)}, bf16[256,2048]{1,0:T(8,128)(2,1)}) custom-call(bf16[512,2048]{1,0:T(8,128)(2,1)} %get-tuple-element.75.refs_0_, bf16[512,2048]{1,0:T(8,128)(2,1)} %get-tuple-element.76.refs_1_, bf16[2048,2048]{1,0:T(8,128)(2,1)} %refs_2_.11, bf16[256,2048]{1,0:T(8,128)(2,1)} %copy-done.21, ...), custom_call_target="tpu_custom_call" | custom-call | tf_op jit(solution)/shard_map/pallas_call | solution.py:44
  228.2 8.6 %shard_map.382 = (bf16[256,2048]{1,0:T(8,128)(2,1)}, bf16[256,2048]{1,0:T(8,128)(2,1)}) custom-call(bf16[512,2048]{1,0:T(8,128)(2,1)} %get-tuple-element.73.refs_1_.refs_0_, bf16[512,2048]{1,0:T(8,128)(2,1)} %get-tuple-element.74.refs_1_, bf16[2048,2048]{1,0:T(8,128)(2,1)} %refs_2_.14, bf16[256,2048]{1,0:T(8,128)(2,1)} %get-tuple-element.79.refs_3_), custom_call_target="tpu_custom_call" | custom-call | tf_op jit(solution)/shard_map/pallas_call | solution.py:44
  236.8 15.3 %collective-permute-done.14.refs_4_ = bf16[256,2048]{1,0:T(8,128)(2,1)S(1)} collective-permute-done((bf16[256,2048]{1,0:T(8,128)(2,1)}, bf16[256,2048]{1,0:T(8,128)(2,1)S(1)}, u32[]{:S(2)}, u32[]{:S(2)}) %collective-permute-start.14) | collective-permute-done | bytes 1048608 | tf_op jit(solution)/shard_map/ppermute | solution.py:583
  268.4 8.7 %shard_map.385 = (bf16[256,2048]{1,0:T(8,128)(2,1)}, bf16[256,2048]{1,0:T(8,128)(2,1)}) custom-call(bf16[512,2048]{1,0:T(8,128)(2,1)} %get-tuple-element.73.refs_1_.refs_0_, bf16[512,2048]{1,0:T(8,128)(2,1)} %get-tuple-element.74.refs_1_, bf16[2048,2048]{1,0:T(8,128)(2,1)} %refs_2_.14, bf16[256,2048]{1,0:T(8,128)(2,1)} %copy-done.37, ...), custom_call_target="tpu_custom_call" | custom-call | tf_op jit(solution)/shard_map/pallas_call | solution.py:44
  277.1 7.4 %collective-permute-done.19.refs_0_ = bf16[256,2048]{1,0:T(8,128)(2,1)S(1)} collective-permute-done((bf16[256,2048]{1,0:T(8,128)(2,1)}, bf16[256,2048]{1,0:T(8,128)(2,1)S(1)}, u32[]{:S(2)}, u32[]{:S(2)}) %collective-permute-start.19) | collective-permute-done | bytes 1048608 | tf_op jit(solution)/shard_map/ppermute | solution.py:583
  286.3 11.2 %shard_map.387 = (bf16[2,256,2048]{2,1,0:T(8,128)(2,1)}, bf16[2,256,2048]{2,1,0:T(8,128)(2,1)}) custom-call(s32[4]{0:T(128)} %get-tuple-element.144.refs_0_, bf16[256,2048]{1,0:T(8,128)(2,1)} %bitcast.51, bf16[256,2048]{1,0:T(8,128)(2,1)} %copy-done.9, bf16[256,2048]{1,0:T(8,128)(2,1)} %bitcast.58, ...), custom_call_target="tpu_custom_call" | custom-call | tf_op jit(solution)/shard_map/pallas_call | solution.py:48
  311.5 11.1 %shard_map.390 = (bf16[2,256,2048]{2,1,0:T(8,128)(2,1)}, bf16[2,256,2048]{2,1,0:T(8,128)(2,1)}) custom-call(s32[4]{0:T(128)} %get-tuple-element.146.refs_0_, bf16[256,2048]{1,0:T(8,128)(2,1)} %get-tuple-element.72.refs_0_.refs_1_, bf16[256,2048]{1,0:T(8,128)(2,1)} %copy-done.8, bf16[256,2048]{1,0:T(8,128)(2,1)} %shard_map.376.refs_0_.refs_3_, ...), custom_call_target="tpu_custom_call" | custom-call | tf_op jit(solution)/shard_map/pallas_call | solution.py:48
  334.0 23.6 %shard_map.392.refs_2_.refs_0_.refs_1_.refs_5_ = bf16[3,1024,512]{2,1,0:T(8,128)(2,1)} custom-call(bf16[3,512,512]{2,1,0:T(8,128)(2,1)} %shard_map.367.refs_1_.refs_0_.refs_2_, bf16[3,512,512]{2,1,0:T(8,128)(2,1)} %shard_map.369.refs_1_.refs_3_, bf16[256,512]{1,0:T(8,128)(2,1)} %get-tuple-element.90.refs_2_, ...), custom_call_target="tpu_custom_call" | custom-call | tf_op jit(solution)/shard_map/pallas_call | solution.py:44
  357.7 6.2 %collective-permute-done.23.refs_1_ = bf16[2,256,2048]{2,1,0:T(8,128)(2,1)} collective-permute-done((bf16[2,256,2048]{2,1,0:T(8,128)(2,1)}, bf16[2,256,2048]{2,1,0:T(8,128)(2,1)}, u32[]{:S(2)}, u32[]{:S(2)}) %collective-permute-start.23) | collective-permute-done | bytes 2097184 | tf_op jit(solution)/shard_map/ppermute | solution.py:583
  368.0 7.4 %shard_map.394 = (bf16[256,2048]{1,0:T(8,128)(2,1)}, bf16[256,2048]{1,0:T(8,128)(2,1)}) custom-call(bf16[3,1024,512]{2,1,0:T(8,128)(2,1)} %shard_map.392.refs_2_.refs_0_.refs_1_.refs_5_, bf16[3,1024,512]{2,1,0:T(8,128)(2,1)} %shard_map.392.refs_2_.refs_0_.refs_1_.refs_5_, bf16[3,2048,512]{2,1,0:T(8,128)(2,1)} %bitcast.37, ...), custom_call_target="tpu_custom_call" | custom-call | tf_op jit(solution)/shard_map/pallas_call | solution.py:44
  382.7 7.6 %shard_map.396 = (bf16[256,2048]{1,0:T(8,128)(2,1)}, bf16[256,2048]{1,0:T(8,128)(2,1)}) custom-call(bf16[3,1024,512]{2,1,0:T(8,128)(2,1)} %shard_map.392.refs_2_.refs_0_.refs_1_.refs_5_, bf16[3,1024,512]{2,1,0:T(8,128)(2,1)} %shard_map.392.refs_2_.refs_0_.refs_1_.refs_5_, bf16[3,2048,512]{2,1,0:T(8,128)(2,1)} %bitcast.38, ...), custom_call_target="tpu_custom_call" | custom-call | tf_op jit(solution)/shard_map/pallas_call | solution.py:44
  405.1 9.1 %collective-permute-done.30.refs_7_.refs_6_ = bf16[4,256,512]{2,1,0:T(8,128)(2,1)} collective-permute-done((bf16[4,256,512]{2,1,0:T(8,128)(2,1)}, bf16[4,256,512]{2,1,0:T(8,128)(2,1)}, u32[]{:S(2)}, u32[]{:S(2)}) %collective-permute-start.30) | collective-permute-done | bytes 1048608 | tf_op jit(solution)/shard_map/ppermute | solution.py:583
  451.5 8.0 %collective-permute-done.31.refs_1_ = bf16[2,256,512]{2,1,0:T(8,128)(2,1)} collective-permute-done((bf16[2,256,512]{2,1,0:T(8,128)(2,1)}, bf16[2,256,512]{2,1,0:T(8,128)(2,1)}, u32[]{:S(2)}, u32[]{:S(2)}) %collective-permute-start.31) | collective-permute-done | bytes 524320 | tf_op jit(solution)/shard_map/ppermute | solution.py:583
  478.0 13.1 %collective-permute-done.37.refs_3_.refs_6_ = bf16[4,256,512]{2,1,0:T(8,128)(2,1)} collective-permute-done((bf16[4,256,512]{2,1,0:T(8,128)(2,1)S(1)}, bf16[4,256,512]{2,1,0:T(8,128)(2,1)}, u32[]{:S(2)}, u32[]{:S(2)}) %collective-permute-start.37) | collective-permute-done | bytes 1048608 | tf_op jit(solution)/shard_map/ppermute | solution.py:583
  503.4 14.4 %collective-permute-done.36.refs_1_ = bf16[2,256,512]{2,1,0:T(8,128)(2,1)S(1)} collective-permute-done((bf16[2,256,512]{2,1,0:T(8,128)(2,1)}, bf16[2,256,512]{2,1,0:T(8,128)(2,1)S(1)}, u32[]{:S(2)}, u32[]{:S(2)}) %collective-permute-start.36) | collective-permute-done | bytes 524320 | tf_op jit(solution)/shard_map/ppermute | solution.py:583
  520.8 8.2 %collective-permute-done.41.refs_4_.refs_1_ = bf16[2,256,512]{2,1,0:T(8,128)(2,1)S(1)} collective-permute-done((bf16[2,256,512]{2,1,0:T(8,128)(2,1)}, bf16[2,256,512]{2,1,0:T(8,128)(2,1)S(1)}, u32[]{:S(2)}, u32[]{:S(2)}) %collective-permute-start.41) | collective-permute-done | bytes 524320 | tf_op jit(solution)/shard_map/ppermute | solution.py:583
  542.9 6.7 %shard_map.411.refs_3_ = bf16[1024,2048]{1,0:T(8,128)(2,1)} custom-call(s32[1,512]{1,0:T(1,128)} %broadcast_in_dim.129.refs_0_, bf16[256,2048]{1,0:T(8,128)(2,1)} %shard_map.409.refs_2_.refs_1_, bf16[256,2048]{1,0:T(8,128)(2,1)} %collective-permute-done.42.refs_2_, bf16[1024,2048]{1,0:T(8,128)(2,1)} %shard_map.403.refs_2_.refs_3_, ...), custom_call_target="tpu_custom_call" | custom-call | tf_op jit(solution)/shard_map/pallas_call | solution.py:44
  569.2 6.7 %shard_map.416.refs_2_ = bf16[1024,2048]{1,0:T(8,128)(2,1)} custom-call(s32[1,512]{1,0:T(1,128)} %broadcast_in_dim.129.refs_0_, bf16[256,2048]{1,0:T(8,128)(2,1)} %shard_map.414.refs_2_.refs_1_, bf16[256,2048]{1,0:T(8,128)(2,1)} %copy-done.36, bf16[1024,2048]{1,0:T(8,128)(2,1)} %shard_map.412.refs_2_.refs_3_, f32[256,2048]{1,0:T(8,128)} %shard_map.415.refs_4_), custom_call_target="tpu_custom_call" | custom-call | tf_op jit(solution)/shard_map/pallas_call | solution.py:44
  (279 shorter events, 247.9 us)
Async XLA Ops:
  8.8 33.0 %all-to-all-start = ((bf16[8,32,2048]{2,1,0:T(8,128)(2,1)}), bf16[8,32,2048]{2,1,0:T(8,128)(2,1)S(1)}, u32[]{:S(2)}, u32[]{:S(2)}) async-start(bf16[8,32,2048]{2,1,0:T(8,128)(2,1)} %bitcast.1), calls=%async_computation | async-start | bytes 2097152 | tf_op jit(solution)/shard_map/all_to_all | solution.py:586
  45.5 25.8 %collective-permute-start.1 = (bf16[256,2048]{1,0:T(8,128)(2,1)}, bf16[256,2048]{1,0:T(8,128)(2,1)S(1)}, u32[]{:S(2)}, u32[]{:S(2)}) collective-permute-start(bf16[256,2048]{1,0:T(8,128)(2,1)} %shard_map.366.refs_0_.refs_1_), channel_id=1, source_target_pairs={{0,2},{1,3},{2,0},{3,1},{4,6},{5,7},{6,4},{7,5},{8,10},{9,11},{10,... | collective-permute-start | bytes 3145736 | tf_op jit(solution)/shard_map/ppermute | solution.py:583
  50.1 59.9 %all-to-all-start.1 = ((bf16[8,64,2048]{2,1,0:T(8,128)(2,1)}), bf16[8,64,2048]{2,1,0:T(8,128)(2,1)}, u32[]{:S(2)}, u32[]{:S(2)}) async-start(bf16[8,64,2048]{2,1,0:T(8,128)(2,1)} %pad_maximum_fusion), calls=%async_computation.1 | async-start | bytes 4194304 | tf_op jit(solution)/shard_map/all_to_all | solution.py:586
  108.5 25.9 %collective-permute-start.5 = (bf16[256,2048]{1,0:T(8,128)(2,1)}, bf16[256,2048]{1,0:T(8,128)(2,1)}, u32[]{:S(2)}, u32[]{:S(2)}) collective-permute-start(bf16[256,2048]{1,0:T(8,128)(2,1)} %get-tuple-element.70), channel_id=1, source_target_pairs={{0,2},{1,3},{2,0},{3,1},{4,6},{5,7},{6,4},{7,5},{8,10},{9,11},{10,... | collective-permute-start | bytes 3145736 | tf_op jit(solution)/shard_map/ppermute | solution.py:583
  111.8 28.2 %collective-permute-start.7 = (bf16[256,2048]{1,0:T(8,128)(2,1)S(1)}, bf16[256,2048]{1,0:T(8,128)(2,1)S(1)}, u32[]{:S(2)}, u32[]{:S(2)}) collective-permute-start(bf16[256,2048]{1,0:T(8,128)(2,1)S(1)} %bitcast.47), channel_id=1, source_target_pairs={{0,1},{1,0},{2,3},{3,2},{4,5},{5,4},{6,7},{7,6},{8,9},{9,8},{10,11... | collective-permute-start | bytes 3145736 | tf_op jit(solution)/shard_map/ppermute | solution.py:583
  138.3 25.8 %collective-permute-start.8 = (bf16[256,2048]{1,0:T(8,128)(2,1)}, bf16[256,2048]{1,0:T(8,128)(2,1)S(1)}, u32[]{:S(2)}, u32[]{:S(2)}) collective-permute-start(bf16[256,2048]{1,0:T(8,128)(2,1)} %get-tuple-element.72.refs_0_.refs_1_), channel_id=1, source_target_pairs={{0,2},{1,3},{2,0},{3,1},{4,6},{5,7},{6,4},{7,5},{8,10},{9,11},{10,... | collective-permute-start | bytes 3145736 | tf_op jit(solution)/shard_map/ppermute | solution.py:583
  139.8 25.7 %collective-permute-start.10 = (bf16[256,2048]{1,0:T(8,128)(2,1)S(1)}, bf16[256,2048]{1,0:T(8,128)(2,1)}, u32[]{:S(2)}, u32[]{:S(2)}) collective-permute-start(bf16[256,2048]{1,0:T(8,128)(2,1)S(1)} %bitcast.55), channel_id=1, source_target_pairs={{0,1},{1,0},{2,3},{3,2},{4,5},{5,4},{6,7},{7,6},{8,9},{9,8},{10,11... | collective-permute-start | bytes 3145736 | tf_op jit(solution)/shard_map/ppermute | solution.py:583
  193.4 92.9 %collective-permute-start.21 = (bf16[4,256,2048]{2,1,0:T(8,128)(2,1)}, bf16[4,256,2048]{2,1,0:T(8,128)(2,1)}, u32[]{:S(2)}, u32[]{:S(2)}) collective-permute-start(bf16[4,256,2048]{2,1,0:T(8,128)(2,1)} %shard_map.378.refs_7_), channel_id=1, source_target_pairs={{0,4},{4,0},{8,12},{12,8},{16,20},{20,16},{24,28},{28,24},{1,5},{5... | collective-permute-start | bytes 12582920 | tf_op jit(solution)/shard_map/ppermute | solution.py:583
  214.1 97.4 %collective-permute-start.18 = (bf16[4,256,2048]{2,1,0:T(8,128)(2,1)}, bf16[4,256,2048]{2,1,0:T(8,128)(2,1)}, u32[]{:S(2)}, u32[]{:S(2)}) collective-permute-start(bf16[4,256,2048]{2,1,0:T(8,128)(2,1)} %shard_map.379.refs_3_), channel_id=1, source_target_pairs={{0,8},{4,12},{8,0},{12,4},{16,24},{20,28},{24,16},{28,20},{1,9},{5... | collective-permute-start | bytes 12582920 | tf_op jit(solution)/shard_map/ppermute | solution.py:583
  226.7 25.4 %collective-permute-start.14 = (bf16[256,2048]{1,0:T(8,128)(2,1)}, bf16[256,2048]{1,0:T(8,128)(2,1)S(1)}, u32[]{:S(2)}, u32[]{:S(2)}) collective-permute-start(bf16[256,2048]{1,0:T(8,128)(2,1)} %get-tuple-element.79.refs_3_), channel_id=1, source_target_pairs={{0,2},{1,3},{2,0},{3,1},{4,6},{5,7},{6,4},{7,5},{8,10},{9,11},{10,... | collective-permute-start | bytes 3145736 | tf_op jit(solution)/shard_map/ppermute | solution.py:583
  259.2 25.4 %collective-permute-start.19 = (bf16[256,2048]{1,0:T(8,128)(2,1)}, bf16[256,2048]{1,0:T(8,128)(2,1)S(1)}, u32[]{:S(2)}, u32[]{:S(2)}) collective-permute-start(bf16[256,2048]{1,0:T(8,128)(2,1)} %get-tuple-element.83.refs_0_.refs_3_), channel_id=1, source_target_pairs={{0,2},{1,3},{2,0},{3,1},{4,6},{5,7},{6,4},{7,5},{8,10},{9,11},{10,... | collective-permute-start | bytes 3145736 | tf_op jit(solution)/shard_map/ppermute | solution.py:583
  297.5 66.4 %collective-permute-start.23 = (bf16[2,256,2048]{2,1,0:T(8,128)(2,1)}, bf16[2,256,2048]{2,1,0:T(8,128)(2,1)}, u32[]{:S(2)}, u32[]{:S(2)}) collective-permute-start(bf16[2,256,2048]{2,1,0:T(8,128)(2,1)} %get-tuple-element.92), channel_id=1, source_target_pairs={{0,8},{4,12},{8,0},{12,4},{16,24},{20,28},{24,16},{28,20},{1,9},{5... | collective-permute-start | bytes 6291464 | tf_op jit(solution)/shard_map/ppermute | solution.py:583
  297.6 25.6 %collective-permute-start.17 = (bf16[256,2048]{1,0:T(8,128)(2,1)S(1)}, bf16[256,2048]{1,0:T(8,128)(2,1)S(1)}, u32[]{:S(2)}, u32[]{:S(2)}) collective-permute-start(bf16[256,2048]{1,0:T(8,128)(2,1)S(1)} %copy-done.23), channel_id=1, source_target_pairs={{0,2},{1,3},{2,0},{3,1},{4,6},{5,7},{6,4},{7,5},{8,10},{9,11},{10,... | collective-permute-start | bytes 3145736 | tf_op jit(solution)/shard_map/ppermute | solution.py:583
  310.1 57.9 %collective-permute-start.24 = (bf16[4,256,512]{2,1,0:T(8,128)(2,1)}, bf16[4,256,512]{2,1,0:T(8,128)(2,1)}, u32[]{:S(2)}, u32[]{:S(2)}) collective-permute-start(bf16[4,256,512]{2,1,0:T(8,128)(2,1)} %shard_map.389.refs_8_), channel_id=1, source_target_pairs={{0,4},{4,0},{8,12},{12,8},{16,20},{20,16},{24,28},{28,24},{1,5},{5... | collective-permute-start | bytes 3145736 | tf_op jit(solution)/shard_map/ppermute | solution.py:583
  327.7 54.1 %all-to-all-start.2 = ((bf16[8,32,2048]{2,1,0:T(8,128)(2,1)}), bf16[8,32,2048]{2,1,0:T(8,128)(2,1)S(1)}, u32[]{:S(2)}, u32[]{:S(2)}) async-start(bf16[8,32,2048]{2,1,0:T(8,128)(2,1)} %bitcast.63), calls=%async_computation.2 | async-start | bytes 2097152 | tf_op jit(solution)/shard_map/all_to_all | solution.py:586
  332.0 60.5 %collective-permute-start.26 = (bf16[2,256,2048]{2,1,0:T(8,128)(2,1)}, bf16[2,256,2048]{2,1,0:T(8,128)(2,1)S(1)}, u32[]{:S(2)}, u32[]{:S(2)}) collective-permute-start(bf16[2,256,2048]{2,1,0:T(8,128)(2,1)} %get-tuple-element.97), channel_id=1, source_target_pairs={{0,4},{4,0},{8,12},{12,8},{16,20},{20,16},{24,28},{28,24},{1,5},{5... | collective-permute-start | bytes 6291464 | tf_op jit(solution)/shard_map/ppermute | solution.py:583
  375.4 38.9 %collective-permute-start.28 = (bf16[256,2048]{1,0:T(8,128)(2,1)}, bf16[256,2048]{1,0:T(8,128)(2,1)}, u32[]{:S(2)}, u32[]{:S(2)}) collective-permute-start(bf16[256,2048]{1,0:T(8,128)(2,1)} %get-tuple-element.95.refs_6_), channel_id=1, source_target_pairs={{0,1},{1,0},{2,3},{3,2},{4,5},{5,4},{6,7},{7,6},{8,9},{9,8},{10,11... | collective-permute-start | bytes 3145736 | tf_op jit(solution)/shard_map/ppermute | solution.py:583
  381.8 32.5 %collective-permute-start.30 = (bf16[4,256,512]{2,1,0:T(8,128)(2,1)}, bf16[4,256,512]{2,1,0:T(8,128)(2,1)}, u32[]{:S(2)}, u32[]{:S(2)}) collective-permute-start(bf16[4,256,512]{2,1,0:T(8,128)(2,1)} %shard_map.395.refs_4_), channel_id=1, source_target_pairs={{0,4},{4,0},{8,12},{12,8},{16,20},{20,16},{24,28},{28,24},{1,5},{5... | collective-permute-start | bytes 3145736 | tf_op jit(solution)/shard_map/ppermute | solution.py:583
  391.8 47.4 %collective-permute-start.33 = (bf16[1,256,2048]{2,1,0:T(8,128)(2,1)}, bf16[1,256,2048]{2,1,0:T(8,128)(2,1)S(1)}, u32[]{:S(2)}, u32[]{:S(2)}) collective-permute-start(bf16[1,256,2048]{2,1,0:T(8,128)(2,1)} %get-tuple-element.103), channel_id=1, source_target_pairs={{0,16},{4,20},{8,24},{12,28},{16,0},{20,4},{24,8},{28,12},{1,17},{... | collective-permute-start | bytes 3145736 | tf_op jit(solution)/shard_map/ppermute | solution.py:583
  392.5 58.0 %collective-permute-start.32 = (bf16[256,2048]{1,0:T(8,128)(2,1)}, bf16[256,2048]{1,0:T(8,128)(2,1)}, u32[]{:S(2)}, u32[]{:S(2)}) collective-permute-start(bf16[256,2048]{1,0:T(8,128)(2,1)} %bitcast.65), channel_id=1, source_target_pairs={{0,1},{1,0},{2,3},{3,2},{4,5},{5,4},{6,7},{7,6},{8,9},{9,8},{10,11... | collective-permute-start | bytes 3145736 | tf_op jit(solution)/shard_map/ppermute | solution.py:583
  427.8 31.7 %collective-permute-start.31 = (bf16[2,256,512]{2,1,0:T(8,128)(2,1)}, bf16[2,256,512]{2,1,0:T(8,128)(2,1)}, u32[]{:S(2)}, u32[]{:S(2)}) collective-permute-start(bf16[2,256,512]{2,1,0:T(8,128)(2,1)} %get-tuple-element.102), channel_id=1, source_target_pairs={{0,8},{4,12},{8,0},{12,4},{16,24},{20,28},{24,16},{28,20},{1,9},{5... | collective-permute-start | bytes 1572872 | tf_op jit(solution)/shard_map/ppermute | solution.py:583
  428.4 101.4 %all-to-all-start.3 = ((bf16[8,32,2048]{2,1,0:T(8,128)(2,1)}), bf16[8,32,2048]{2,1,0:T(8,128)(2,1)}, u32[]{:S(2)}, u32[]{:S(2)}) async-start(bf16[8,32,2048]{2,1,0:T(8,128)(2,1)} %bitcast.21), calls=%async_computation.3 | async-start | bytes 2097152 | tf_op jit(solution)/shard_map/all_to_all | solution.py:586
  432.8 36.3 %collective-permute-start.27 = (bf16[4,256,512]{2,1,0:T(8,128)(2,1)}, bf16[4,256,512]{2,1,0:T(8,128)(2,1)}, u32[]{:S(2)}, u32[]{:S(2)}) collective-permute-start(bf16[4,256,512]{2,1,0:T(8,128)(2,1)} %shard_map.397.refs_6_), channel_id=1, source_target_pairs={{0,4},{4,0},{8,12},{12,8},{16,20},{20,16},{24,28},{28,24},{1,5},{5... | collective-permute-start | bytes 3145736 | tf_op jit(solution)/shard_map/ppermute | solution.py:583
  434.8 56.4 %collective-permute-start.37 = (bf16[4,256,512]{2,1,0:T(8,128)(2,1)S(1)}, bf16[4,256,512]{2,1,0:T(8,128)(2,1)}, u32[]{:S(2)}, u32[]{:S(2)}) collective-permute-start(bf16[4,256,512]{2,1,0:T(8,128)(2,1)S(1)} %copy-done.18), channel_id=1, source_target_pairs={{0,4},{4,0},{8,12},{12,8},{16,20},{20,16},{24,28},{28,24},{1,5},{5... | collective-permute-start | bytes 3145736 | tf_op jit(solution)/shard_map/ppermute | solution.py:583
  450.4 70.3 %collective-permute-start.22 = (bf16[256,2048]{1,0:T(8,128)(2,1)S(1)}, bf16[256,2048]{1,0:T(8,128)(2,1)S(1)}, u32[]{:S(2)}, u32[]{:S(2)}) collective-permute-start(bf16[256,2048]{1,0:T(8,128)(2,1)S(1)} %bitcast.67), channel_id=1, source_target_pairs={{0,2},{1,3},{2,0},{3,1},{4,6},{5,7},{6,4},{7,5},{8,10},{9,11},{10,... | collective-permute-start | bytes 3145736 | tf_op jit(solution)/shard_map/ppermute | solution.py:583
  451.5 39.6 %collective-permute-start.38 = (bf16[2,256,512]{2,1,0:T(8,128)(2,1)}, bf16[2,256,512]{2,1,0:T(8,128)(2,1)}, u32[]{:S(2)}, u32[]{:S(2)}) collective-permute-start(bf16[2,256,512]{2,1,0:T(8,128)(2,1)} %get-tuple-element.113), channel_id=1, source_target_pairs={{0,8},{4,12},{8,0},{12,4},{16,24},{20,28},{24,16},{28,20},{1,9},{5... | collective-permute-start | bytes 1572872 | tf_op jit(solution)/shard_map/ppermute | solution.py:583
  459.5 69.4 %collective-permute-start.39 = (bf16[1,256,2048]{2,1,0:T(8,128)(2,1)}, bf16[1,256,2048]{2,1,0:T(8,128)(2,1)}, u32[]{:S(2)}, u32[]{:S(2)}) collective-permute-start(bf16[1,256,2048]{2,1,0:T(8,128)(2,1)} %get-tuple-element.117), channel_id=1, source_target_pairs={{0,16},{4,20},{8,24},{12,28},{16,0},{20,4},{24,8},{28,12},{1,17},{... | collective-permute-start | bytes 3145736 | tf_op jit(solution)/shard_map/ppermute | solution.py:583
  475.2 42.6 %collective-permute-start.36 = (bf16[2,256,512]{2,1,0:T(8,128)(2,1)}, bf16[2,256,512]{2,1,0:T(8,128)(2,1)S(1)}, u32[]{:S(2)}, u32[]{:S(2)}) collective-permute-start(bf16[2,256,512]{2,1,0:T(8,128)(2,1)} %get-tuple-element.112), channel_id=1, source_target_pairs={{0,8},{4,12},{8,0},{12,4},{16,24},{20,28},{24,16},{28,20},{1,9},{5... | collective-permute-start | bytes 1572872 | tf_op jit(solution)/shard_map/ppermute | solution.py:583
  499.4 29.5 %collective-permute-start.41 = (bf16[2,256,512]{2,1,0:T(8,128)(2,1)}, bf16[2,256,512]{2,1,0:T(8,128)(2,1)S(1)}, u32[]{:S(2)}, u32[]{:S(2)}) collective-permute-start(bf16[2,256,512]{2,1,0:T(8,128)(2,1)} %get-tuple-element.119), channel_id=1, source_target_pairs={{0,8},{4,12},{8,0},{12,4},{16,24},{20,28},{24,16},{28,20},{1,9},{5... | collective-permute-start | bytes 1572872 | tf_op jit(solution)/shard_map/ppermute | solution.py:583
  530.3 31.0 %collective-permute-start.43 = (bf16[256,2048]{1,0:T(8,128)(2,1)}, bf16[256,2048]{1,0:T(8,128)(2,1)S(1)}, u32[]{:S(2)}, u32[]{:S(2)}) collective-permute-start(bf16[256,2048]{1,0:T(8,128)(2,1)} %bitcast.22.refs_1_), channel_id=1, source_target_pairs={{0,2},{1,3},{2,0},{3,1},{4,6},{5,7},{6,4},{7,5},{8,10},{9,11},{10,... | collective-permute-start | bytes 3145736 | tf_op jit(solution)/shard_map/ppermute | solution.py:583
  531.3 27.1 %collective-permute-start.46 = (bf16[1,256,512]{2,1,0:T(8,128)(2,1)S(1)}, bf16[1,256,512]{2,1,0:T(8,128)(2,1)S(1)}, u32[]{:S(2)}, u32[]{:S(2)}) collective-permute-start(bf16[1,256,512]{2,1,0:T(8,128)(2,1)S(1)} %copy-done.54), channel_id=1, source_target_pairs={{0,16},{4,20},{8,24},{12,28},{16,0},{20,4},{24,8},{28,12},{1,17},{... | collective-permute-start | bytes 786440 | tf_op jit(solution)/shard_map/ppermute | solution.py:583
  533.7 27.5 %all-to-all-start.4 = ((f32[8,4,256]{2,1,0:T(4,128)}), f32[8,4,256]{2,1,0:T(4,128)S(1)}, u32[]{:S(2)}, u32[]{:S(2)}) async-start(f32[8,4,256]{2,1,0:T(4,128)} %bitcast.24), calls=%async_computation.4 | async-start | bytes 65536 | tf_op jit(solution)/shard_map/all_to_all | solution.py:586
  (78 other events, 621.0 us)
